TPU v7x, 32 devices: a whole 2x2x4 slice. The times are simulated.
32 devices in a mesh: dp: 2 (over x), context: 4 (over z), tensor: 4 (over y, core).
Axes of the slice: x: 2, y: 2, z: 4, core: 2. Of those that a mesh axis runs over, the one named last changes fastest.
Arguments:
- tokens: bfloat16 [2, 2048, 2560], P('dp', 'context'), may hold values from -6 to 6
- cotangent: bfloat16 [2, 2048, 2560], P('dp', 'context'), may hold values from -6 to 6
- group_order: int32 [8], replicated, may hold values from 0 to 7, each once
- attn_gain: float32 [2560], replicated, may hold values from 0.25 to 1.75
- query_down: bfloat16 [2560, 768], replicated, may hold values from -0.125 to 0.125
- query_gain: float32 [768], replicated, may hold values from 0.25 to 1.75
- latent_down: bfloat16 [2560, 288], replicated, may hold values from -0.125 to 0.125
- latent_gain: float32 [256], replicated, may hold values from 0.25 to 1.75
- query_up: bfloat16 [768, 3840], P(None, 'tensor'), may hold values from -0.4375 to 0.4375
- latent_up: bfloat16 [256, 5120], P(None, 'tensor'), may hold values from -0.375 to 0.375
- attn_out: bfloat16 [2560, 2560], P('tensor'), may hold values from -4 to 4
- mlp_gain: float32 [2560], replicated, may hold values from 0.25 to 1.75
- gate_proj: bfloat16 [2560, 6400], P(None, 'tensor'), may hold values from -0.125 to 0.125
- up_proj: bfloat16 [2560, 6400], P(None, 'tensor'), may hold values from -0.125 to 0.125
- down_proj: bfloat16 [6400, 2560], P('tensor'), may hold values from -0.875 to 0.875
Outputs:
- layer_out: bfloat16 [2, 2048, 2560], P('dp', 'context')
- token_grad: float32 [2, 2048, 2560], P('dp', 'context')
- attn_gain_grad: float32 [2560], P(('dp', 'context'))
- query_down_grad: float32 [2560, 768], P(('dp', 'context'))
- query_gain_grad: float32 [768], P(('dp', 'context'))
- latent_down_grad: float32 [2560, 288], P(('dp', 'context'))
- latent_gain_grad: float32 [256], P(('dp', 'context'))
- query_up_grad: float32 [768, 3840], P(('dp', 'context'), 'tensor')
- latent_up_grad: float32 [256, 5120], P(('dp', 'context'), 'tensor')
- attn_out_grad: float32 [2560, 2560], P('tensor', ('dp', 'context'))
- mlp_gain_grad: float32 [2560], P(('dp', 'context'))
- gate_proj_grad: float32 [2560, 6400], P(('dp', 'context'), 'tensor')
- up_proj_grad: float32 [2560, 6400], P(('dp', 'context'), 'tensor')
- down_proj_grad: float32 [6400, 2560], P('tensor', ('dp', 'context'))
Inputs may be any that keep to these rules, and one draw needn't show every extreme that they name: group_order is a permutation; the shard of context index c holds, in this order, the blocks group_order[2 c] and group_order[2 c + 1] of 256 consecutive positions of each of its sequences.
All inputs are finite; a program needn't handle non-finite values.
Results may differ from a plain program's by a relative error of at most 0.025.
Values may be sent and summed in bfloat16 or wider, within the bound.
A program may use at most 192 MiB of HBM per device.

v0:
```python
import math

import jax
import jax.numpy as jnp
from jax import lax
from jax.sharding import PartitionSpec as P

NOPE = 64
ROPE = 32
V_DIM = 64
KV_RANK = 256
HALF = 256


EPS = 1e-05
RESIDUAL = 1.4 / math.sqrt(62.0)
PRECISE = lax.Precision.HIGHEST


def matmul(left, right):
    return jnp.dot(left, right, preferred_element_type=jnp.float32)


def times_transposed(left, right):
    return lax.dot_general(
        left, right, (((1,), (1,)), ((), ())), preferred_element_type=jnp.float32
    )


def transposed_times(left, right):
    return lax.dot_general(
        left, right, (((0,), (0,)), ((), ())), preferred_element_type=jnp.float32
    )


def exact_times_transposed(left, right):
    return lax.dot_general(
        left, right, (((1,), (1,)), ((), ())), precision=PRECISE, preferred_element_type=jnp.float32
    )


def exact_transposed_times(left, right):
    return lax.dot_general(
        left, right, (((0,), (0,)), ((), ())), precision=PRECISE, preferred_element_type=jnp.float32
    )


def scaled(value):
    inverse = lax.rsqrt(jnp.mean(value * value, axis=-1, keepdims=True) + EPS)
    return (value * inverse, inverse)


def norm_back(incoming, normed, inverse, gain):
    weighted = incoming * gain
    grad_gain = jnp.sum(incoming * normed, axis=0)
    grad_value = inverse * (weighted - normed * jnp.mean(weighted * normed, axis=-1, keepdims=True))
    return (grad_value, grad_gain)


def rope_tables(positions):
    count = ROPE // 2
    freq = 10000.0 ** (-2.0 * jnp.arange(count, dtype=jnp.float32) / ROPE)
    angle = positions.astype(jnp.float32)[:, None] * freq[None, :]
    return (jnp.cos(angle), jnp.sin(angle))


def rotate(value, cosine, sine):
    count = value.shape[-1] // 2
    first = value[..., :count]
    second = value[..., count:]
    return jnp.concatenate(
        [first * cosine - second * sine, second * cosine + first * sine], axis=-1
    )


def unrotate(value, cosine, sine):
    count = value.shape[-1] // 2
    first = value[..., :count]
    second = value[..., count:]
    return jnp.concatenate(
        [first * cosine + second * sine, second * cosine - first * sine], axis=-1
    )


def per_device(
    tokens,
    cotangent,
    group_order,
    attn_gain,
    query_down,
    query_gain,
    latent_down,
    latent_gain,
    query_up,
    latent_up,
    attn_out,
    mlp_gain,
    gate_proj,
    up_proj,
    down_proj,
):
    rows = tokens.shape[1]
    blocks = group_order.shape[0]
    seq_length = blocks * HALF
    local_heads = query_up.shape[1] // (NOPE + ROPE)
    scale = 1.0 / math.sqrt(NOPE + ROPE)
    offsets = jnp.arange(HALF, dtype=jnp.int32)
    place = lax.axis_index("context")
    mine = lax.dynamic_slice_in_dim(group_order, 2 * place, 2)
    query_pos = (mine[:, None] * HALF + offsets[None, :]).reshape(rows)
    last_pos = jnp.max(query_pos)
    cosine, sine = rope_tables(query_pos)
    head_cos = cosine[:, None, :]
    head_sin = sine[:, None, :]
    latent_up_wide = latent_up.astype(jnp.float32)
    weights = (
        attn_gain,
        query_down,
        query_gain,
        latent_down,
        latent_gain,
        query_up,
        latent_up,
        attn_out,
        mlp_gain,
        gate_proj,
        up_proj,
        down_proj,
    )
    totals = tuple((jnp.zeros(w.shape, jnp.float32) for w in weights))
    inputs = tokens[0].astype(jnp.float32)
    upstream = cotangent[0].astype(jnp.float32)
    first_normed, first_inverse = scaled(inputs)
    hidden_one = (first_normed * attn_gain).astype(jnp.bfloat16)
    query_low = matmul(hidden_one, query_down)
    latent_raw = matmul(hidden_one, latent_down)
    query_normed, query_inverse = scaled(query_low)
    query_latent = (query_normed * query_gain).astype(jnp.bfloat16)
    cache_normed, cache_inverse = scaled(latent_raw[:, :KV_RANK])
    latent = (cache_normed * latent_gain).astype(jnp.bfloat16)
    key_rope = rotate(latent_raw[:, KV_RANK:], cosine, sine).astype(jnp.bfloat16)
    query_full = matmul(query_latent, query_up).reshape(rows, local_heads, NOPE + ROPE)
    query_nope = query_full[:, :, :NOPE].astype(jnp.bfloat16)
    query_rope = rotate(query_full[:, :, NOPE:], head_cos, head_sin).astype(jnp.bfloat16)
    latent_all = lax.all_gather(latent, "context", axis=0, tiled=True)
    rope_all = lax.all_gather(key_rope, "context", axis=0, tiled=True)
    keys_all = matmul(latent_all, latent_up).astype(jnp.bfloat16)
    key_values = keys_all.reshape(seq_length, local_heads, NOPE + V_DIM)
    key_nope = key_values[:, :, :NOPE]
    values = key_values[:, :, NOPE:]

    def block_scores(index):
        start = index * HALF
        nope_block = lax.dynamic_slice_in_dim(key_nope, start, HALF, 0)
        rope_block = lax.dynamic_slice_in_dim(rope_all, start, HALF, 0)
        value_block = lax.dynamic_slice_in_dim(values, start, HALF, 0)
        raw = jnp.einsum("qhd,khd->hqk", query_nope, nope_block, preferred_element_type=jnp.float32)
        raw = (
            raw
            + jnp.einsum("qhd,kd->hqk", query_rope, rope_block, preferred_element_type=jnp.float32)
        ) * scale
        key_at = group_order[index] * HALF + offsets
        allowed = (key_at[None, :] <= query_pos[:, None])[None]
        return (raw, allowed, nope_block, rope_block, value_block)

    def stats_step(index, carry):

        def stats_work(state):
            top, total = state
            raw, allowed, nope_block, rope_block, value_block = block_scores(index)
            masked = jnp.where(allowed, raw, -1e30)
            new_top = jnp.maximum(top, jnp.max(masked, axis=-1))
            weight = jnp.where(allowed, jnp.exp(masked - new_top[..., None]), 0.0)
            return (new_top, total * jnp.exp(top - new_top) + jnp.sum(weight, axis=-1))

        return lax.cond(
            group_order[index] * HALF <= last_pos, stats_work, lambda state: state, carry
        )

    start_top = jnp.full((local_heads, rows), -1e30, jnp.float32)
    start_total = jnp.zeros((local_heads, rows), jnp.float32)
    top, total = lax.fori_loop(0, blocks, stats_step, (start_top, start_total))
    log_total = top + jnp.log(total)

    def block_prob(raw, allowed):
        return jnp.where(
            allowed, jnp.exp(jnp.where(allowed, raw, -1e30) - log_total[..., None]), 0.0
        )

    def out_step(index, carry):

        def out_work(state):
            mixed, extra = state
            raw, allowed, nope_block, rope_block, value_block = block_scores(index)
            prob = block_prob(raw, allowed)
            low_prob = prob.astype(jnp.bfloat16)
            rest = (prob - low_prob.astype(jnp.float32)).astype(jnp.bfloat16)
            mixed = mixed + jnp.einsum(
                "hqk,khd->qhd", low_prob, value_block, preferred_element_type=jnp.float32
            )
            extra = extra + jnp.einsum(
                "hqk,khd->qhd", rest, value_block, preferred_element_type=jnp.float32
            )
            return (mixed, extra)

        return lax.cond(group_order[index] * HALF <= last_pos, out_work, lambda state: state, carry)

    empty = jnp.zeros((rows, local_heads, V_DIM), jnp.float32)
    mixed, extra = lax.fori_loop(0, blocks, out_step, (empty, empty))
    exact = mixed + extra
    joined = mixed.astype(jnp.bfloat16).reshape(rows, local_heads * V_DIM)
    branch = lax.psum(matmul(joined, attn_out).astype(jnp.bfloat16), "tensor").astype(jnp.float32)
    middle = inputs + RESIDUAL * branch
    second_normed, second_inverse = scaled(middle)
    hidden_two = (second_normed * mlp_gain).astype(jnp.bfloat16)
    gate = matmul(hidden_two, gate_proj)
    upper = matmul(hidden_two, up_proj)
    sigma = jax.nn.sigmoid(gate)
    hidden_mid = (gate * sigma * upper).astype(jnp.bfloat16)
    feed = lax.psum(matmul(hidden_mid, down_proj).astype(jnp.bfloat16), "tensor").astype(
        jnp.float32
    )
    outputs = [(middle + RESIDUAL * feed).astype(jnp.bfloat16)]
    grad_feed = (RESIDUAL * upstream).astype(jnp.bfloat16)
    grad_down = transposed_times(hidden_mid, grad_feed)
    grad_hidden = times_transposed(grad_feed, down_proj)
    grad_gate = (grad_hidden * upper * sigma * (1.0 + gate * (1.0 - sigma))).astype(jnp.bfloat16)
    grad_upper = (grad_hidden * gate * sigma).astype(jnp.bfloat16)
    grad_gate_proj = transposed_times(hidden_two, grad_gate)
    grad_up_proj = transposed_times(hidden_two, grad_upper)
    partial_two = times_transposed(grad_gate, gate_proj) + times_transposed(grad_upper, up_proj)
    grad_hidden_two = lax.psum(partial_two.astype(jnp.bfloat16), "tensor").astype(jnp.float32)
    grad_norm_two, grad_mlp_gain = norm_back(
        grad_hidden_two, second_normed, second_inverse, mlp_gain
    )
    grad_middle = upstream + grad_norm_two
    grad_branch = (RESIDUAL * grad_middle).astype(jnp.bfloat16)
    grad_attn_out = transposed_times(joined, grad_branch)
    grad_mixed = (
        times_transposed(grad_branch, attn_out)
        .astype(jnp.bfloat16)
        .reshape(rows, local_heads, V_DIM)
    )
    delta = jnp.einsum("qhd,qhd->hq", grad_mixed.astype(jnp.float32), exact)

    def back_step(index, carry):

        def back_work(state):
            grad_qn, grad_qr, grad_kv, grad_kr = state
            raw, allowed, nope_block, rope_block, value_block = block_scores(index)
            prob = block_prob(raw, allowed)
            low_prob = prob.astype(jnp.bfloat16)
            grad_prob = jnp.einsum(
                "qhd,khd->hqk", grad_mixed, value_block, preferred_element_type=jnp.float32
            )
            grad_score = (prob * (grad_prob - delta[..., None])).astype(jnp.bfloat16)
            grad_qn = grad_qn + jnp.einsum(
                "hqk,khd->qhd", grad_score, nope_block, preferred_element_type=jnp.float32
            )
            grad_qr = grad_qr + jnp.einsum(
                "hqk,kd->qhd", grad_score, rope_block, preferred_element_type=jnp.float32
            )
            grad_kn = (
                jnp.einsum(
                    "hqk,qhd->khd", grad_score, query_nope, preferred_element_type=jnp.float32
                )
                * scale
            )
            grad_rope = (
                jnp.einsum(
                    "hqk,qhd->kd", grad_score, query_rope, preferred_element_type=jnp.float32
                )
                * scale
            )
            grad_value = jnp.einsum(
                "hqk,qhd->khd", low_prob, grad_mixed, preferred_element_type=jnp.float32
            )
            stacked = jnp.concatenate([grad_kn, grad_value], axis=-1).reshape(
                HALF, local_heads * (NOPE + V_DIM)
            )
            grad_kv = lax.dynamic_update_slice_in_dim(grad_kv, stacked, index * HALF, 0)
            grad_kr = lax.dynamic_update_slice_in_dim(grad_kr, grad_rope, index * HALF, 0)
            return (grad_qn, grad_qr, grad_kv, grad_kr)

        return lax.cond(
            group_order[index] * HALF <= last_pos, back_work, lambda state: state, carry
        )

    start_state = (
        jnp.zeros((rows, local_heads, NOPE), jnp.float32),
        jnp.zeros((rows, local_heads, ROPE), jnp.float32),
        jnp.zeros((seq_length, local_heads * (NOPE + V_DIM)), jnp.float32),
        jnp.zeros((seq_length, ROPE), jnp.float32),
    )
    grad_qn, grad_qr, grad_kv, grad_kr = lax.fori_loop(0, blocks, back_step, start_state)
    grad_latent_up = exact_transposed_times(latent_all.astype(jnp.float32), grad_kv)
    every_latent = exact_times_transposed(grad_kv, latent_up_wide)
    partial_latent = lax.psum_scatter(
        every_latent.astype(jnp.bfloat16), "context", scatter_dimension=0, tiled=True
    )
    own_rope = lax.psum_scatter(
        grad_kr.astype(jnp.bfloat16), "context", scatter_dimension=0, tiled=True
    )
    query_part = jnp.concatenate(
        [grad_qn * scale, unrotate(grad_qr * scale, head_cos, head_sin)], axis=-1
    )
    grad_query_full = query_part.reshape(rows, local_heads * (NOPE + ROPE)).astype(jnp.bfloat16)
    grad_query_up = transposed_times(query_latent, grad_query_full)
    partial_query = times_transposed(grad_query_full, query_up)
    grad_qlat = lax.psum(partial_query.astype(jnp.bfloat16), "tensor").astype(jnp.float32)
    grad_lat = lax.psum(partial_latent, "tensor").astype(jnp.float32)
    grad_rope_sum = lax.psum(own_rope, "tensor").astype(jnp.float32)
    grad_query_low, grad_query_gain = norm_back(grad_qlat, query_normed, query_inverse, query_gain)
    grad_cache, grad_latent_gain = norm_back(grad_lat, cache_normed, cache_inverse, latent_gain)
    grad_query_low = grad_query_low.astype(jnp.bfloat16)
    grad_latent_raw = jnp.concatenate(
        [grad_cache, unrotate(grad_rope_sum, cosine, sine)], axis=-1
    ).astype(jnp.bfloat16)
    grad_query_down = transposed_times(hidden_one, grad_query_low)
    grad_latent_down = transposed_times(hidden_one, grad_latent_raw)
    grad_hidden_one = times_transposed(grad_query_low, query_down) + times_transposed(
        grad_latent_raw, latent_down
    )
    grad_norm_one, grad_attn_gain = norm_back(
        grad_hidden_one, first_normed, first_inverse, attn_gain
    )
    input_grads = [grad_middle + grad_norm_one]
    current = (
        grad_attn_gain,
        grad_query_down,
        grad_query_gain,
        grad_latent_down,
        grad_latent_gain,
        grad_query_up,
        grad_latent_up,
        grad_attn_out,
        grad_mlp_gain,
        grad_gate_proj,
        grad_up_proj,
        grad_down,
    )
    totals = jax.tree.map(lambda a, b: b, totals, current)
    summed = (
        lax.psum_scatter(
            totals[0].astype(jnp.bfloat16), ("dp", "context"), scatter_dimension=0, tiled=True
        ).astype(jnp.float32),
        lax.psum_scatter(
            totals[1].astype(jnp.bfloat16), ("dp", "context"), scatter_dimension=0, tiled=True
        ).astype(jnp.float32),
        lax.psum_scatter(
            totals[2].astype(jnp.bfloat16), ("dp", "context"), scatter_dimension=0, tiled=True
        ).astype(jnp.float32),
        lax.psum_scatter(
            totals[3].astype(jnp.bfloat16), ("dp", "context"), scatter_dimension=0, tiled=True
        ).astype(jnp.float32),
        lax.psum_scatter(
            totals[4].astype(jnp.bfloat16), ("dp", "context"), scatter_dimension=0, tiled=True
        ).astype(jnp.float32),
        lax.psum_scatter(
            totals[5].astype(jnp.bfloat16), ("dp", "context"), scatter_dimension=0, tiled=True
        ).astype(jnp.float32),
        lax.psum_scatter(
            totals[6].astype(jnp.bfloat16), ("dp", "context"), scatter_dimension=0, tiled=True
        ).astype(jnp.float32),
        lax.psum_scatter(
            totals[7].astype(jnp.bfloat16), ("dp", "context"), scatter_dimension=1, tiled=True
        ).astype(jnp.float32),
        lax.psum_scatter(
            totals[8].astype(jnp.bfloat16), ("dp", "context"), scatter_dimension=0, tiled=True
        ).astype(jnp.float32),
        lax.psum_scatter(
            totals[9].astype(jnp.bfloat16), ("dp", "context"), scatter_dimension=0, tiled=True
        ).astype(jnp.float32),
        lax.psum_scatter(
            totals[10].astype(jnp.bfloat16), ("dp", "context"), scatter_dimension=0, tiled=True
        ).astype(jnp.float32),
        lax.psum_scatter(
            totals[11].astype(jnp.bfloat16), ("dp", "context"), scatter_dimension=1, tiled=True
        ).astype(jnp.float32),
    )
    return (
        jnp.stack(outputs),
        jnp.stack(input_grads),
        summed[0],
        summed[1],
        summed[2],
        summed[3],
        summed[4],
        summed[5],
        summed[6],
        summed[7],
        summed[8],
        summed[9],
        summed[10],
        summed[11],
    )


def solution(mesh):
    in_specs = (
        P("dp", "context", None),
        P("dp", "context", None),
        P(),
        P(),
        P(),
        P(),
        P(),
        P(),
        P(None, "tensor"),
        P(None, "tensor"),
        P("tensor", None),
        P(),
        P(None, "tensor"),
        P(None, "tensor"),
        P("tensor", None),
    )
    out_specs = (
        P("dp", "context", None),
        P("dp", "context", None),
        P(("dp", "context")),
        P(("dp", "context"), None),
        P(("dp", "context")),
        P(("dp", "context"), None),
        P(("dp", "context")),
        P(("dp", "context"), "tensor"),
        P(("dp", "context"), "tensor"),
        P("tensor", ("dp", "context")),
        P(("dp", "context")),
        P(("dp", "context"), "tensor"),
        P(("dp", "context"), "tensor"),
        P("tensor", ("dp", "context")),
    )
    return jax.shard_map(
        per_device, mesh=mesh, in_specs=in_specs, out_specs=out_specs, check_vma=False
    )
```

profile of v0, /device:TPU:9, one launch (start us, length us, event | category | flops | bytes accessed | tf_op | source)
XLA Modules:
  0.0 1587.4 jit_solution(13894450399839518336)
XLA Ops:
  15.3 6.3 multiply_reduce_fusion.1
  27.5 11.8 all_gather.7
  40.1 6.2 all-gather.2.cloned.1.call-done
  52.4 69.8 %while.52 = (s32[]{:T(128)}, f32[10,512]{1,0:T(8,128)S(1)}, f32[10,512]{1,0:T(8,128)S(1)}, s32[8]{0:T(128)S(1)}, s32[]{:T(128)}, /*index=5*/bf16[2048,10,64]{0,2...) while((s32[]{:T(128)}, f32[10,512]{1,0:T(8,128)S(1)}, ...), condition=%wide.region_9.10_spmd.clone, body=%wide.region_4.9_spmd.clone.sunk | while | flops 260975360 | bytes 22974880 | solution.py:182
  54.3 6.8 conditional.9
  63.0 6.8 conditional.9
  71.8 6.8 conditional.9
  80.5 6.8 conditional.9
  89.2 6.8 conditional.9
  97.9 6.8 conditional.9
  106.6 6.8 conditional.9
  115.3 6.8 conditional.9
  124.7 106.4 %while.53 = (s32[]{:T(128)}, f32[512,10,64]{0,2,1:T(8,128)}, f32[512,10,64]{0,2,1:T(8,128)}, s32[8]{0:T(128)S(1)}, s32[]{:T(128)}, /*index=5*/bf16[2048,10,64]{0...) while((s32[]{:T(128)}, f32[512,10,64]{0,2,1:T(8,128)}, ...), condition=%wide.region_13.14_spmd.clone, body=%wide.region_10.13_spmd.clone.sunk | while | flops 601096960 | bytes 54723128 | solution.py:209
  126.6 11.4 conditional.10
  139.9 11.4 conditional.10
  153.2 11.4 conditional.10
  166.5 11.4 conditional.10
  179.8 11.4 conditional.10
  193.1 11.4 conditional.10
  206.4 11.4 conditional.10
  219.7 11.4 conditional.10
  237.2 59.2 %all-reduce.10.cloned.1.call-done = bf16[512,2560]{1,0:T(8,128)(2,1)} async-done(((bf16[512,2560]{1,0:T(8,128)(2,1)}), bf16[512,2560]{1,0:T(8,128)(2,1)}) %all-reduce.10.cloned.1.call-update) | async-done | bytes 2621456 | tf_op jit(solution)/shard_map/psum | solution.py:212
  301.9 9.8 fusion.141
  311.7 6.4 fusion.140
  318.2 11.5 multiply_convert_fusion.2
  329.7 7.1 fusion.142
  336.8 6.9 add_convert_fusion
  343.8 60.1 %all-reduce.12.cloned.1.call-done = bf16[512,2560]{1,0:T(8,128)(2,1)} async-done(((bf16[512,2560]{1,0:T(8,128)(2,1)}), bf16[512,2560]{1,0:T(8,128)(2,1)}) %all-reduce.12.cloned.1.call-update) | async-done | bytes 2621456 | tf_op jit(solution)/shard_map/psum | solution.py:232
  403.9 6.1 fusion.78
  410.1 6.5 convolution_convert_fusion.13
  423.8 5.4 broadcast_in_dim.96
  429.2 180.9 %while.54 = (s32[]{:T(128)}, f32[512,10,64]{0,2,1:T(8,128)}, f32[512,10,32]{0,2,1:T(8,128)}, f32[2048,1280]{0,1:T(8,128)}, bf16[2048,32]{0,1:T(8,128)(2,1)}, /*i...) while((s32[]{:T(128)}, f32[512,10,64]{0,2,1:T(8,128)}, ...), condition=%wide.region_22.0_spmd.clone, body=%wide.region_19.22_spmd.clone.sunk | while | flops 1103438592 | bytes 54465072 | solution.py:295
  431.2 20.7 %conditional.11 = ((f32[512,10,64]{0,2,1:T(8,128)}, f32[512,10,32]{0,2,1:T(8,128)}, f32[2048,1280]{0,1:T(8,128)}, bf16[2048,32]{0,1:T(8,128)(2,1)})) conditional(s32[]{:T(128)} %convert_element_type.434, (f32[512,10,64]{0,2,1:T(8,128)}, f32[512,10,32]{0,2,1:T(8,128)}, f32[2048,1280]{0,1:T(8,128)}, bf16[2048,32]{0,1:T(8,128)(2,1)}) %tuple.145, ...), branch_computations={%region_20.20_spmd, %region_21.21_spmd} | conditional | flops 1103438592 | bytes 54461624 | solution.py:285
  453.8 20.7 %conditional.11 = ((f32[512,10,64]{0,2,1:T(8,128)}, f32[512,10,32]{0,2,1:T(8,128)}, f32[2048,1280]{0,1:T(8,128)}, bf16[2048,32]{0,1:T(8,128)(2,1)})) conditional(s32[]{:T(128)} %convert_element_type.434, (f32[512,10,64]{0,2,1:T(8,128)}, f32[512,10,32]{0,2,1:T(8,128)}, f32[2048,1280]{0,1:T(8,128)}, bf16[2048,32]{0,1:T(8,128)(2,1)}) %tuple.145, ...), branch_computations={%region_20.20_spmd, %region_21.21_spmd} | conditional | flops 1103438592 | bytes 54461624 | solution.py:285
  476.4 20.7 %conditional.11 = ((f32[512,10,64]{0,2,1:T(8,128)}, f32[512,10,32]{0,2,1:T(8,128)}, f32[2048,1280]{0,1:T(8,128)}, bf16[2048,32]{0,1:T(8,128)(2,1)})) conditional(s32[]{:T(128)} %convert_element_type.434, (f32[512,10,64]{0,2,1:T(8,128)}, f32[512,10,32]{0,2,1:T(8,128)}, f32[2048,1280]{0,1:T(8,128)}, bf16[2048,32]{0,1:T(8,128)(2,1)}) %tuple.145, ...), branch_computations={%region_20.20_spmd, %region_21.21_spmd} | conditional | flops 1103438592 | bytes 54461624 | solution.py:285
  498.9 20.7 %conditional.11 = ((f32[512,10,64]{0,2,1:T(8,128)}, f32[512,10,32]{0,2,1:T(8,128)}, f32[2048,1280]{0,1:T(8,128)}, bf16[2048,32]{0,1:T(8,128)(2,1)})) conditional(s32[]{:T(128)} %convert_element_type.434, (f32[512,10,64]{0,2,1:T(8,128)}, f32[512,10,32]{0,2,1:T(8,128)}, f32[2048,1280]{0,1:T(8,128)}, bf16[2048,32]{0,1:T(8,128)(2,1)}) %tuple.145, ...), branch_computations={%region_20.20_spmd, %region_21.21_spmd} | conditional | flops 1103438592 | bytes 54461624 | solution.py:285
  521.5 20.7 %conditional.11 = ((f32[512,10,64]{0,2,1:T(8,128)}, f32[512,10,32]{0,2,1:T(8,128)}, f32[2048,1280]{0,1:T(8,128)}, bf16[2048,32]{0,1:T(8,128)(2,1)})) conditional(s32[]{:T(128)} %convert_element_type.434, (f32[512,10,64]{0,2,1:T(8,128)}, f32[512,10,32]{0,2,1:T(8,128)}, f32[2048,1280]{0,1:T(8,128)}, bf16[2048,32]{0,1:T(8,128)(2,1)}) %tuple.145, ...), branch_computations={%region_20.20_spmd, %region_21.21_spmd} | conditional | flops 1103438592 | bytes 54461624 | solution.py:285
  544.2 20.7 %conditional.11 = ((f32[512,10,64]{0,2,1:T(8,128)}, f32[512,10,32]{0,2,1:T(8,128)}, f32[2048,1280]{0,1:T(8,128)}, bf16[2048,32]{0,1:T(8,128)(2,1)})) conditional(s32[]{:T(128)} %convert_element_type.434, (f32[512,10,64]{0,2,1:T(8,128)}, f32[512,10,32]{0,2,1:T(8,128)}, f32[2048,1280]{0,1:T(8,128)}, bf16[2048,32]{0,1:T(8,128)(2,1)}) %tuple.145, ...), branch_computations={%region_20.20_spmd, %region_21.21_spmd} | conditional | flops 1103438592 | bytes 54461624 | solution.py:285
  566.7 20.8 %conditional.11 = ((f32[512,10,64]{0,2,1:T(8,128)}, f32[512,10,32]{0,2,1:T(8,128)}, f32[2048,1280]{0,1:T(8,128)}, bf16[2048,32]{0,1:T(8,128)(2,1)})) conditional(s32[]{:T(128)} %convert_element_type.434, (f32[512,10,64]{0,2,1:T(8,128)}, f32[512,10,32]{0,2,1:T(8,128)}, f32[2048,1280]{0,1:T(8,128)}, bf16[2048,32]{0,1:T(8,128)(2,1)}) %tuple.145, ...), branch_computations={%region_20.20_spmd, %region_21.21_spmd} | conditional | flops 1103438592 | bytes 54461624 | solution.py:285
  589.4 20.7 %conditional.11 = ((f32[512,10,64]{0,2,1:T(8,128)}, f32[512,10,32]{0,2,1:T(8,128)}, f32[2048,1280]{0,1:T(8,128)}, bf16[2048,32]{0,1:T(8,128)(2,1)})) conditional(s32[]{:T(128)} %convert_element_type.434, (f32[512,10,64]{0,2,1:T(8,128)}, f32[512,10,32]{0,2,1:T(8,128)}, f32[2048,1280]{0,1:T(8,128)}, bf16[2048,32]{0,1:T(8,128)(2,1)}) %tuple.145, ...), branch_computations={%region_20.20_spmd, %region_21.21_spmd} | conditional | flops 1103438592 | bytes 54461624 | solution.py:285
  610.1 10.3 convolution_convert_fusion.10
  620.6 10.0 convolution_convert_fusion.7
  637.1 7.0 reduce-scatter.13.cloned.1.call-done
  644.2 8.9 convolution_convert_fusion.9
  653.3 4.2 convolution_convert_fusion.11
  657.5 8.9 convolution_convert_fusion.5
  666.5 11.7 psum.47
  679.1 66.8 %all-reduce.14.cloned.1.call-done = (bf16[512,2560]{1,0:T(8,128)(2,1)}, bf16[512,768]{1,0:T(8,128)(2,1)}, bf16[512,256]{0,1:T(8,128)(2,1)}) async-done(((bf16[512,2560]{1,0:T(8,128)(2,1)}, bf16[512,768]{1,0:T(8,128)(2,1)}, bf16[512,256]{0,1:T(8,128)(2,1)}), (bf16[512,2560]{1,0:T(8,128)(2,1)}, bf16[512,768]{1,0:T(8,128)(2,1)}, bf16[512,256]{0,1:T(8,128)(2,1)})) %all-reduce.14.cloned.1.call-update) | async-done | bytes 3670032 | tf_op jit(solution)/shard_map/psum | solution.py:220
  757.2 6.2 convolution_convert_fusion.4
  763.5 10.6 convolution_convert_fusion.1
  774.1 10.6 convolution_convert_fusion.2
  784.9 10.6 convolution_convert_fusion
  798.7 10.8 reduce-scatter.21.cloned.1.call-done
  811.0 66.7 %reduce-scatter.19.cloned.1.call-done = bf16[96,960]{1,0:T(8,128)(2,1)} async-done(((bf16[768,960]{1,0:T(8,128)(2,1)}), bf16[96,960]{1,0:T(8,128)(2,1)}) %reduce-scatter.19.cloned.1.call-update) | async-done | bytes 184336 | tf_op jit(solution)/shard_map/reduce_scatter | solution.py:359
  879.5 5.3 fusion.138
  884.8 4.2 fusion.86
  889.0 27.2 %all-reduce.4 = (bf16[2560]{0:T(1024)(128)(2,1)S(1)}, bf16[768]{0:T(1024)(128)(2,1)S(1)}, bf16[256]{0:T(256)(128)(2,1)S(1)}, bf16[2560]{0:T(1024)(128)(2,1)S(1)}) all-reduce(bf16[2560]{0:T(1024)(128)(2,1)S(1)} %get-tuple-element.976, ...), channel_id=4, replica_groups=mesh['dp'=2,'context'=4,'tensor'=4] {'dp','context'}, use_global_device_ids=true, to_apply=%region_32.33.clone | all-reduce | flops 6144 | bytes 24576
  918.0 9.8 fusion.85
  927.8 30.8 %reduce-scatter.23.cloned.1.call-done = bf16[640,320]{0,1:T(8,128)(2,1)} async-done(((bf16[640,2560]{0,1:T(8,128)(2,1)}), bf16[640,320]{0,1:T(8,128)(2,1)}) %reduce-scatter.23.cloned.1.call-update) | async-done | bytes 409616 | tf_op jit(solution)/shard_map/reduce_scatter | solution.py:365
  960.6 67.2 %reduce-scatter.31.cloned.1.call-done = bf16[320,288]{1,0:T(8,128)(2,1)} async-done(((bf16[2560,288]{1,0:T(8,128)(2,1)}), bf16[320,288]{1,0:T(8,128)(2,1)}) %reduce-scatter.31.cloned.1.call-update) | async-done | bytes 184336
  1029.7 86.9 %reduce-scatter.17.cloned.1.call-done = bf16[320,768]{1,0:T(8,128)(2,1)} async-done(((bf16[2560,768]{1,0:T(8,128)(2,1)}), bf16[320,768]{1,0:T(8,128)(2,1)}) %reduce-scatter.17.cloned.1.call-update) | async-done | bytes 491536 | tf_op jit(solution)/shard_map/reduce_scatter | solution.py:347
  1118.6 151.2 %reduce-scatter.27.cloned.1.call-done = bf16[320,1600]{1,0:T(8,128)(2,1)} async-done(((bf16[2560,1600]{1,0:T(8,128)(2,1)}), bf16[320,1600]{1,0:T(8,128)(2,1)}) %reduce-scatter.27.cloned.1.call-update) | async-done | bytes 1024016 | tf_op jit(solution)/shard_map/reduce_scatter | solution.py:374
  1272.6 151.1 %reduce-scatter.25.cloned.1.call-done = bf16[320,1600]{1,0:T(8,128)(2,1)} async-done(((bf16[2560,1600]{1,0:T(8,128)(2,1)}), bf16[320,1600]{1,0:T(8,128)(2,1)}) %reduce-scatter.25.cloned.1.call-update) | async-done | bytes 1024016 | tf_op jit(solution)/shard_map/reduce_scatter | solution.py:371
  1426.4 151.5 %reduce-scatter.29.cloned.1.call-done = bf16[1600,320]{0,1:T(8,128)(2,1)} async-done(((bf16[1600,2560]{0,1:T(8,128)(2,1)}), bf16[1600,320]{0,1:T(8,128)(2,1)}) %reduce-scatter.29.cloned.1.call-update) | async-done | bytes 1024016 | tf_op jit(solution)/shard_map/reduce_scatter | solution.py:377
  (622 shorter events, 389.9 us)
Async XLA Ops:
  7.2 226.2 %copy-start = (bf16[640,2560]{1,0:T(8,128)(2,1)S(1)}, bf16[640,2560]{1,0:T(8,128)(2,1)}, u32[]{:S(2)}) copy-start(bf16[640,2560]{1,0:T(8,128)(2,1)} %param.37) | copy-start | bytes 9830404
  7.2 39.1 %all-gather.2.cloned.1.call-start = ((), (), s32[]{:S(2)}) async-start(), calls=%async_computation.10 | async-start | bytes 1310720 | tf_op jit(solution)/shard_map/all_gather | solution.py:145
  9.7 5.6 copy-start.39
  9.7 4.7 copy-start.41
  9.8 5.5 copy-start.30
  15.2 281.2 %all-reduce.10.cloned.1.call-start = ((), (), s32[]{:S(2)}) async-start(), calls=%async_computation.11 | async-start | bytes 5242880 | tf_op jit(solution)/shard_map/psum | solution.py:212
  15.3 6.4 copy-start.53
  15.3 7.2 copy-start.48
  22.5 3.9 copy-start.37
  26.5 12.8 copy-start.51
  27.5 11.9 copy-start.23
  27.5 11.9 copy-start.25
  237.1 63.1 %copy-start.27 = (f32[2560]{0:T(1024)S(1)}, f32[2560]{0:T(1024)}, u32[]{:S(2)}) copy-start(f32[2560]{0:T(1024)} %param.38) | copy-start | bytes 30724
  237.1 166.8 %all-reduce.12.cloned.1.call-start = ((), (), s32[]{:S(2)}) async-start(), calls=%async_computation.12 | async-start | bytes 5242880 | tf_op jit(solution)/shard_map/psum | solution.py:232
  296.4 4.1 copy-start.10
  300.5 357.0 %copy-start.34 = (f32[512]{0:T(512)}, f32[512]{0:T(512)S(1)}, u32[]{:S(2)}) copy-start(f32[512]{0:T(512)S(1)} %add_rsqrt_fusion) | copy-start | bytes 6148
  300.5 11.2 slice-start.2
  301.9 9.8 copy-start.18
  301.9 9.8 slice-start.3
  311.7 6.5 copy-start.17
  311.7 25.1 %slice-start = ((s8[8192000]{0:T(1024)(128)(4,1)}), s8[4194304]{0:T(1024)(128)(4,1)S(1)}, s32[]{:S(2)}) async-start(s8[8192000]{0:T(1024)(128)(4,1)} %bitcast.221), calls=%async_computation.24 | async-start | bytes 8388608
  318.2 18.6 %slice-start.1 = ((s8[8192000]{0:T(1024)(128)(4,1)}), s8[3997696]{0:T(1024)(128)(4,1)S(1)}, s32[]{:S(2)}) async-start(s8[8192000]{0:T(1024)(128)(4,1)} %bitcast.221), calls=%async_computation.25 | async-start | bytes 7995392
  329.7 7.1 copy-start.16
  343.8 300.3 %reduce-scatter.13.cloned.1.call-start = ((), (), s32[]{:S(2)}) async-start(), calls=%async_computation.13 | async-start | bytes 1310720 | tf_op jit(solution)/shard_map/reduce_scatter | solution.py:298
  403.9 6.2 copy-start.4
  403.9 6.2 copy-start.11
  403.9 6.2 copy-start.12
  410.1 247.4 %copy-start.43 = (f32[512]{0:T(512)}, f32[512]{0:T(512)S(1)}, u32[]{:S(2)}) copy-start(f32[512]{0:T(512)S(1)} %broadcast_multiply_fusion.4) | copy-start | bytes 6148
  423.8 5.4 copy-start.2
  610.1 10.4 copy-start.55
  620.5 46.0 %reduce-scatter.15.cloned.1.call-start = ((), (), s32[]{:S(2)}) async-start(), calls=%async_computation.14 | async-start | bytes 163840 | tf_op jit(solution)/shard_map/reduce_scatter | solution.py:301
  620.5 11.1 copy-start.24
  620.6 11.1 copy-start.26
  633.3 112.6 %all-reduce.14.cloned.1.call-start = ((), (), s32[]{:S(2)}) async-start(), calls=%async_computation.23 | async-start | bytes 7340032 | tf_op jit(solution)/shard_map/psum | solution.py:220
  633.4 10.7 copy-start.22
  633.5 10.8 copy-start.15
  644.2 9.1 copy-start.46
  644.2 9.1 copy-start.49
  644.2 165.3 %reduce-scatter.21.cloned.1.call-start = ((), (), s32[]{:S(2)}) async-start(), calls=%async_computation.17 | async-start | bytes 737280 | tf_op jit(solution)/shard_map/reduce_scatter | solution.py:362
  653.2 4.4 copy-start.5
  653.2 4.4 copy-start.20
  653.2 224.6 %reduce-scatter.19.cloned.1.call-start = ((), (), s32[]{:S(2)}) async-start(), calls=%async_computation.16 | async-start | bytes 1769472 | tf_op jit(solution)/shard_map/reduce_scatter | solution.py:359
  657.5 301.2 %reduce-scatter.23.cloned.1.call-start = ((), (), s32[]{:S(2)}) async-start(), calls=%async_computation.18 | async-start | bytes 3686400 | tf_op jit(solution)/shard_map/reduce_scatter | solution.py:365
  666.4 11.9 copy-start.38
  666.4 11.9 copy-start.52
  666.4 79.5 %copy-start.14 = (f32[512,288]{0,1:T(8,128)S(1)}, f32[512,288]{0,1:T(8,128)}, u32[]{:S(2)}) copy-start(f32[512,288]{0,1:T(8,128)} %copy-done.13) | copy-start | bytes 1769476
  666.4 79.5 %copy-start.33 = (f32[512]{0:T(512)S(1)}, f32[512]{0:T(512)}, u32[]{:S(2)}) copy-start(f32[512]{0:T(512)} %copy-done.32) | copy-start | bytes 6148
  666.4 79.5 %copy-start.42 = (f32[256]{0:T(256)S(1)}, f32[256]{0:T(256)}, u32[]{:S(2)}) copy-start(f32[256]{0:T(256)} %param.34) | copy-start | bytes 3076
  666.5 361.3 %reduce-scatter.31.cloned.1.call-start = ((), (), s32[]{:S(2)}) async-start(), calls=%async_computation.22 | async-start | bytes 2211840
  751.0 3.9 copy-start.47
  751.1 3.9 copy-start.50
  751.1 6.2 copy-start.31
  751.1 6.2 copy-start.40
  754.9 361.6 %reduce-scatter.17.cloned.1.call-start = ((), (), s32[]{:S(2)}) async-start(), calls=%async_computation.15 | async-start | bytes 4423680 | tf_op jit(solution)/shard_map/reduce_scatter | solution.py:347
  763.4 506.3 %reduce-scatter.27.cloned.1.call-start = ((), (), s32[]{:S(2)}) async-start(), calls=%async_computation.20 | async-start | bytes 9584640 | tf_op jit(solution)/shard_map/reduce_scatter | solution.py:374
  774.1 649.6 %reduce-scatter.25.cloned.1.call-start = ((), (), s32[]{:S(2)}) async-start(), calls=%async_computation.19 | async-start | bytes 9584640 | tf_op jit(solution)/shard_map/reduce_scatter | solution.py:371
  784.7 793.2 %reduce-scatter.29.cloned.1.call-start = ((), (), s32[]{:S(2)}) async-start(), calls=%async_computation.21 | async-start | bytes 9584640 | tf_op jit(solution)/shard_map/reduce_scatter | solution.py:377
  879.5 5.3 copy-start.21
  879.5 5.3 copy-start.28
  879.5 5.3 copy-start.29
  884.8 4.3 copy-start.36
  884.8 33.3 %copy-start.35 = (f32[512]{0:T(512)S(1)}, f32[512]{0:T(512)}, u32[]{:S(2)}) copy-start(f32[512]{0:T(512)} %copy-done.34) | copy-start | bytes 6148
  884.8 33.3 %copy-start.44 = (f32[512]{0:T(512)S(1)}, f32[512]{0:T(512)}, u32[]{:S(2)}) copy-start(f32[512]{0:T(512)} %copy-done.43) | copy-start | bytes 6148
  1269.8 310.8 %copy-start.1 = (bf16[640,2560]{1,0:T(8,128)(2,1)S(1)}, bf16[640,2560]{1,0:T(8,128)(2,1)}, u32[]{:S(2)}) copy-start(bf16[640,2560]{1,0:T(8,128)(2,1)} %param.37) | copy-start | bytes 9830404
  (38 other events, 72.1 us)
Sparse Core Ops, SparseCore 0:
  15.4 30.9 all-gather.1
  237.3 59.1 all-reduce.9
  343.9 59.9 all-reduce.11
  620.6 23.4 reduce-scatter.12
  646.9 15.3 reduce-scatter.14
  665.8 80.0 all-reduce.13
  749.2 60.2 reduce-scatter.20
  813.8 63.8 reduce-scatter.18
  881.4 77.2 reduce-scatter.22
  962.9 64.7 reduce-scatter.30
  1031.4 85.0 reduce-scatter.16
  1120.4 149.3 reduce-scatter.26
  1273.4 150.2 reduce-scatter.24
  1427.6 150.2 reduce-scatter.28
where the time goes:
time: 1600 us; the launch traced here: 1590 us
  waiting for transfers between devices  916 us (57%)
  matrix products  411 us (26%)
  local copies, waits for them, and re-layouts  72.6 us (5%)
  other arithmetic  71 us (4%)
  blocking collectives  50.7 us (3%)
  loops' own time  49.2 us (3%)
  between operations  16.8 us (1%)
    reduce_scatter x1, waiting for transfers between devices, per_device(): lax.psum_scatter(totals[11].astype(jnp.bfloat16), ('dp', 'context'), scat...  152 us
    reduce_scatter x1, waiting for transfers between devices, per_device(): lax.psum_scatter(totals[10].astype(jnp.bfloat16), ('dp', 'context'), scat...  151 us
    reduce_scatter x1, waiting for transfers between devices, per_device(): lax.psum_scatter(totals[9].astype(jnp.bfloat16), ('dp', 'context'), scatt...  151 us
    reduce_scatter x1, waiting for transfers between devices, per_device(): lax.psum_scatter(totals[1].astype(jnp.bfloat16), ('dp', 'context'), scatt...  86.9 us
    unnamed x15, waiting for transfers between devices  67.4 us
    psum x1, waiting for transfers between devices, per_device(): lax.psum(matmul(hidden_mid, down_proj).astype(jnp.bfloat16), 'tensor')  66.8 us
    reduce_scatter x1, waiting for transfers between devices, per_device(): lax.psum_scatter(totals[5].astype(jnp.bfloat16), ('dp', 'context'), scatt...  66.7 us
    dot_general x24, matrix products, block_scores(): jnp.einsum('qhd,kd->hqk', query_rope, rope_block, preferred_element_type=...  65.5 us
  transfers between devices with their start and end apart: 14, of which 13 were waited for; matrix products, arithmetic and copies ran while one was open for 9% of the time, Pallas kernels for 0%

commit v1 on v0

v1 whole, which is shorter than its diff:
```python
import functools
import math

import jax
import jax.numpy as jnp
from jax import lax
from jax.experimental import pallas as pl
from jax.experimental.pallas import tpu as pltpu
from jax.sharding import PartitionSpec as P

NOPE = 64
ROPE = 32
V_DIM = 64
KV_RANK = 256
HALF = 256
GROUP = 5

EPS = 1e-05
RESIDUAL = 1.4 / math.sqrt(62.0)
SCALE = 1.0 / math.sqrt(NOPE + ROPE)
LOG2E = 1.0 / math.log(2.0)
F32 = jnp.float32
BF16 = jnp.bfloat16


def matmul(left, right):
    return jnp.dot(left, right, preferred_element_type=F32)


def times_transposed(left, right):
    return lax.dot_general(left, right, (((1,), (1,)), ((), ())), preferred_element_type=F32)


def transposed_times(left, right):
    return lax.dot_general(left, right, (((0,), (0,)), ((), ())), preferred_element_type=F32)


def scaled(value):
    inverse = lax.rsqrt(jnp.mean(value * value, axis=-1, keepdims=True) + EPS)
    return (value * inverse, inverse)


def norm_back(incoming, normed, inverse, gain):
    weighted = incoming * gain
    grad_gain = jnp.sum(incoming * normed, axis=0)
    grad_value = inverse * (weighted - normed * jnp.mean(weighted * normed, axis=-1, keepdims=True))
    return (grad_value, grad_gain)


def rotate(value, cosine, sine):
    count = value.shape[-1] // 2
    first = value[..., :count]
    second = value[..., count:]
    return jnp.concatenate(
        [first * cosine - second * sine, second * cosine + first * sine], axis=-1
    )


def unrotate(value, cosine, sine):
    count = value.shape[-1] // 2
    first = value[..., :count]
    second = value[..., count:]
    return jnp.concatenate(
        [first * cosine + second * sine, second * cosine - first * sine], axis=-1
    )


def load_heads(heads, latent, rope_keys, latent_up, q_t, kcat, q_wide):
    for h in range(heads):
        kcat[h, :, :128] = matmul(latent[...], latent_up[:, h * 128 : (h + 1) * 128]).astype(BF16)
        kcat[h, :, 128:] = rope_keys[...]
        q_wide[h, 0:64, :] = q_t[h, 0:64, :]
        q_wide[h, 64:128, :] = jnp.zeros((64, q_wide.shape[2]), BF16)
        q_wide[h, 128:160, :] = q_t[h, 64:96, :]
        q_wide[h, 160:256, :] = jnp.zeros((96, q_wide.shape[2]), BF16)


def causal():
    key_row = lax.broadcasted_iota(jnp.int32, (HALF, HALF), 0)
    query_col = lax.broadcasted_iota(jnp.int32, (HALF, HALF), 1)
    return key_row <= query_col


def fold(value, op):
    return op(value.reshape(HALF // 8, 8, value.shape[-1]), axis=0)


def forward_kernel(
    heads,
    place,
    q_t,
    latent,
    latent_t,
    rope_keys,
    latent_up,
    latent_up_t,
    joined_t,
    exact_t,
    lse,
    kcat,
    v_t,
    q_wide,
    scores,
    top,
    total,
    acc,
):
    load_heads(heads, latent, rope_keys, latent_up, q_t, kcat, q_wide)
    for h in range(heads):
        v_t[h] = matmul(latent_up_t[h * 128 + 64 : (h + 1) * 128, :], latent_t[...]).astype(BF16)
    factor = SCALE * LOG2E
    for block in range(2):
        cols = slice(block * HALF, (block + 1) * HALF)
        position = place[block]

        def score(j, masked):
            rows = pl.ds(pl.multiple_of(place[2 + j], HALF), HALF)
            spot = pl.ds(pl.multiple_of(j * HALF, HALF), HALF)
            for h in range(heads):
                s = matmul(kcat[h, rows, :], q_wide[h, :, cols])
                if masked:
                    s = jnp.where(causal(), s, -1e30)
                scores[h, spot, :] = s
                peak = fold(s, jnp.max)
                top[h] = peak if masked else jnp.maximum(top[h], peak)

        score(position, True)

        @pl.loop(0, position)
        def _(j):
            score(j, False)

        for h in range(heads):
            peak = jnp.max(top[h], axis=0, keepdims=True) * factor
            top[h] = jnp.broadcast_to(peak, (8, HALF))
            total[h] = jnp.zeros((8, HALF), F32)
            acc[h] = jnp.zeros((V_DIM, HALF), F32)

        @pl.loop(0, position + 1)
        def _(j):
            rows = pl.ds(pl.multiple_of(place[2 + j], HALF), HALF)
            spot = pl.ds(pl.multiple_of(j * HALF, HALF), HALF)
            for h in range(heads):
                p = jnp.exp2(scores[h, spot, :] * factor - top[h, 0:1, :])
                total[h] += fold(p, jnp.sum)
                acc[h] += matmul(v_t[h, :, rows], p.astype(BF16))

        for h in range(heads):
            summed = jnp.sum(total[h], axis=0, keepdims=True)
            out = acc[h] / summed
            joined_t[h * V_DIM : (h + 1) * V_DIM, cols] = out.astype(BF16)
            exact_t[h, :, cols] = out
            lse[h, :, cols] = top[h, 0:1, :] + jnp.log2(summed)


def backward_kernel(
    heads,
    place,
    q_t,
    latent,
    latent_t,
    rope_keys,
    rope_keys_t,
    latent_up,
    latent_up_t,
    exact_t,
    lse,
    dmix_t,
    cos_t,
    sin_t,
    dq_t,
    grad_up,
    dlat_t,
    kcat,
    k_t,
    q_wide,
    dmix_wide,
    delta,
    dk,
    dq,
    lat_acc,
    rope_acc,
):
    factor = SCALE * LOG2E
    step = pl.program_id(0)
    load_heads(heads, latent, rope_keys, latent_up, q_t, kcat, q_wide)
    for h in range(heads):
        k_t[h, 0:64, :] = matmul(latent_up_t[h * 128 : h * 128 + 64, :], latent_t[...]).astype(BF16)
        k_t[h, 64:96, :] = rope_keys_t[...]
        piece = dmix_t[h * V_DIM : (h + 1) * V_DIM, :]
        dmix_wide[h, 0:64, :] = jnp.zeros_like(piece)
        dmix_wide[h, 64:128, :] = piece
        delta[h] = jnp.sum(piece.astype(F32) * exact_t[h], axis=0, keepdims=True)
        dk[h] = jnp.zeros(dk.shape[1:], F32)

    for block in range(2):
        cols = slice(block * HALF, (block + 1) * HALF)
        position = place[block]

        def tile(j, masked):
            rows = pl.ds(pl.multiple_of(place[2 + j], HALF), HALF)
            for h in range(heads):
                s = matmul(kcat[h, rows, :], q_wide[h, :, cols])
                p = jnp.exp2(s * factor - lse[h, :, cols])
                if masked:
                    p = jnp.where(causal(), p, 0.0)
                dp = matmul(kcat[h, rows, :128], dmix_wide[h, :, cols])
                ds = (p * (dp - delta[h, :, cols])).astype(BF16)
                change = matmul(k_t[h, :, rows], ds)
                dq[h] = change if masked else dq[h] + change
                dk[h, rows, :] += times_transposed(ds, q_wide[h, :, cols])
                dk[h, rows, :128] += times_transposed(p.astype(BF16), dmix_wide[h, :, cols])

        tile(position, True)

        @pl.loop(0, position)
        def _(j):
            tile(j, False)

        cosine = cos_t[:, cols]
        sine = sin_t[:, cols]
        for h in range(heads):
            value = dq[h] * SCALE
            first = value[64:80]
            second = value[80:96]
            dq_t[h, 0:64, cols] = value[0:64].astype(BF16)
            dq_t[h, 64:80, cols] = (first * cosine + second * sine).astype(BF16)
            dq_t[h, 80:96, cols] = (second * cosine - first * sine).astype(BF16)

    @pl.when(step == 0)
    def _():
        lat_acc[...] = jnp.zeros_like(lat_acc)
        rope_acc[...] = jnp.zeros_like(rope_acc)

    lane = lax.broadcasted_iota(jnp.int32, (1, 128), 1)
    weight = jnp.where(lane < NOPE, SCALE, 1.0).astype(F32)
    for h in range(heads):
        pair = (dk[h, :, :128] * weight).astype(BF16)
        grad_up[:, h * 128 : (h + 1) * 128] = matmul(latent_t[...], pair).astype(BF16)
        lat_acc[...] += times_transposed(latent_up[:, h * 128 : (h + 1) * 128], pair)
        rope_acc[...] += dk[h, :, 128:]

    @pl.when(step == pl.num_programs(0) - 1)
    def _():
        dlat_t[0:KV_RANK, :] = lat_acc[...].astype(BF16)
        dlat_t[KV_RANK:, :] = (rope_acc[...] * SCALE).T[:ROPE].astype(BF16)


def whole_spec(shape):
    return pl.BlockSpec(shape, lambda g: (0,) * len(shape))


def attention_forward(place, q_t, latent, latent_t, rope_keys, latent_up, latent_up_t):
    count, _, rows = q_t.shape
    keys = latent.shape[0]
    heads = GROUP
    flops = 2 * count * rows * keys * 384
    return pl.pallas_call(
        functools.partial(forward_kernel, heads),
        grid=(count // heads,),
        in_specs=[
            pl.BlockSpec(memory_space=pltpu.SMEM),
            pl.BlockSpec((heads, 96, rows), lambda g: (g, 0, 0)),
            whole_spec((keys, KV_RANK)),
            whole_spec((KV_RANK, keys)),
            whole_spec((keys, 128)),
            pl.BlockSpec((KV_RANK, heads * 128), lambda g: (0, g)),
            pl.BlockSpec((heads * 128, KV_RANK), lambda g: (g, 0)),
        ],
        out_specs=[
            pl.BlockSpec((heads * V_DIM, rows), lambda g: (g, 0)),
            pl.BlockSpec((heads, V_DIM, rows), lambda g: (g, 0, 0)),
            pl.BlockSpec((heads, 1, rows), lambda g: (g, 0, 0)),
        ],
        out_shape=[
            jax.ShapeDtypeStruct((count * V_DIM, rows), BF16),
            jax.ShapeDtypeStruct((count, V_DIM, rows), F32),
            jax.ShapeDtypeStruct((count, 1, rows), F32),
        ],
        scratch_shapes=[
            pltpu.VMEM((heads, keys, 256), BF16),
            pltpu.VMEM((heads, V_DIM, keys), BF16),
            pltpu.VMEM((heads, 256, rows), BF16),
            pltpu.VMEM((heads, keys, HALF), F32),
            pltpu.VMEM((heads, 8, HALF), F32),
            pltpu.VMEM((heads, 8, HALF), F32),
            pltpu.VMEM((heads, V_DIM, HALF), F32),
        ],
        compiler_params=pltpu.CompilerParams(vmem_limit_bytes=56 * 1024 * 1024),
        cost_estimate=pl.CostEstimate(
            flops=flops, bytes_accessed=12 * 1024 * 1024, transcendentals=count * rows * keys
        ),
        name="attention_forward",
    )(place, q_t, latent, latent_t, rope_keys, latent_up, latent_up_t)


def attention_backward(
    place,
    q_t,
    latent,
    latent_t,
    rope_keys,
    rope_keys_t,
    latent_up,
    latent_up_t,
    exact_t,
    lse,
    dmix_t,
    cos_t,
    sin_t,
):
    count, _, rows = q_t.shape
    keys = latent.shape[0]
    heads = GROUP
    flops = 2 * count * rows * keys * 1000
    return pl.pallas_call(
        functools.partial(backward_kernel, heads),
        grid=(count // heads,),
        in_specs=[
            pl.BlockSpec(memory_space=pltpu.SMEM),
            pl.BlockSpec((heads, 96, rows), lambda g: (g, 0, 0)),
            whole_spec((keys, KV_RANK)),
            whole_spec((KV_RANK, keys)),
            whole_spec((keys, 128)),
            whole_spec((ROPE, keys)),
            pl.BlockSpec((KV_RANK, heads * 128), lambda g: (0, g)),
            pl.BlockSpec((heads * 128, KV_RANK), lambda g: (g, 0)),
            pl.BlockSpec((heads, V_DIM, rows), lambda g: (g, 0, 0)),
            pl.BlockSpec((heads, 1, rows), lambda g: (g, 0, 0)),
            pl.BlockSpec((heads * V_DIM, rows), lambda g: (g, 0)),
            whole_spec((ROPE // 2, rows)),
            whole_spec((ROPE // 2, rows)),
        ],
        out_specs=[
            pl.BlockSpec((heads, 96, rows), lambda g: (g, 0, 0)),
            pl.BlockSpec((KV_RANK, heads * 128), lambda g: (0, g)),
            whole_spec((KV_RANK + ROPE, keys)),
        ],
        out_shape=[
            jax.ShapeDtypeStruct((count, 96, rows), BF16),
            jax.ShapeDtypeStruct((KV_RANK, count * 128), BF16),
            jax.ShapeDtypeStruct((KV_RANK + ROPE, keys), BF16),
        ],
        scratch_shapes=[
            pltpu.VMEM((heads, keys, 256), BF16),
            pltpu.VMEM((heads, 96, keys), BF16),
            pltpu.VMEM((heads, 256, rows), BF16),
            pltpu.VMEM((heads, 128, rows), BF16),
            pltpu.VMEM((heads, 1, rows), F32),
            pltpu.VMEM((heads, keys, 256), F32),
            pltpu.VMEM((heads, 96, HALF), F32),
            pltpu.VMEM((KV_RANK, keys), F32),
            pltpu.VMEM((keys, 128), F32),
        ],
        compiler_params=pltpu.CompilerParams(vmem_limit_bytes=60 * 1024 * 1024),
        cost_estimate=pl.CostEstimate(
            flops=flops, bytes_accessed=16 * 1024 * 1024, transcendentals=count * rows * keys
        ),
        name="attention_backward",
    )(
        place,
        q_t,
        latent,
        latent_t,
        rope_keys,
        rope_keys_t,
        latent_up,
        latent_up_t,
        exact_t,
        lse,
        dmix_t,
        cos_t,
        sin_t,
    )


def swap(value, axis, size, bit):
    return lax.ppermute(value, axis, [(i, i ^ bit) for i in range(size)])


def shift(value, axis, size, by):
    return lax.ppermute(value, axis, [(i, (i + by) % size) for i in range(size)])


def tensor_sum(value, size):
    low = value.astype(BF16)
    bit = lax.axis_index("tensor") % 2
    half = low.shape[0] // 2
    keep = lax.dynamic_slice_in_dim(low, bit * half, half, 0)
    give = lax.dynamic_slice_in_dim(low, (1 - bit) * half, half, 0)
    mine = (keep.astype(F32) + swap(give, "tensor", size, 1).astype(F32)).astype(BF16)
    step = 2
    while step < size:
        mine = (mine.astype(F32) + swap(mine, "tensor", size, step).astype(F32)).astype(BF16)
        step *= 2
    other = swap(mine, "tensor", size, 1)
    first = jnp.where(bit == 0, mine, other)
    second = jnp.where(bit == 0, other, mine)
    return jnp.concatenate([first, second], axis=0).astype(F32)


def line_scatter(pieces, size):
    z = lax.axis_index("context")
    last = size - 1

    def take(index):
        return lax.dynamic_index_in_dim(pieces, index, 0, keepdims=False)

    right = left = None
    for step in range(1, size):
        up = take(jnp.clip(size + z - step, 0, last))
        down = take(jnp.clip(last - (size + (last - z) - step), 0, last))
        if right is not None:
            up = (up.astype(F32) + right.astype(F32)).astype(BF16)
            down = (down.astype(F32) + left.astype(F32)).astype(BF16)
        right = lax.ppermute(up, "context", [(i, i + 1) for i in range(step)])
        left = lax.ppermute(down, "context", [(last - i, last - i - 1) for i in range(step)])
    return take(z).astype(F32) + right.astype(F32) + left.astype(F32)


def direct_scatter(pieces, size):
    z = lax.axis_index("context")
    total = lax.dynamic_index_in_dim(pieces, z, 0, keepdims=False).astype(F32)
    for by in range(1, size):
        piece = lax.dynamic_index_in_dim(pieces, (z + by) % size, 0, keepdims=False)
        total = total + shift(piece, "context", size, by).astype(F32)
    return total


def pair_scatter(value):
    d = lax.axis_index("dp")
    keep = lax.dynamic_index_in_dim(value, d, 0, keepdims=False)
    give = lax.dynamic_index_in_dim(value, 1 - d, 0, keepdims=False)
    return (keep.astype(F32) + swap(give, "dp", 2, 1).astype(F32)).astype(BF16)


def tensor_gather(value, size):
    t = lax.axis_index("tensor")
    out = jnp.zeros((size,) + value.shape, value.dtype)
    out = lax.dynamic_update_index_in_dim(out, value, t, 0)
    for by in range(1, size):
        got = shift(value, "tensor", size, by)
        out = lax.dynamic_update_index_in_dim(out, got, (t - by) % size, 0)
    return out


def per_device(
    sizes,
    tokens,
    cotangent,
    group_order,
    attn_gain,
    query_down,
    query_gain,
    latent_down,
    latent_gain,
    query_up,
    latent_up,
    attn_out,
    mlp_gain,
    gate_proj,
    up_proj,
    down_proj,
):
    contexts, tensors = sizes
    rows, width = tokens.shape[1:]
    blocks = group_order.shape[0]
    heads = query_up.shape[1] // (NOPE + ROPE)
    z = lax.axis_index("context")
    d = lax.axis_index("dp")
    t = lax.axis_index("tensor")
    half_width = width // 2

    mine = lax.dynamic_slice_in_dim(group_order, 2 * z, 2)
    offsets = jnp.arange(HALF, dtype=jnp.int32)
    query_pos = (mine[:, None] * HALF + offsets[None, :]).reshape(rows)
    index = jnp.arange(blocks, dtype=jnp.int32)
    spot = ((z - index // 2) % contexts) * 2 * HALF + (index % 2) * HALF
    where = jnp.sum(
        jnp.where(group_order[None, :] == index[:, None], spot[None, :], 0), axis=1
    ).astype(jnp.int32)
    place = jnp.concatenate([mine, where])

    freq = 10000.0 ** (-2.0 * jnp.arange(ROPE // 2, dtype=F32) / ROPE)
    angle = query_pos.astype(F32)[:, None] * freq[None, :]
    cosine, sine = jnp.cos(angle), jnp.sin(angle)
    angle_t = freq[:, None] * query_pos.astype(F32)[None, :]
    cos_t, sin_t = jnp.cos(angle_t), jnp.sin(angle_t)

    inputs = tokens[0].astype(F32)
    upstream = cotangent[0].astype(F32)
    grad_feed = (RESIDUAL * upstream).astype(BF16)

    def own_half(value):
        return lax.dynamic_slice_in_dim(value, d * half_width, half_width, 1)

    def other_half(value):
        return lax.dynamic_slice_in_dim(value, (1 - d) * half_width, half_width, 1)

    grad_feed_both = jnp.concatenate(
        [own_half(grad_feed), swap(other_half(grad_feed), "dp", 2, 1)], axis=0
    )

    first_normed, first_inverse = scaled(inputs)
    hidden_one = (first_normed * attn_gain).astype(BF16)
    latent_raw = matmul(hidden_one, latent_down)
    cache_normed, cache_inverse = scaled(latent_raw[:, :KV_RANK])
    latent = (cache_normed * latent_gain).astype(BF16)
    key_rope = rotate(latent_raw[:, KV_RANK:], cosine, sine).astype(BF16)
    keys_own = jnp.concatenate([latent, key_rope], axis=1)
    bit = t % 2
    part = lax.dynamic_slice_in_dim(keys_own, bit * (rows // 2), rows // 2, 0)
    far = jnp.stack([shift(part, "context", contexts, by) for by in range(1, contexts)])
    far_other = swap(far, "tensor", tensors, 1)
    far_all = jnp.concatenate(
        [jnp.where(bit == 0, far, far_other), jnp.where(bit == 0, far_other, far)], axis=1
    )
    keys_all = jnp.concatenate([keys_own[None], far_all], axis=0).reshape(
        contexts * rows, KV_RANK + ROPE
    )
    latent_all = keys_all[:, :KV_RANK]
    rope_all = jnp.pad(keys_all[:, KV_RANK:], ((0, 0), (0, 128 - ROPE)))
    keys_all_t = keys_all.T
    latent_all_t = keys_all_t[:KV_RANK]
    rope_all_t = keys_all_t[KV_RANK:]
    latent_up_t = latent_up.T

    query_low = matmul(hidden_one, query_down)
    query_normed, query_inverse = scaled(query_low)
    query_latent = (query_normed * query_gain).astype(BF16)
    query_full_t = lax.dot_general(
        query_up, query_latent, (((0,), (1,)), ((), ())), preferred_element_type=F32
    ).reshape(heads, NOPE + ROPE, rows)
    first = query_full_t[:, 64:80]
    second = query_full_t[:, 80:96]
    q_t = jnp.concatenate(
        [
            query_full_t[:, :64],
            first * cos_t - second * sin_t,
            second * cos_t + first * sin_t,
        ],
        axis=1,
    ).astype(BF16)

    joined_t, exact_t, lse = attention_forward(
        place, q_t, latent_all, latent_all_t, rope_all, latent_up, latent_up_t
    )

    branch = tensor_sum(transposed_times(joined_t, attn_out), tensors)
    middle = inputs + RESIDUAL * branch
    second_normed, second_inverse = scaled(middle)
    hidden_two = (second_normed * mlp_gain).astype(BF16)
    hidden_two_both = jnp.concatenate(
        [own_half(hidden_two), swap(other_half(hidden_two), "dp", 2, 1)], axis=0
    )
    grad_hidden = times_transposed(grad_feed, down_proj)
    gate = matmul(hidden_two, gate_proj)
    upper = matmul(hidden_two, up_proj)
    sigma = jax.nn.sigmoid(gate)
    hidden_mid = (gate * sigma * upper).astype(BF16)
    grad_gate = (grad_hidden * upper * sigma * (1.0 + gate * (1.0 - sigma))).astype(BF16)
    grad_upper = (grad_hidden * gate * sigma).astype(BF16)

    def both(value):
        return jnp.concatenate([value, swap(value, "dp", 2, 1)], axis=0)

    def weight_pieces(left, right):
        full = transposed_times(left, right).astype(BF16)
        return full.reshape(contexts, half_width // contexts, right.shape[1])

    grad_hidden_two = tensor_sum(
        times_transposed(grad_gate, gate_proj) + times_transposed(grad_upper, up_proj), tensors
    )
    feed = tensor_sum(matmul(hidden_mid, down_proj), tensors)
    layer_out = (middle + RESIDUAL * feed).astype(BF16)

    grad_down = line_scatter(weight_pieces(grad_feed_both, both(hidden_mid)), contexts).T
    grad_gate_proj = line_scatter(weight_pieces(hidden_two_both, both(grad_gate)), contexts)
    grad_up_proj = line_scatter(weight_pieces(hidden_two_both, both(grad_upper)), contexts)

    grad_norm_two, grad_mlp_gain = norm_back(
        grad_hidden_two, second_normed, second_inverse, mlp_gain
    )
    grad_middle = upstream + grad_norm_two
    grad_branch = (RESIDUAL * grad_middle).astype(BF16)
    grad_attn_out_t = lax.dot_general(
        grad_branch, joined_t, (((0,), (1,)), ((), ())), preferred_element_type=F32
    ).astype(BF16)
    grad_attn_out = line_scatter(
        pair_scatter(
            grad_attn_out_t.reshape(2, contexts, half_width // contexts, joined_t.shape[0])
        ),
        contexts,
    ).T
    dmix_t = times_transposed(attn_out, grad_branch).astype(BF16)

    dq_t, grad_latent_up, dlat_t = attention_backward(
        place,
        q_t,
        latent_all,
        latent_all_t,
        rope_all,
        rope_all_t,
        latent_up,
        latent_up_t,
        exact_t,
        lse,
        dmix_t,
        cos_t,
        sin_t,
    )
    grad_query_full_t = dq_t.reshape(heads * (NOPE + ROPE), rows)
    grad_query_latent = tensor_sum(
        lax.dot_general(
            grad_query_full_t, query_up, (((0,), (1,)), ((), ())), preferred_element_type=F32
        ),
        tensors,
    )
    grad_query_up = lax.dot_general(
        query_latent, grad_query_full_t, (((0,), (1,)), ((), ())), preferred_element_type=F32
    ).astype(BF16)

    dlat = tensor_sum(dlat_t, tensors).astype(BF16)
    total = dlat[:, :rows].astype(F32)
    for by in range(1, contexts):
        total = total + shift(dlat[:, by * rows : (by + 1) * rows], "context", contexts, -by).astype(
            F32
        )
    grad_keys = total.T
    grad_query_low, grad_query_gain = norm_back(
        grad_query_latent, query_normed, query_inverse, query_gain
    )
    grad_cache, grad_latent_gain = norm_back(
        grad_keys[:, :KV_RANK], cache_normed, cache_inverse, latent_gain
    )
    grad_low = jnp.concatenate(
        [grad_query_low, grad_cache, unrotate(grad_keys[:, KV_RANK:], cosine, sine)], axis=1
    ).astype(BF16)
    rank = query_down.shape[1]
    grad_hidden_one = times_transposed(grad_low[:, :rank], query_down) + times_transposed(
        grad_low[:, rank:], latent_down
    )
    grad_norm_one, grad_attn_gain = norm_back(
        grad_hidden_one, first_normed, first_inverse, attn_gain
    )
    token_grad = grad_middle + grad_norm_one

    grad_query_up = direct_scatter(
        pair_scatter(grad_query_up.reshape(2, contexts, -1, grad_query_up.shape[1])), contexts
    )
    grad_latent_up = direct_scatter(
        pair_scatter(grad_latent_up.reshape(2, contexts, -1, grad_latent_up.shape[1])), contexts
    )
    grad_down_low = transposed_times(hidden_one, grad_low).astype(BF16)
    grad_down_low = grad_down_low.reshape(2, contexts, tensors, -1, grad_low.shape[1])
    grad_down_low = lax.dynamic_index_in_dim(grad_down_low, t, 2, keepdims=False)
    grad_down_low = direct_scatter(pair_scatter(grad_down_low), contexts).astype(BF16)
    grad_down_low = (
        tensor_gather(grad_down_low, tensors).reshape(-1, grad_low.shape[1]).astype(F32)
    )

    def pieces(value):
        return value.reshape(2 * contexts, -1)

    gains = jnp.concatenate(
        [
            pieces(grad_attn_gain),
            pieces(grad_query_gain),
            pieces(grad_latent_gain),
            pieces(grad_mlp_gain),
        ],
        axis=1,
    )
    gains = lax.dynamic_index_in_dim(
        lax.psum(gains, ("dp", "context")), d * contexts + z, 0, keepdims=False
    )
    sizes = [v.shape[0] // (2 * contexts) for v in (attn_gain, query_gain, latent_gain, mlp_gain)]
    edges = [0]
    for size in sizes:
        edges.append(edges[-1] + size)
    gain_grads = [gains[a:b] for a, b in zip(edges[:-1], edges[1:])]

    return (
        layer_out[None],
        token_grad[None],
        gain_grads[0],
        grad_down_low[:, :rank],
        gain_grads[1],
        grad_down_low[:, rank:],
        gain_grads[2],
        grad_query_up,
        grad_latent_up,
        grad_attn_out,
        gain_grads[3],
        grad_gate_proj,
        grad_up_proj,
        grad_down,
    )


def solution(mesh):
    in_specs = (
        P("dp", "context", None),
        P("dp", "context", None),
        P(),
        P(),
        P(),
        P(),
        P(),
        P(),
        P(None, "tensor"),
        P(None, "tensor"),
        P("tensor", None),
        P(),
        P(None, "tensor"),
        P(None, "tensor"),
        P("tensor", None),
    )
    out_specs = (
        P("dp", "context", None),
        P("dp", "context", None),
        P(("dp", "context")),
        P(("dp", "context"), None),
        P(("dp", "context")),
        P(("dp", "context"), None),
        P(("dp", "context")),
        P(("dp", "context"), "tensor"),
        P(("dp", "context"), "tensor"),
        P("tensor", ("dp", "context")),
        P(("dp", "context")),
        P(("dp", "context"), "tensor"),
        P(("dp", "context"), "tensor"),
        P("tensor", ("dp", "context")),
    )
    sizes = (mesh.shape["context"], mesh.shape["tensor"])
    return jax.shard_map(
        functools.partial(per_device, sizes),
        mesh=mesh,
        in_specs=in_specs,
        out_specs=out_specs,
        check_vma=False,
    )
```

time: 1600 us -> 873 us (0.55)
  waiting for transfers between devices: 916 us -> 319 us
  matrix products: 411 us -> 117 us
  starting transfers between devices: 0.79 us -> 154 us
  Pallas kernels: 0 us -> 58.8 us
  loops' own time: 49.2 us -> 0 us
  other arithmetic: 71 us -> 93.7 us
  blocking collectives: 50.7 us -> 28.5 us
    reduce_scatter x9 -> x0, waiting for transfers between devices: 656 us -> none  [the longest x1 152 us: per_device(): lax.psum_scatter(totals[11].astype(jnp.bfloat16), ('dp', 'context'), scat...]
    ppermute x0 -> x67, waiting for transfers between devices: none -> 319 us  [the longest x25 147 us: swap(): return lax.ppermute(value, axis, [(i, i ^ bit) for i in range(size)])]
    dot_general x122 -> x9, matrix products: 312 us -> 45 us  [the longest x5 33.3 us: matmul(): return jnp.dot(left, right, preferred_element_type=F32)]
    psum x3 -> x0, waiting for transfers between devices: 186 us -> none  [the longest x1 66.8 us: per_device(): lax.psum(matmul(hidden_mid, down_proj).astype(jnp.bfloat16), 'tensor')]
    ppermute x0 -> x67, starting transfers between devices: none -> 154 us  [the longest x18 60.3 us: shift(): lax.ppermute(value, axis, [(i, (i + by) % size) for i in range(size)])]
    unnamed x15 -> x0, waiting for transfers between devices: 67.4 us -> none
    pallas_call x0 -> x2, Pallas kernels: none -> 58.8 us  [the longest x1 40.9 us: attention_backward(): pl.pallas_call(functools.partial(backward_kernel, heads), grid=(count //...]
    another operation x27 -> x0, loops' own time: 49.2 us -> none  [the longest x1 10.5 us: per_device(): top, total = lax.fori_loop(0, blocks, stats_step, (start_top, start_total))]
  transfers between devices with their start and end apart: 14 -> 67, of which waited for: 13 -> 21; matrix products, arithmetic and copies ran while one was open for 9% -> 26% of each run, Pallas kernels for 0% -> 5%
where the time goes in v1:
time: 873 us; the launch traced here: 862 us
  waiting for transfers between devices  319 us (37%)
  starting transfers between devices  154 us (18%)
  matrix products  117 us (13%)
  other arithmetic  93.7 us (11%)
  local copies, waits for them, and re-layouts  87.7 us (10%)
  Pallas kernels  58.8 us (7%)
  blocking collectives  28.5 us (3%)
    ppermute x25, waiting for transfers between devices, swap(): return lax.ppermute(value, axis, [(i, i ^ bit) for i in range(size)])  147 us
    ppermute x12, waiting for transfers between devices, line_scatter(): right = lax.ppermute(up, 'context', [(i, i + 1) for i in range(step)])  80.6 us
    ppermute x12, waiting for transfers between devices, line_scatter(): lax.ppermute(down, 'context', [(last - i, last - i - 1) for i in range(st...  73 us
    ppermute x18, starting transfers between devices, shift(): lax.ppermute(value, axis, [(i, (i + by) % size) for i in range(size)])  60.3 us
    pallas_call x1, Pallas kernels, attention_backward(): pl.pallas_call(functools.partial(backward_kernel, heads), grid=(count //...  40.9 us
    dot_general x6, matrix products, times_transposed(): lax.dot_general(left, right, (((1,), (1,)), ((), ())), preferred_element_...  38.6 us
    ppermute x25, starting transfers between devices, swap(): return lax.ppermute(value, axis, [(i, i ^ bit) for i in range(size)])  36.2 us
    dot_general x5, matrix products, transposed_times(): lax.dot_general(left, right, (((0,), (0,)), ((), ())), preferred_element_...  33.5 us
  transfers between devices with their start and end apart: 67, of which 21 were waited for; matrix products, arithmetic and copies ran while one was open for 26% of the time, Pallas kernels for 5%

profile of v1, /device:TPU:9, one launch (start us, length us, event | category | flops | bytes accessed | tf_op | source)
XLA Modules:
  0.0 861.6 jit_solution(15245031644127239476)
XLA Ops:
  16.1 5.3 multiply_reduce_fusion.1
  45.2 17.9 %attention_forward.1 = (bf16[640,512]{1,0:T(8,128)(2,1)}, f32[10,64,512]{2,1,0:T(8,128)}, f32[10,1,512]{2,1,0:T(1,128)}) custom-call(s32[10]{0:T(128)} %pad_add_fusion.place, bf16[10,96,512]{2,1,0:T(8,128)(2,1)} %pad_maximum_fusion.5.q_t, bf16[2048,256]{1,0:T(8,128)(2,1)} %copy.85.latent, bf16[256,2048]{1,0:T(8,128)(2,1)} %slice.128.latent_t, ...), custom_call_target="tpu_custom_call" | custom-call | flops 8053063680 | bytes 12582912 | tf_op jit(solution)/shard_map/attention_forward/pallas_call | solution.py:258
  63.1 3.3 convolution_convert_fusion.5
  66.7 3.0 collective-permute-done.4
  71.3 29.0 %collective-permute-done.5 = bf16[256,2560]{1,0:T(8,128)(2,1)S(1)} collective-permute-done((bf16[256,2560]{1,0:T(8,128)(2,1)S(1)}, bf16[256,2560]{1,0:T(8,128)(2,1)S(1)}, u32[]{:S(2)}, u32[]{:S(2)}) %collective-permute-start.5) | collective-permute-done | bytes 1310752 | tf_op jit(solution)/shard_map/ppermute | solution.py:378
  101.7 8.8 %fusion.114 = f32[512,1600]{0,1:T(8,128)} fusion(bf16[1600,2560]{1,0:T(8,128)(2,1)} %param.29, bf16[1,512,2560]{2,1,0:T(8,128)(2,1)S(1)} %copy-done.37), kind=kOutput, calls=%fused_computation.285 | convolution fusion | flops 4198236160 | bytes 14090240 | tf_op jit(solution)/shard_map/dot_general | solution.py:31
  115.7 4.4 fusion.122
  120.2 11.2 %multiply_convert_fusion.2 = (bf16[512,1600]{0,1:T(8,128)(2,1)S(1)}, bf16[512,1600]{0,1:T(8,128)(2,1)S(1)}, bf16[512,1600]{0,1:T(8,128)(2,1)}) fusion(f32[512,1600]{0,1:T(8,128)} %fusion.114, f32[512,1600]{0,1:T(8,128)S(1)} %fusion.122, bf16[512,2560]{1,0:T(8,128)(2,1)S(1)} %multiply_convert_fusion.1, bf16[2560,1600]{0,1:T(8,128)(2,1)} %param.27), kind=kOutput, calls=%fused_computation.53 | convolution fusion | flops 4207411200 | bytes 22282240 | tf_op jit(solution)/shard_map/dot_general | solution.py:27
  131.4 10.0 %convolution_convert_fusion.6 = bf16[512,2560]{1,0:T(8,128)(2,1)S(1)} fusion(bf16[512,1600]{0,1:T(8,128)(2,1)} %get-tuple-element.84, bf16[1600,2560]{1,0:T(8,128)(2,1)} %param.29), kind=kOutput, calls=%fused_computation.41 | convolution fusion | flops 4195614720 | bytes 12451840 | tf_op jit(solution)/shard_map/dot_general | solution.py:27
  143.3 7.5 fusion.123
  150.8 5.4 add_convert_fusion
  169.1 2.8 add_convert_fusion.2
  172.2 88.6 %collective-permute-done.44 = bf16[512,1280]{1,0:T(8,128)(2,1)S(1)} collective-permute-done((bf16[512,1280]{1,0:T(8,128)(2,1)S(1)}, bf16[512,1280]{1,0:T(8,128)(2,1)S(1)}, u32[]{:S(2)}, u32[]{:S(2)}) %collective-permute-start.44) | collective-permute-done | bytes 1310752 | tf_op jit(solution)/shard_map/ppermute | solution.py:378
  262.0 6.0 convolution_convert_fusion.2
  268.0 6.8 copy.96
  274.8 9.1 %convolution_convert_fusion.3 = bf16[1280,1600]{0,1:T(8,128)(2,1)} fusion(bf16[512,1600]{0,1:T(8,128)(2,1)} %collective-permute-done.45, bf16[512,1600]{0,1:T(8,128)(2,1)} %copy-done.71, bf16[512,1280]{1,0:T(8,128)(2,1)} %copy-done.73, bf16[512,1280]{1,0:T(8,128)(2,1)} %copy-done.42), kind=kOutput, calls=%fused_computation.3 | convolution fusion | flops 4208148480 | bytes 9994240 | tf_op jit(solution)/shard_map/dot_general | solution.py:35
  283.9 6.8 copy.95
  299.3 19.0 %collective-permute-done.46 = bf16[320,1600]{1,0:T(8,128)(2,1)S(1)} collective-permute-done((bf16[320,1600]{1,0:T(8,128)(2,1)S(1)}, bf16[320,1600]{1,0:T(8,128)(2,1)S(1)}, u32[]{:S(2)}, u32[]{:S(2)}) %collective-permute-start.46) | collective-permute-done | bytes 1024032 | tf_op jit(solution)/shard_map/ppermute | solution.py:416
  318.3 4.1 collective-permute-start.12
  322.7 18.4 %collective-permute-done.53 = bf16[320,1600]{1,0:T(8,128)(2,1)S(1)} collective-permute-done((bf16[320,1600]{1,0:T(8,128)(2,1)S(1)}, bf16[320,1600]{1,0:T(8,128)(2,1)S(1)}, u32[]{:S(2)}, u32[]{:S(2)}) %collective-permute-start.53) | collective-permute-done | bytes 1024032 | tf_op jit(solution)/shard_map/ppermute | solution.py:416
  345.2 3.1 add_convert_fusion.3
  349.5 16.3 %collective-permute-done.47 = bf16[320,1600]{1,0:T(8,128)(2,1)S(1)} collective-permute-done((bf16[320,1600]{1,0:T(8,128)(2,1)S(1)}, bf16[320,1600]{1,0:T(8,128)(2,1)S(1)}, u32[]{:S(2)}, u32[]{:S(2)}) %collective-permute-start.47) | collective-permute-done | bytes 1024032 | tf_op jit(solution)/shard_map/ppermute | solution.py:416
  365.9 5.8 collective-permute-start.9
  373.5 15.0 %collective-permute-done.54 = bf16[320,1600]{1,0:T(8,128)(2,1)S(1)} collective-permute-done((bf16[320,1600]{1,0:T(8,128)(2,1)S(1)}, bf16[320,1600]{1,0:T(8,128)(2,1)S(1)}, u32[]{:S(2)}, u32[]{:S(2)}) %collective-permute-start.54) | collective-permute-done | bytes 1024032 | tf_op jit(solution)/shard_map/ppermute | solution.py:416
  393.9 3.7 fusion.21
  397.7 6.3 fusion.22
  406.8 40.9 %attention_backward.1 = (bf16[10,96,512]{2,1,0:T(8,128)(2,1)}, bf16[256,1280]{1,0:T(8,128)(2,1)}, bf16[288,2048]{1,0:T(8,128)(2,1)}) custom-call(s32[10]{0:T(128)} %pad_add_fusion.place, bf16[10,96,512]{2,1,0:T(8,128)(2,1)} %pad_maximum_fusion.5.q_t, bf16[2048,256]{1,0:T(8,128)(2,1)} %copy.85.latent, bf16[256,2048]{1,0:T(8,128)(2,1)} %slice.128.latent_t, ...), custom_call_target="tpu_custom_call" | custom-call | flops 20971520000 | bytes 16777216 | tf_op jit(solution)/shard_map/attention_backward/pallas_call | solution.py:316
  452.6 3.4 collective-permute-start.16
  456.0 2.8 convolution_convert_fusion.8
  461.8 5.4 convolution_convert_fusion.4
  478.1 9.8 %collective-permute-start.34 = (bf16[32,1280]{1,0:T(8,128)(2,1)S(1)}, bf16[32,1280]{1,0:T(8,128)(2,1)S(1)}, u32[]{:S(2)}, u32[]{:S(2)}) collective-permute-start(bf16[32,1280]{1,0:T(8,128)(2,1)S(1)} %get-tuple-element.134), channel_id=1, source_target_pairs={{0,4},{4,8},{8,12},{12,0},{1,5},{5,9},{9,13},{13,1},{2,6},{6,10},{... | collective-permute-start | bytes 245768 | tf_op jit(solution)/shard_map/ppermute | solution.py:382
  496.8 12.1 %collective-permute-done.29 = bf16[4,96,960]{2,1,0:T(8,128)(2,1)S(1)} collective-permute-done((bf16[4,96,960]{2,1,0:T(8,128)(2,1)S(1)}, bf16[4,96,960]{2,1,0:T(8,128)(2,1)S(1)}, u32[]{:S(2)}, u32[]{:S(2)}) %collective-permute-start.29) | collective-permute-done | bytes 737312 | tf_op jit(solution)/shard_map/ppermute | solution.py:378
  511.8 6.1 collective-permute-done.50
  520.9 21.9 %collective-permute-done.57 = bf16[320,1600]{1,0:T(8,128)(2,1)S(1)} collective-permute-done((bf16[320,1600]{1,0:T(8,128)(2,1)S(1)}, bf16[320,1600]{1,0:T(8,128)(2,1)S(1)}, u32[]{:S(2)}, u32[]{:S(2)}) %collective-permute-start.57) | collective-permute-done | bytes 1024032 | tf_op jit(solution)/shard_map/ppermute | solution.py:417
  542.8 2.9 collective-permute-start.15
  556.5 8.4 collective-permute-done.17
  568.4 7.0 fusion.124
  575.4 9.8 %collective-permute-start.51 = (bf16[320,1600]{1,0:T(8,128)(2,1)}, bf16[320,1600]{1,0:T(8,128)(2,1)}, u32[]{:S(2)}, u32[]{:S(2)}) collective-permute-start(bf16[320,1600]{1,0:T(8,128)(2,1)} %fusion.49), channel_id=1, source_target_pairs={{12,8},{8,4},{4,0},{13,9},{9,5},{5,1},{14,10},{10,6},{6,2},{15,11}... | collective-permute-start | bytes 3072008 | tf_op jit(solution)/shard_map/ppermute | solution.py:417
  585.2 4.6 collective-permute-start.18
  589.8 8.8 %convolution_convert_fusion.1 = bf16[1280,1600]{0,1:T(8,128)(2,1)} fusion(bf16[512,1600]{0,1:T(8,128)(2,1)} %collective-permute-done.60, bf16[512,1600]{0,1:T(8,128)(2,1)} %get-tuple-element.84, bf16[512,1280]{1,0:T(8,128)(2,1)} %collective-permute-done.59, bf16[512,1280]{1,0:T(8,128)(2,1)S(1)} %copy-done.41), kind=kOutput, calls=%fused_computation.1 | convolution fusion | flops 4208148480 | bytes 9994240 | tf_op jit(solution)/shard_map/dot_general | solution.py:35
  598.5 6.8 copy.97
  605.4 3.2 dynamic-slice_bitcast_fusion.2
  608.6 6.2 collective-permute-done.37
  614.8 9.8 %collective-permute-start.58 = (bf16[320,1600]{1,0:T(8,128)(2,1)}, bf16[320,1600]{1,0:T(8,128)(2,1)S(1)}, u32[]{:S(2)}, u32[]{:S(2)}) collective-permute-start(bf16[320,1600]{1,0:T(8,128)(2,1)} %fusion.44), channel_id=1, source_target_pairs={{12,8},{8,4},{4,0},{13,9},{9,5},{5,1},{14,10},{10,6},{6,2},{15,11}... | collective-permute-start | bytes 3072008 | tf_op jit(solution)/shard_map/ppermute | solution.py:417
  631.2 3.2 collective-permute-start.19
  634.4 3.5 fusion.52
  637.9 7.1 collective-permute-done.58
  645.1 3.3 fusion.47
  648.5 11.8 %collective-permute-done.38 = bf16[320,640]{1,0:T(8,128)(2,1)S(1)} collective-permute-done((bf16[320,640]{1,0:T(8,128)(2,1)S(1)}, bf16[320,640]{1,0:T(8,128)(2,1)S(1)}, u32[]{:S(2)}, u32[]{:S(2)}) %collective-permute-start.38) | collective-permute-done | bytes 409632 | tf_op jit(solution)/shard_map/ppermute | solution.py:416
  664.5 8.2 collective-permute-done.21
  677.3 3.0 concatenate.100
  680.3 6.3 convolution_convert_fusion
  686.7 8.6 copy.93
  697.6 7.3 fusion.17
  705.1 28.5 %psum.7 = f32[8,768]{1,0:T(8,128)S(1)} all-reduce(f32[8,768]{1,0:T(8,128)S(1)} %pad_maximum_fusion.10), channel_id=1, replica_groups=mesh['dp'=2,'context'=4,'tensor'=4] {'dp','context'}, use_global_device_ids=true, to_apply=%region_13.14 | all-reduce | flops 6144 | bytes 49152 | tf_op jit(solution)/shard_map/psum | solution.py:675
  733.5 8.0 fusion.16
  754.6 8.4 collective-permute-done.23
  766.4 29.6 %collective-permute-start.26 = (bf16[80,1056]{1,0:T(8,128)(2,1)S(1)}, bf16[80,1056]{1,0:T(8,128)(2,1)S(1)}, u32[]{:S(2)}, u32[]{:S(2)}) collective-permute-start(bf16[80,1056]{1,0:T(8,128)(2,1)S(1)} %get-tuple-element.79), channel_id=1, source_target_pairs={{0,1},{1,2},{2,3},{3,0},{4,5},{5,6},{6,7},{7,4},{8,9},{9,10},{10,1... | collective-permute-start | bytes 506888 | tf_op jit(solution)/shard_map/ppermute | solution.py:382
  802.4 4.4 collective-permute-start.28
  806.9 4.9 collective-permute-start.63
  811.8 15.4 %collective-permute-done.65 = bf16[320,1600]{1,0:T(8,128)(2,1)S(1)} collective-permute-done((bf16[320,1600]{1,0:T(8,128)(2,1)S(1)}, bf16[320,1600]{1,0:T(8,128)(2,1)S(1)}, u32[]{:S(2)}, u32[]{:S(2)}) %collective-permute-start.65) | collective-permute-done | bytes 1024032 | tf_op jit(solution)/shard_map/ppermute | solution.py:417
  832.6 3.4 collective-permute-done.43
  838.4 19.2 %collective-permute-done.66 = bf16[320,1600]{1,0:T(8,128)(2,1)} collective-permute-done((bf16[320,1600]{1,0:T(8,128)(2,1)}, bf16[320,1600]{1,0:T(8,128)(2,1)}, u32[]{:S(2)}, u32[]{:S(2)}) %collective-permute-start.66) | collective-permute-done | bytes 1024032 | tf_op jit(solution)/shard_map/ppermute | solution.py:417
  857.6 3.5 fusion.42
  (389 shorter events, 183.8 us)
Async XLA Ops:
  11.2 17.2 %collective-permute-start.2 = (bf16[256,288]{0,1:T(8,128)(2,1)}, bf16[256,288]{0,1:T(8,128)(2,1)S(1)}, u32[]{:S(2)}, u32[]{:S(2)}) collective-permute-start(bf16[256,288]{0,1:T(8,128)(2,1)} %constant_dynamic-slice_fusion.10), channel_id=1, source_target_pairs={{0,12},{4,0},{8,4},{12,8},{1,13},{5,1},{9,5},{13,9},{2,14},{6,2},{... | collective-permute-start | bytes 442376 | tf_op jit(solution)/shard_map/ppermute | solution.py:382
  11.2 17.2 %collective-permute-start.1 = (bf16[256,288]{0,1:T(8,128)(2,1)}, bf16[256,288]{0,1:T(8,128)(2,1)}, u32[]{:S(2)}, u32[]{:S(2)}) collective-permute-start(bf16[256,288]{0,1:T(8,128)(2,1)} %constant_dynamic-slice_fusion.10), channel_id=1, source_target_pairs={{0,8},{4,12},{8,0},{12,4},{1,9},{5,13},{9,1},{13,5},{2,10},{6,14},... | collective-permute-start | bytes 442376 | tf_op jit(solution)/shard_map/ppermute | solution.py:382
  13.7 14.8 %collective-permute-start = (bf16[256,288]{0,1:T(8,128)(2,1)}, bf16[256,288]{0,1:T(8,128)(2,1)}, u32[]{:S(2)}, u32[]{:S(2)}) collective-permute-start(bf16[256,288]{0,1:T(8,128)(2,1)} %constant_dynamic-slice_fusion.10), channel_id=1, source_target_pairs={{0,4},{4,8},{8,12},{12,0},{1,5},{5,9},{9,13},{13,1},{2,6},{6,10},{... | collective-permute-start | bytes 442376 | tf_op jit(solution)/shard_map/ppermute | solution.py:382
  70.0 30.3 %collective-permute-start.5 = (bf16[256,2560]{1,0:T(8,128)(2,1)S(1)}, bf16[256,2560]{1,0:T(8,128)(2,1)S(1)}, u32[]{:S(2)}, u32[]{:S(2)}) collective-permute-start(bf16[256,2560]{1,0:T(8,128)(2,1)S(1)} %add_convert_fusion.6), channel_id=1, source_target_pairs={{0,2},{1,3},{2,0},{3,1},{4,6},{5,7},{6,4},{7,5},{8,10},{9,11},{10,... | collective-permute-start | bytes 3932168 | tf_op jit(solution)/shard_map/ppermute | solution.py:378
  100.6 9.8 %collective-permute-start.6 = (bf16[256,2560]{1,0:T(8,128)(2,1)S(1)}, bf16[256,2560]{1,0:T(8,128)(2,1)S(1)}, u32[]{:S(2)}, u32[]{:S(2)}) collective-permute-start(bf16[256,2560]{1,0:T(8,128)(2,1)S(1)} %add_convert_fusion.5), channel_id=1, source_target_pairs={{0,1},{1,0},{2,3},{3,2},{4,5},{5,4},{6,7},{7,6},{8,9},{9,8},{10,11... | collective-permute-start | bytes 3932168 | tf_op jit(solution)/shard_map/ppermute | solution.py:378
  142.6 22.5 %collective-permute-start.7 = (bf16[256,2560]{1,0:T(8,128)(2,1)}, bf16[256,2560]{1,0:T(8,128)(2,1)}, u32[]{:S(2)}, u32[]{:S(2)}) collective-permute-start(bf16[256,2560]{1,0:T(8,128)(2,1)} %constant_dynamic-slice_fusion.8), channel_id=1, source_target_pairs={{0,1},{1,0},{2,3},{3,2},{4,5},{5,4},{6,7},{7,6},{8,9},{9,8},{10,11... | collective-permute-start | bytes 3932168 | tf_op jit(solution)/shard_map/ppermute | solution.py:378
  158.9 10.2 %collective-permute-start.10 = (bf16[256,2560]{1,0:T(8,128)(2,1)}, bf16[256,2560]{1,0:T(8,128)(2,1)}, u32[]{:S(2)}, u32[]{:S(2)}) collective-permute-start(bf16[256,2560]{1,0:T(8,128)(2,1)} %constant_dynamic-slice_fusion.7), channel_id=1, source_target_pairs={{0,1},{1,0},{2,3},{3,2},{4,5},{5,4},{6,7},{7,6},{8,9},{9,8},{10,11... | collective-permute-start | bytes 3932168 | tf_op jit(solution)/shard_map/ppermute | solution.py:378
  160.5 100.3 %collective-permute-start.52 = (bf16[512,1600]{0,1:T(8,128)(2,1)}, bf16[512,1600]{0,1:T(8,128)(2,1)S(1)}, u32[]{:S(2)}, u32[]{:S(2)}) collective-permute-start(bf16[512,1600]{0,1:T(8,128)(2,1)} %copy-done.32), channel_id=1, source_target_pairs={{0,16},{16,0},{1,17},{17,1},{2,18},{18,2},{3,19},{19,3},{4,20},{20... | collective-permute-start | bytes 4915208 | tf_op jit(solution)/shard_map/ppermute | solution.py:378
  161.7 113.1 %collective-permute-start.45 = (bf16[512,1600]{0,1:T(8,128)(2,1)}, bf16[512,1600]{0,1:T(8,128)(2,1)}, u32[]{:S(2)}, u32[]{:S(2)}) collective-permute-start(bf16[512,1600]{0,1:T(8,128)(2,1)} %copy-done.71), channel_id=1, source_target_pairs={{0,16},{16,0},{1,17},{17,1},{2,18},{18,2},{3,19},{19,3},{4,20},{20... | collective-permute-start | bytes 4915208 | tf_op jit(solution)/shard_map/ppermute | solution.py:378
  163.9 96.9 %collective-permute-start.44 = (bf16[512,1280]{1,0:T(8,128)(2,1)S(1)}, bf16[512,1280]{1,0:T(8,128)(2,1)S(1)}, u32[]{:S(2)}, u32[]{:S(2)}) collective-permute-start(bf16[512,1280]{1,0:T(8,128)(2,1)S(1)} %get-tuple-element.102), channel_id=1, source_target_pairs={{0,16},{16,0},{1,17},{17,1},{2,18},{18,2},{3,19},{19,3},{4,20},{20... | collective-permute-start | bytes 3932168 | tf_op jit(solution)/shard_map/ppermute | solution.py:378
  167.8 175.5 %collective-permute-start.8 = (bf16[256,2560]{1,0:T(8,128)(2,1)}, bf16[256,2560]{1,0:T(8,128)(2,1)}, u32[]{:S(2)}, u32[]{:S(2)}) collective-permute-start(bf16[256,2560]{1,0:T(8,128)(2,1)} %add_convert_fusion.4), channel_id=1, source_target_pairs={{0,2},{1,3},{2,0},{3,1},{4,6},{5,7},{6,4},{7,5},{8,10},{9,11},{10,... | collective-permute-start | bytes 3932168 | tf_op jit(solution)/shard_map/ppermute | solution.py:378
  171.9 124.6 %collective-permute-start.11 = (bf16[256,2560]{1,0:T(8,128)(2,1)}, bf16[256,2560]{1,0:T(8,128)(2,1)}, u32[]{:S(2)}, u32[]{:S(2)}) collective-permute-start(bf16[256,2560]{1,0:T(8,128)(2,1)} %add_convert_fusion.2), channel_id=1, source_target_pairs={{0,2},{1,3},{2,0},{3,1},{4,6},{5,7},{6,4},{7,5},{8,10},{9,11},{10,... | collective-permute-start | bytes 3932168 | tf_op jit(solution)/shard_map/ppermute | solution.py:378
  292.6 25.7 %collective-permute-start.46 = (bf16[320,1600]{1,0:T(8,128)(2,1)S(1)}, bf16[320,1600]{1,0:T(8,128)(2,1)S(1)}, u32[]{:S(2)}, u32[]{:S(2)}) collective-permute-start(bf16[320,1600]{1,0:T(8,128)(2,1)S(1)} %get-tuple-element.95), channel_id=1, source_target_pairs={{0,4},{1,5},{2,6},{3,7},{16,20},{17,21},{18,22},{19,23}} | collective-permute-start | bytes 3072008 | tf_op jit(solution)/shard_map/ppermute | solution.py:416
  294.0 54.3 %collective-permute-start.49 = (bf16[320,1600]{1,0:T(8,128)(2,1)S(1)}, bf16[320,1600]{1,0:T(8,128)(2,1)S(1)}, u32[]{:S(2)}, u32[]{:S(2)}) collective-permute-start(bf16[320,1600]{1,0:T(8,128)(2,1)S(1)} %get-tuple-element.96), channel_id=1, source_target_pairs={{12,8},{13,9},{14,10},{15,11},{28,24},{29,25},{30,26},{31,27}} | collective-permute-start | bytes 3072008 | tf_op jit(solution)/shard_map/ppermute | solution.py:417
  295.0 46.2 %collective-permute-start.53 = (bf16[320,1600]{1,0:T(8,128)(2,1)S(1)}, bf16[320,1600]{1,0:T(8,128)(2,1)S(1)}, u32[]{:S(2)}, u32[]{:S(2)}) collective-permute-start(bf16[320,1600]{1,0:T(8,128)(2,1)S(1)} %get-tuple-element.91), channel_id=1, source_target_pairs={{0,4},{1,5},{2,6},{3,7},{16,20},{17,21},{18,22},{19,23}} | collective-permute-start | bytes 3072008 | tf_op jit(solution)/shard_map/ppermute | solution.py:416
  296.5 77.0 %collective-permute-start.56 = (bf16[320,1600]{1,0:T(8,128)(2,1)S(1)}, bf16[320,1600]{1,0:T(8,128)(2,1)S(1)}, u32[]{:S(2)}, u32[]{:S(2)}) collective-permute-start(bf16[320,1600]{1,0:T(8,128)(2,1)S(1)} %get-tuple-element.92), channel_id=1, source_target_pairs={{12,8},{13,9},{14,10},{15,11},{28,24},{29,25},{30,26},{31,27}} | collective-permute-start | bytes 3072008 | tf_op jit(solution)/shard_map/ppermute | solution.py:417
  318.3 72.1 %collective-permute-start.12 = (bf16[256,2560]{1,0:T(8,128)(2,1)S(1)}, bf16[256,2560]{1,0:T(8,128)(2,1)S(1)}, u32[]{:S(2)}, u32[]{:S(2)}) collective-permute-start(bf16[256,2560]{1,0:T(8,128)(2,1)S(1)} %add_convert_fusion.1), channel_id=1, source_target_pairs={{0,1},{1,0},{2,3},{3,2},{4,5},{5,4},{6,7},{7,6},{8,9},{9,8},{10,11... | collective-permute-start | bytes 3932168 | tf_op jit(solution)/shard_map/ppermute | solution.py:378
  341.1 24.7 %collective-permute-start.47 = (bf16[320,1600]{1,0:T(8,128)(2,1)S(1)}, bf16[320,1600]{1,0:T(8,128)(2,1)S(1)}, u32[]{:S(2)}, u32[]{:S(2)}) collective-permute-start(bf16[320,1600]{1,0:T(8,128)(2,1)S(1)} %fusion.50), channel_id=1, source_target_pairs={{0,4},{4,8},{1,5},{5,9},{2,6},{6,10},{3,7},{7,11},{16,20},{20,24},... | collective-permute-start | bytes 3072008 | tf_op jit(solution)/shard_map/ppermute | solution.py:416
  343.3 45.3 %collective-permute-start.54 = (bf16[320,1600]{1,0:T(8,128)(2,1)S(1)}, bf16[320,1600]{1,0:T(8,128)(2,1)S(1)}, u32[]{:S(2)}, u32[]{:S(2)}) collective-permute-start(bf16[320,1600]{1,0:T(8,128)(2,1)S(1)} %fusion.45), channel_id=1, source_target_pairs={{0,4},{4,8},{1,5},{5,9},{2,6},{6,10},{3,7},{7,11},{16,20},{20,24},... | collective-permute-start | bytes 3072008 | tf_op jit(solution)/shard_map/ppermute | solution.py:416
  348.3 227.0 %collective-permute-start.60 = (bf16[512,1600]{0,1:T(8,128)(2,1)}, bf16[512,1600]{0,1:T(8,128)(2,1)}, u32[]{:S(2)}, u32[]{:S(2)}) collective-permute-start(bf16[512,1600]{0,1:T(8,128)(2,1)} %get-tuple-element.84), channel_id=1, source_target_pairs={{0,16},{16,0},{1,17},{17,1},{2,18},{18,2},{3,19},{19,3},{4,20},{20... | collective-permute-start | bytes 4915208 | tf_op jit(solution)/shard_map/ppermute | solution.py:378
  365.9 103.7 %collective-permute-start.9 = (bf16[256,2560]{1,0:T(8,128)(2,1)}, bf16[256,2560]{1,0:T(8,128)(2,1)}, u32[]{:S(2)}, u32[]{:S(2)}) collective-permute-start(bf16[256,2560]{1,0:T(8,128)(2,1)} %add_convert_fusion.3), channel_id=1, source_target_pairs={{0,1},{1,0},{2,3},{3,2},{4,5},{5,4},{6,7},{7,6},{8,9},{9,8},{10,11... | collective-permute-start | bytes 3932168 | tf_op jit(solution)/shard_map/ppermute | solution.py:378
  449.4 27.4 %collective-permute-start.33 = (bf16[4,32,1280]{2,1,0:T(8,128)(2,1)}, bf16[4,32,1280]{2,1,0:T(8,128)(2,1)}, u32[]{:S(2)}, u32[]{:S(2)}) collective-permute-start(bf16[4,32,1280]{2,1,0:T(8,128)(2,1)} %dynamic-slice_bitcast_fusion.11), channel_id=1, source_target_pairs={{0,16},{16,0},{1,17},{17,1},{2,18},{18,2},{3,19},{19,3},{4,20},{20... | collective-permute-start | bytes 983048 | tf_op jit(solution)/shard_map/ppermute | solution.py:378
  452.6 41.8 %collective-permute-start.16 = (bf16[144,2048]{1,0:T(8,128)(2,1)}, bf16[144,2048]{1,0:T(8,128)(2,1)}, u32[]{:S(2)}, u32[]{:S(2)}) collective-permute-start(bf16[144,2048]{1,0:T(8,128)(2,1)} %constant_dynamic-slice_fusion.5), channel_id=1, source_target_pairs={{0,1},{1,0},{2,3},{3,2},{4,5},{5,4},{6,7},{7,6},{8,9},{9,8},{10,11... | collective-permute-start | bytes 1769480 | tf_op jit(solution)/shard_map/ppermute | solution.py:378
  459.9 28.1 %collective-permute-start.13 = (bf16[256,768]{1,0:T(8,128)(2,1)}, bf16[256,768]{1,0:T(8,128)(2,1)}, u32[]{:S(2)}, u32[]{:S(2)}) collective-permute-start(bf16[256,768]{1,0:T(8,128)(2,1)} %constant_dynamic-slice_fusion.6), channel_id=1, source_target_pairs={{0,1},{1,0},{2,3},{3,2},{4,5},{5,4},{6,7},{7,6},{8,9},{9,8},{10,11... | collective-permute-start | bytes 1179656 | tf_op jit(solution)/shard_map/ppermute | solution.py:378
  478.1 12.2 %collective-permute-start.34 = (bf16[32,1280]{1,0:T(8,128)(2,1)S(1)}, bf16[32,1280]{1,0:T(8,128)(2,1)S(1)}, u32[]{:S(2)}, u32[]{:S(2)}) collective-permute-start(bf16[32,1280]{1,0:T(8,128)(2,1)S(1)} %get-tuple-element.134), channel_id=1, source_target_pairs={{0,4},{4,8},{8,12},{12,0},{1,5},{5,9},{9,13},{13,1},{2,6},{6,10},{... | collective-permute-start | bytes 245768 | tf_op jit(solution)/shard_map/ppermute | solution.py:382
  488.0 5.4 collective-permute-start.35
  490.4 27.5 %collective-permute-start.50 = (bf16[320,1600]{1,0:T(8,128)(2,1)S(1)}, bf16[320,1600]{1,0:T(8,128)(2,1)S(1)}, u32[]{:S(2)}, u32[]{:S(2)}) collective-permute-start(bf16[320,1600]{1,0:T(8,128)(2,1)S(1)} %copy-done.46), channel_id=1, source_target_pairs={{12,8},{8,4},{13,9},{9,5},{14,10},{10,6},{15,11},{11,7},{28,24},{2... | collective-permute-start | bytes 3072008 | tf_op jit(solution)/shard_map/ppermute | solution.py:417
  491.7 51.1 %collective-permute-start.57 = (bf16[320,1600]{1,0:T(8,128)(2,1)S(1)}, bf16[320,1600]{1,0:T(8,128)(2,1)S(1)}, u32[]{:S(2)}, u32[]{:S(2)}) collective-permute-start(bf16[320,1600]{1,0:T(8,128)(2,1)S(1)} %copy-done.45), channel_id=1, source_target_pairs={{12,8},{8,4},{13,9},{9,5},{14,10},{10,6},{15,11},{11,7},{28,24},{2... | collective-permute-start | bytes 3072008 | tf_op jit(solution)/shard_map/ppermute | solution.py:417
  493.4 15.5 %collective-permute-start.29 = (bf16[4,96,960]{2,1,0:T(8,128)(2,1)S(1)}, bf16[4,96,960]{2,1,0:T(8,128)(2,1)S(1)}, u32[]{:S(2)}, u32[]{:S(2)}) collective-permute-start(bf16[4,96,960]{2,1,0:T(8,128)(2,1)S(1)} %dynamic-slice_bitcast_fusion.7), channel_id=1, source_target_pairs={{0,16},{16,0},{1,17},{17,1},{2,18},{18,2},{3,19},{19,3},{4,20},{20... | collective-permute-start | bytes 2211848 | tf_op jit(solution)/shard_map/ppermute | solution.py:378
  494.3 26.0 %collective-permute-start.14 = (bf16[256,768]{1,0:T(8,128)(2,1)S(1)}, bf16[256,768]{1,0:T(8,128)(2,1)S(1)}, u32[]{:S(2)}, u32[]{:S(2)}) collective-permute-start(bf16[256,768]{1,0:T(8,128)(2,1)S(1)} %add_convert_fusion.10), channel_id=1, source_target_pairs={{0,2},{1,3},{2,0},{3,1},{4,6},{5,7},{6,4},{7,5},{8,10},{9,11},{10,... | collective-permute-start | bytes 1179656 | tf_op jit(solution)/shard_map/ppermute | solution.py:378
  509.2 39.0 %collective-permute-start.30 = (bf16[96,960]{1,0:T(8,128)(2,1)S(1)}, bf16[96,960]{1,0:T(8,128)(2,1)S(1)}, u32[]{:S(2)}, u32[]{:S(2)}) collective-permute-start(bf16[96,960]{1,0:T(8,128)(2,1)S(1)} %get-tuple-element.122), channel_id=1, source_target_pairs={{0,4},{4,8},{8,12},{12,0},{1,5},{5,9},{9,13},{13,1},{2,6},{6,10},{... | collective-permute-start | bytes 552968 | tf_op jit(solution)/shard_map/ppermute | solution.py:382
  517.9 33.4 %collective-permute-start.32 = (bf16[96,960]{1,0:T(8,128)(2,1)S(1)}, bf16[96,960]{1,0:T(8,128)(2,1)S(1)}, u32[]{:S(2)}, u32[]{:S(2)}) collective-permute-start(bf16[96,960]{1,0:T(8,128)(2,1)S(1)} %get-tuple-element.123), channel_id=1, source_target_pairs={{0,12},{4,0},{8,4},{12,8},{1,13},{5,1},{9,5},{13,9},{2,14},{6,2},{... | collective-permute-start | bytes 552968 | tf_op jit(solution)/shard_map/ppermute | solution.py:382
  520.3 33.0 %collective-permute-start.31 = (bf16[96,960]{1,0:T(8,128)(2,1)S(1)}, bf16[96,960]{1,0:T(8,128)(2,1)S(1)}, u32[]{:S(2)}, u32[]{:S(2)}) collective-permute-start(bf16[96,960]{1,0:T(8,128)(2,1)S(1)} %get-tuple-element.124), channel_id=1, source_target_pairs={{0,8},{4,12},{8,0},{12,4},{1,9},{5,13},{9,1},{13,5},{2,10},{6,14},... | collective-permute-start | bytes 552968 | tf_op jit(solution)/shard_map/ppermute | solution.py:382
  542.8 11.7 %collective-permute-start.15 = (bf16[256,768]{1,0:T(8,128)(2,1)S(1)}, bf16[256,768]{1,0:T(8,128)(2,1)S(1)}, u32[]{:S(2)}, u32[]{:S(2)}) collective-permute-start(bf16[256,768]{1,0:T(8,128)(2,1)S(1)} %add_convert_fusion.9), channel_id=1, source_target_pairs={{0,1},{1,0},{2,3},{3,2},{4,5},{5,4},{6,7},{7,6},{8,9},{9,8},{10,11... | collective-permute-start | bytes 1179656 | tf_op jit(solution)/shard_map/ppermute | solution.py:378
  548.2 81.7 %collective-permute-start.48 = (bf16[320,1600]{1,0:T(8,128)(2,1)}, bf16[320,1600]{1,0:T(8,128)(2,1)}, u32[]{:S(2)}, u32[]{:S(2)}) collective-permute-start(bf16[320,1600]{1,0:T(8,128)(2,1)} %get-tuple-element.93), channel_id=1, source_target_pairs={{0,4},{4,8},{8,12},{1,5},{5,9},{9,13},{2,6},{6,10},{10,14},{3,7},{... | collective-permute-start | bytes 3072008 | tf_op jit(solution)/shard_map/ppermute | solution.py:416
  551.2 86.7 %collective-permute-start.55 = (bf16[320,1600]{1,0:T(8,128)(2,1)}, bf16[320,1600]{1,0:T(8,128)(2,1)}, u32[]{:S(2)}, u32[]{:S(2)}) collective-permute-start(bf16[320,1600]{1,0:T(8,128)(2,1)} %get-tuple-element.89), channel_id=1, source_target_pairs={{0,4},{4,8},{8,12},{1,5},{5,9},{9,13},{2,6},{6,10},{10,14},{3,7},{... | collective-permute-start | bytes 3072008 | tf_op jit(solution)/shard_map/ppermute | solution.py:416
  553.4 31.8 %collective-permute-start.59 = (bf16[512,1280]{1,0:T(8,128)(2,1)}, bf16[512,1280]{1,0:T(8,128)(2,1)}, u32[]{:S(2)}, u32[]{:S(2)}) collective-permute-start(bf16[512,1280]{1,0:T(8,128)(2,1)} %get-tuple-element.98), channel_id=1, source_target_pairs={{0,16},{16,0},{1,17},{17,1},{2,18},{18,2},{3,19},{19,3},{4,20},{20... | collective-permute-start | bytes 3932168 | tf_op jit(solution)/shard_map/ppermute | solution.py:378
  554.5 10.3 %collective-permute-start.17 = (bf16[144,2048]{1,0:T(8,128)(2,1)S(1)}, bf16[144,2048]{1,0:T(8,128)(2,1)S(1)}, u32[]{:S(2)}, u32[]{:S(2)}) collective-permute-start(bf16[144,2048]{1,0:T(8,128)(2,1)S(1)} %add_convert_fusion.8), channel_id=1, source_target_pairs={{0,2},{1,3},{2,0},{3,1},{4,6},{5,7},{6,4},{7,5},{8,10},{9,11},{10,... | collective-permute-start | bytes 1769480 | tf_op jit(solution)/shard_map/ppermute | solution.py:378
  564.8 49.9 %collective-permute-start.37 = (bf16[4,320,640]{2,1,0:T(8,128)(2,1)}, bf16[4,320,640]{2,1,0:T(8,128)(2,1)}, u32[]{:S(2)}, u32[]{:S(2)}) collective-permute-start(bf16[4,320,640]{2,1,0:T(8,128)(2,1)} %dynamic-slice_bitcast_fusion), channel_id=1, source_target_pairs={{0,16},{16,0},{1,17},{17,1},{2,18},{18,2},{3,19},{19,3},{4,20},{20... | collective-permute-start | bytes 4915208 | tf_op jit(solution)/shard_map/ppermute | solution.py:378
  575.4 55.8 %collective-permute-start.51 = (bf16[320,1600]{1,0:T(8,128)(2,1)}, bf16[320,1600]{1,0:T(8,128)(2,1)}, u32[]{:S(2)}, u32[]{:S(2)}) collective-permute-start(bf16[320,1600]{1,0:T(8,128)(2,1)} %fusion.49), channel_id=1, source_target_pairs={{12,8},{8,4},{4,0},{13,9},{9,5},{5,1},{14,10},{10,6},{6,2},{15,11}... | collective-permute-start | bytes 3072008 | tf_op jit(solution)/shard_map/ppermute | solution.py:417
  585.2 42.2 %collective-permute-start.18 = (bf16[144,2048]{1,0:T(8,128)(2,1)S(1)}, bf16[144,2048]{1,0:T(8,128)(2,1)}, u32[]{:S(2)}, u32[]{:S(2)}) collective-permute-start(bf16[144,2048]{1,0:T(8,128)(2,1)S(1)} %copy-done.39), channel_id=1, source_target_pairs={{0,1},{1,0},{2,3},{3,2},{4,5},{5,4},{6,7},{7,6},{8,9},{9,8},{10,11... | collective-permute-start | bytes 1769480 | tf_op jit(solution)/shard_map/ppermute | solution.py:378
  614.8 30.2 %collective-permute-start.58 = (bf16[320,1600]{1,0:T(8,128)(2,1)}, bf16[320,1600]{1,0:T(8,128)(2,1)S(1)}, u32[]{:S(2)}, u32[]{:S(2)}) collective-permute-start(bf16[320,1600]{1,0:T(8,128)(2,1)} %fusion.44), channel_id=1, source_target_pairs={{12,8},{8,4},{4,0},{13,9},{9,5},{5,1},{14,10},{10,6},{6,2},{15,11}... | collective-permute-start | bytes 3072008 | tf_op jit(solution)/shard_map/ppermute | solution.py:417
  627.4 116.0 %collective-permute-start.61 = (bf16[320,1600]{1,0:T(8,128)(2,1)}, bf16[320,1600]{1,0:T(8,128)(2,1)}, u32[]{:S(2)}, u32[]{:S(2)}) collective-permute-start(bf16[320,1600]{1,0:T(8,128)(2,1)} %get-tuple-element.87), channel_id=1, source_target_pairs={{0,4},{1,5},{2,6},{3,7},{16,20},{17,21},{18,22},{19,23}} | collective-permute-start | bytes 3072008 | tf_op jit(solution)/shard_map/ppermute | solution.py:416
  629.9 30.4 %collective-permute-start.38 = (bf16[320,640]{1,0:T(8,128)(2,1)S(1)}, bf16[320,640]{1,0:T(8,128)(2,1)S(1)}, u32[]{:S(2)}, u32[]{:S(2)}) collective-permute-start(bf16[320,640]{1,0:T(8,128)(2,1)S(1)} %get-tuple-element.113), channel_id=1, source_target_pairs={{0,4},{1,5},{2,6},{3,7},{16,20},{17,21},{18,22},{19,23}} | collective-permute-start | bytes 1228808 | tf_op jit(solution)/shard_map/ppermute | solution.py:416
  631.2 31.7 %collective-permute-start.19 = (bf16[288,512]{1,0:T(8,128)(2,1)S(1)}, bf16[288,512]{1,0:T(8,128)(2,1)S(1)}, u32[]{:S(2)}, u32[]{:S(2)}) collective-permute-start(bf16[288,512]{1,0:T(8,128)(2,1)S(1)} %get-tuple-element.115), channel_id=1, source_target_pairs={{0,12},{4,0},{8,4},{12,8},{1,13},{5,1},{9,5},{13,9},{2,14},{6,2},{... | collective-permute-start | bytes 884744 | tf_op jit(solution)/shard_map/ppermute | solution.py:382
  637.9 34.7 %collective-permute-start.21 = (bf16[288,512]{1,0:T(8,128)(2,1)S(1)}, bf16[288,512]{1,0:T(8,128)(2,1)S(1)}, u32[]{:S(2)}, u32[]{:S(2)}) collective-permute-start(bf16[288,512]{1,0:T(8,128)(2,1)S(1)} %get-tuple-element.116), channel_id=1, source_target_pairs={{0,4},{4,8},{8,12},{12,0},{1,5},{5,9},{9,13},{13,1},{2,6},{6,10},{... | collective-permute-start | bytes 884744 | tf_op jit(solution)/shard_map/ppermute | solution.py:382
  645.0 29.8 %collective-permute-start.20 = (bf16[288,512]{1,0:T(8,128)(2,1)S(1)}, bf16[288,512]{1,0:T(8,128)(2,1)S(1)}, u32[]{:S(2)}, u32[]{:S(2)}) collective-permute-start(bf16[288,512]{1,0:T(8,128)(2,1)S(1)} %get-tuple-element.117), channel_id=1, source_target_pairs={{0,8},{4,12},{8,0},{12,4},{1,9},{5,13},{9,1},{13,5},{2,10},{6,14},... | collective-permute-start | bytes 884744 | tf_op jit(solution)/shard_map/ppermute | solution.py:382
  660.3 135.7 %collective-permute-start.64 = (bf16[320,1600]{1,0:T(8,128)(2,1)}, bf16[320,1600]{1,0:T(8,128)(2,1)}, u32[]{:S(2)}, u32[]{:S(2)}) collective-permute-start(bf16[320,1600]{1,0:T(8,128)(2,1)} %get-tuple-element.88), channel_id=1, source_target_pairs={{12,8},{13,9},{14,10},{15,11},{28,24},{29,25},{30,26},{31,27}} | collective-permute-start | bytes 3072008 | tf_op jit(solution)/shard_map/ppermute | solution.py:417
  662.9 85.7 %collective-permute-start.41 = (bf16[320,640]{1,0:T(8,128)(2,1)}, bf16[320,640]{1,0:T(8,128)(2,1)}, u32[]{:S(2)}, u32[]{:S(2)}) collective-permute-start(bf16[320,640]{1,0:T(8,128)(2,1)} %get-tuple-element.114), channel_id=1, source_target_pairs={{12,8},{13,9},{14,10},{15,11},{28,24},{29,25},{30,26},{31,27}} | collective-permute-start | bytes 1228808 | tf_op jit(solution)/shard_map/ppermute | solution.py:417
  672.7 77.8 %collective-permute-start.39 = (bf16[320,640]{1,0:T(8,128)(2,1)}, bf16[320,640]{1,0:T(8,128)(2,1)}, u32[]{:S(2)}, u32[]{:S(2)}) collective-permute-start(bf16[320,640]{1,0:T(8,128)(2,1)} %fusion.64), channel_id=1, source_target_pairs={{0,4},{4,8},{1,5},{5,9},{2,6},{6,10},{3,7},{7,11},{16,20},{20,24},... | collective-permute-start | bytes 1228808 | tf_op jit(solution)/shard_map/ppermute | solution.py:416
  697.4 49.6 %collective-permute-start.22 = (bf16[4,80,1056]{2,1,0:T(8,128)(2,1)}, bf16[4,80,1056]{2,1,0:T(8,128)(2,1)}, u32[]{:S(2)}, u32[]{:S(2)}) collective-permute-start(bf16[4,80,1056]{2,1,0:T(8,128)(2,1)} %dynamic-slice_bitcast_fusion.8), channel_id=1, source_target_pairs={{0,16},{16,0},{1,17},{17,1},{2,18},{18,2},{3,19},{19,3},{4,20},{20... | collective-permute-start | bytes 2027528 | tf_op jit(solution)/shard_map/ppermute | solution.py:378
  744.9 51.1 %collective-permute-start.62 = (bf16[320,1600]{1,0:T(8,128)(2,1)S(1)}, bf16[320,1600]{1,0:T(8,128)(2,1)S(1)}, u32[]{:S(2)}, u32[]{:S(2)}) collective-permute-start(bf16[320,1600]{1,0:T(8,128)(2,1)S(1)} %fusion.39), channel_id=1, source_target_pairs={{0,4},{4,8},{1,5},{5,9},{2,6},{6,10},{3,7},{7,11},{16,20},{20,24},... | collective-permute-start | bytes 3072008 | tf_op jit(solution)/shard_map/ppermute | solution.py:416
  748.6 14.4 %collective-permute-start.23 = (bf16[80,1056]{1,0:T(8,128)(2,1)S(1)}, bf16[80,1056]{1,0:T(8,128)(2,1)S(1)}, u32[]{:S(2)}, u32[]{:S(2)}) collective-permute-start(bf16[80,1056]{1,0:T(8,128)(2,1)S(1)} %get-tuple-element.127), channel_id=1, source_target_pairs={{0,4},{4,8},{8,12},{12,0},{1,5},{5,9},{9,13},{13,1},{2,6},{6,10},{... | collective-permute-start | bytes 506888 | tf_op jit(solution)/shard_map/ppermute | solution.py:382
  748.7 16.2 %collective-permute-start.25 = (bf16[80,1056]{1,0:T(8,128)(2,1)S(1)}, bf16[80,1056]{1,0:T(8,128)(2,1)S(1)}, u32[]{:S(2)}, u32[]{:S(2)}) collective-permute-start(bf16[80,1056]{1,0:T(8,128)(2,1)S(1)} %get-tuple-element.128), channel_id=1, source_target_pairs={{0,12},{4,0},{8,4},{12,8},{1,13},{5,1},{9,5},{13,9},{2,14},{6,2},{... | collective-permute-start | bytes 506888 | tf_op jit(solution)/shard_map/ppermute | solution.py:382
  750.5 15.8 %collective-permute-start.24 = (bf16[80,1056]{1,0:T(8,128)(2,1)S(1)}, bf16[80,1056]{1,0:T(8,128)(2,1)S(1)}, u32[]{:S(2)}, u32[]{:S(2)}) collective-permute-start(bf16[80,1056]{1,0:T(8,128)(2,1)S(1)} %get-tuple-element.129), channel_id=1, source_target_pairs={{0,8},{4,12},{8,0},{12,4},{1,9},{5,13},{9,1},{13,5},{2,10},{6,14},... | collective-permute-start | bytes 506888 | tf_op jit(solution)/shard_map/ppermute | solution.py:382
  763.0 69.6 %collective-permute-start.40 = (bf16[320,640]{1,0:T(8,128)(2,1)}, bf16[320,640]{1,0:T(8,128)(2,1)}, u32[]{:S(2)}, u32[]{:S(2)}) collective-permute-start(bf16[320,640]{1,0:T(8,128)(2,1)} %get-tuple-element.111), channel_id=1, source_target_pairs={{0,4},{4,8},{8,12},{1,5},{5,9},{9,13},{2,6},{6,10},{10,14},{3,7},{... | collective-permute-start | bytes 1228808 | tf_op jit(solution)/shard_map/ppermute | solution.py:416
  764.9 35.2 %collective-permute-start.42 = (bf16[320,640]{1,0:T(8,128)(2,1)S(1)}, bf16[320,640]{1,0:T(8,128)(2,1)S(1)}, u32[]{:S(2)}, u32[]{:S(2)}) collective-permute-start(bf16[320,640]{1,0:T(8,128)(2,1)S(1)} %get-tuple-element.112), channel_id=1, source_target_pairs={{12,8},{8,4},{13,9},{9,5},{14,10},{10,6},{15,11},{11,7},{28,24},{2... | collective-permute-start | bytes 1228808 | tf_op jit(solution)/shard_map/ppermute | solution.py:417
  766.4 36.0 %collective-permute-start.26 = (bf16[80,1056]{1,0:T(8,128)(2,1)S(1)}, bf16[80,1056]{1,0:T(8,128)(2,1)S(1)}, u32[]{:S(2)}, u32[]{:S(2)}) collective-permute-start(bf16[80,1056]{1,0:T(8,128)(2,1)S(1)} %get-tuple-element.79), channel_id=1, source_target_pairs={{0,1},{1,2},{2,3},{3,0},{4,5},{5,6},{6,7},{7,4},{8,9},{9,10},{10,1... | collective-permute-start | bytes 506888 | tf_op jit(solution)/shard_map/ppermute | solution.py:382
  798.8 28.4 %collective-permute-start.65 = (bf16[320,1600]{1,0:T(8,128)(2,1)S(1)}, bf16[320,1600]{1,0:T(8,128)(2,1)S(1)}, u32[]{:S(2)}, u32[]{:S(2)}) collective-permute-start(bf16[320,1600]{1,0:T(8,128)(2,1)S(1)} %get-tuple-element.86), channel_id=1, source_target_pairs={{12,8},{8,4},{13,9},{9,5},{14,10},{10,6},{15,11},{11,7},{28,24},{2... | collective-permute-start | bytes 3072008 | tf_op jit(solution)/shard_map/ppermute | solution.py:417
  800.2 35.8 %collective-permute-start.43 = (bf16[320,640]{1,0:T(8,128)(2,1)S(1)}, bf16[320,640]{1,0:T(8,128)(2,1)}, u32[]{:S(2)}, u32[]{:S(2)}) collective-permute-start(bf16[320,640]{1,0:T(8,128)(2,1)S(1)} %fusion.63), channel_id=1, source_target_pairs={{12,8},{8,4},{4,0},{13,9},{9,5},{5,1},{14,10},{10,6},{6,2},{15,11}... | collective-permute-start | bytes 1228808 | tf_op jit(solution)/shard_map/ppermute | solution.py:417
  802.1 4.7 collective-permute-start.27
  802.4 28.0 %collective-permute-start.28 = (bf16[80,1056]{1,0:T(8,128)(2,1)S(1)}, bf16[80,1056]{1,0:T(8,128)(2,1)S(1)}, u32[]{:S(2)}, u32[]{:S(2)}) collective-permute-start(bf16[80,1056]{1,0:T(8,128)(2,1)S(1)} %get-tuple-element.79), channel_id=1, source_target_pairs={{0,3},{1,0},{2,1},{3,2},{4,7},{5,4},{6,5},{7,6},{8,11},{9,8},{10,9... | collective-permute-start | bytes 506888 | tf_op jit(solution)/shard_map/ppermute | solution.py:382
  806.9 31.5 %collective-permute-start.63 = (bf16[320,1600]{1,0:T(8,128)(2,1)}, bf16[320,1600]{1,0:T(8,128)(2,1)}, u32[]{:S(2)}, u32[]{:S(2)}) collective-permute-start(bf16[320,1600]{1,0:T(8,128)(2,1)} %get-tuple-element.85), channel_id=1, source_target_pairs={{0,4},{4,8},{8,12},{1,5},{5,9},{9,13},{2,6},{6,10},{10,14},{3,7},{... | collective-permute-start | bytes 3072008 | tf_op jit(solution)/shard_map/ppermute | solution.py:416
  828.4 29.1 %collective-permute-start.66 = (bf16[320,1600]{1,0:T(8,128)(2,1)}, bf16[320,1600]{1,0:T(8,128)(2,1)}, u32[]{:S(2)}, u32[]{:S(2)}) collective-permute-start(bf16[320,1600]{1,0:T(8,128)(2,1)} %fusion.38), channel_id=1, source_target_pairs={{12,8},{8,4},{4,0},{13,9},{9,5},{5,1},{14,10},{10,6},{6,2},{15,11}... | collective-permute-start | bytes 3072008 | tf_op jit(solution)/shard_map/ppermute | solution.py:417
  (84 other events, 1051.1 us)

commit v2 on v1

--- a/solution.py
+++ b/solution.py
@@ -14,6 +14,7 @@
 KV_RANK = 256
 HALF = 256
 GROUP = 5
+CHUNK = 256
 
 EPS = 1e-05
 RESIDUAL = 1.4 / math.sqrt(62.0)
@@ -374,6 +375,341 @@
     )
 
 
+MESH = pl.DeviceIdType.MESH
+
+
+def cuts(size, step=512):
+    count = max(1, size // step)
+    edges = [i * step for i in range(count)] + [size]
+    return list(zip(edges[:-1], edges[1:]))
+
+
+def feed_forward_kernel(
+    tensors,
+    joined_t,
+    tokens,
+    cotangent,
+    gain,
+    attn_out_h,
+    down_h,
+    gate_h,
+    up_h,
+    branch_o,
+    two_o,
+    hidden_o,
+    dgate_o,
+    dup_o,
+    feed_o,
+    dmiddle_o,
+    dmix_t,
+    gain_o,
+    attn_out,
+    down,
+    gate_w,
+    up_w,
+    part,
+    final,
+    near,
+    across,
+    dhid,
+    two,
+    trio,
+    feed,
+    dmiddle,
+    load_sem,
+    save_sem,
+    send_sem,
+    recv_sem,
+):
+    rows, width = tokens.shape
+    half = width // 2
+    t = lax.axis_index("tensor")
+    bit = lax.rem(t, 2)
+    pair = t + 1 - 2 * bit
+    others = [pair]
+    step = 2
+    while step < tensors:
+        others.append(t + step - 2 * step * lax.rem(t // step, 2))
+        step *= 2
+
+    loads = [
+        pltpu.make_async_copy(src, dst, load_sem.at[i])
+        for i, (src, dst) in enumerate(
+            [(attn_out_h, attn_out), (down_h, down), (gate_h, gate_w), (up_h, up_w)]
+        )
+    ]
+    for load in loads:
+        load.start()
+
+    barrier = pltpu.get_barrier_semaphore()
+    for other in others:
+        pl.semaphore_signal(barrier, inc=1, device_id={"tensor": other}, device_id_type=MESH)
+    pl.semaphore_wait(barrier, len(others))
+
+    def send(src, dst, job, kind, c, device):
+        return pltpu.make_async_remote_copy(
+            src_ref=src,
+            dst_ref=dst,
+            send_sem=send_sem.at[job, kind, c],
+            recv_sem=recv_sem.at[job, kind, c],
+            device_id={"tensor": device},
+            device_id_type=MESH,
+        )
+
+    def span(c):
+        return pl.ds(c * CHUNK, CHUNK)
+
+    last = len(others)
+
+    def hop(job, c, kind):
+        if kind == 0:
+            return send(
+                part.at[1 - bit, span(c)], near.at[job, span(c)], job, 0, c, pair
+            )
+        if kind == last:
+            here = final.at[job, bit, span(c)]
+            return send(here, here, job, last, c, pair)
+        src = near if kind == 1 else across.at[kind - 2]
+        return send(
+            src.at[job, span(c)], across.at[kind - 1, job, span(c)], job, kind, c, others[kind]
+        )
+
+    def reduce_pair(job, c):
+        hop(job, c, 0).wait_recv()
+
+        @pl.loop(0, CHUNK // 32)
+        def _(i):
+            r = pl.ds(pl.multiple_of(c * CHUNK + i * 32, 32), 32)
+            near[job, r, :] = (
+                near[job, r, :].astype(F32) + part[bit, r, :].astype(F32)
+            ).astype(BF16)
+
+        hop(job, c, 1).start()
+
+    def reduce_across(job, c):
+        for kind in range(1, last):
+            hop(job, c, kind).wait_recv()
+            src = near if kind == 1 else across.at[kind - 2]
+            ending = kind == last - 1
+
+            @pl.loop(0, CHUNK // 32)
+            def _(i):
+                r = pl.ds(pl.multiple_of(c * CHUNK + i * 32, 32), 32)
+                value = (
+                    src[job, r, :].astype(F32) + across[kind - 1, job, r, :].astype(F32)
+                ).astype(BF16)
+                if ending:
+                    final[job, bit, r, :] = value
+                else:
+                    across[kind - 1, job, r, :] = value
+
+            hop(job, c, kind + 1).start()
+        hop(job, c, last).wait_recv()
+
+    def middle_rows(r):
+        parts = []
+        for h in range(2):
+            cols = slice(h * half, (h + 1) * half)
+            parts.append(
+                tokens[r, cols].astype(F32) + RESIDUAL * final[0, h, r, :].astype(F32)
+            )
+        square = sum(jnp.sum(p * p, axis=-1, keepdims=True) for p in parts)
+        inverse = lax.rsqrt(square * (1.0 / width) + EPS)
+        return parts, inverse
+
+    chunks = rows // CHUNK
+    loads[0].wait()
+    for c in range(chunks):
+        left = joined_t[:, c * CHUNK : (c + 1) * CHUNK]
+
+        @pl.loop(0, width // 256)
+        def _(n):
+            cols = pl.ds(pl.multiple_of(n * 256, 256), 256)
+            side = n // (half // 256)
+            place = pl.ds(pl.multiple_of(lax.rem(n, half // 256) * 256, 256), 256)
+            part[side, span(c), place] = transposed_times(left, attn_out[:, cols]).astype(BF16)
+
+        hop(0, c, 0).start()
+    for c in range(chunks):
+        reduce_pair(0, c)
+
+    loads[1].wait()
+    for c in range(chunks):
+
+        @pl.loop(0, CHUNK // 32)
+        def _(i):
+            r = pl.ds(pl.multiple_of(c * CHUNK + i * 32, 32), 32)
+            o = pl.ds(pl.multiple_of(i * 32, 32), 32)
+            two[o, :] = (RESIDUAL * cotangent[r, :].astype(F32)).astype(BF16)
+
+        for a, b in cuts(down.shape[0]):
+            dhid[span(c), a:b] = times_transposed(two[...], down[a:b, :]).astype(BF16)
+
+    loads[2].wait()
+    loads[3].wait()
+    saves = []
+
+    def save(src, dst):
+        copy = pltpu.make_async_copy(src, dst, save_sem.at[len(saves)])
+        copy.start()
+        saves.append(copy)
+        return copy
+
+    two_saved = None
+    for c in range(chunks):
+        reduce_across(0, c)
+        if two_saved is not None:
+            two_saved.wait()
+
+        @pl.loop(0, CHUNK // 32)
+        def _(i):
+            r = pl.ds(pl.multiple_of(c * CHUNK + i * 32, 32), 32)
+            o = pl.ds(pl.multiple_of(i * 32, 32), 32)
+            parts, inverse = middle_rows(r)
+            for h in range(2):
+                cols = slice(h * half, (h + 1) * half)
+                two[o, cols] = (parts[h] * inverse * gain[:, cols]).astype(BF16)
+
+        two_saved = save(two, two_o.at[span(c)])
+        for a, b in cuts(gate_w.shape[0]):
+            gate = times_transposed(two[...], gate_w[a:b, :])
+            upper = times_transposed(two[...], up_w[a:b, :])
+            grad = dhid[span(c), a:b].astype(F32)
+            sigma = 1.0 / (1.0 + jnp.exp(-gate))
+            act = gate * sigma
+            trio[0, span(c), a:b] = (act * upper).astype(BF16)
+            trio[1, span(c), a:b] = (
+                grad * upper * sigma * (1.0 + gate * (1.0 - sigma))
+            ).astype(BF16)
+            trio[2, span(c), a:b] = (grad * act).astype(BF16)
+        for k, out in enumerate((hidden_o, dgate_o, dup_o)):
+            save(trio.at[k, span(c)], out.at[span(c)])
+        hop(0, c, 0).wait_send()
+
+        @pl.loop(0, width // 256)
+        def _(n):
+            cols = pl.ds(pl.multiple_of(n * 256, 256), 256)
+            side = n // (half // 256)
+            place = pl.ds(pl.multiple_of(lax.rem(n, half // 256) * 256, 256), 256)
+            value = matmul(trio[1, span(c), :], gate_w[:, cols])
+            value += matmul(trio[2, span(c), :], up_w[:, cols])
+            part[side, span(c), place] = value.astype(BF16)
+
+        hop(1, c, 0).start()
+        if c > 0:
+            reduce_pair(1, c - 1)
+    reduce_pair(1, chunks - 1)
+    two_saved.wait()
+
+    gain_o[...] = jnp.zeros_like(gain_o)
+    feed_saved = dmiddle_saved = None
+    for c in range(chunks):
+        if feed_saved is not None:
+            feed_saved.wait()
+
+        @pl.loop(0, width // 256)
+        def _(n):
+            cols = pl.ds(pl.multiple_of(n * 256, 256), 256)
+            feed[:, cols] = matmul(trio[0, span(c), :], down[:, cols]).astype(BF16)
+
+        feed_saved = save(feed, feed_o.at[span(c)])
+        reduce_across(1, c)
+        if dmiddle_saved is not None:
+            dmiddle_saved.wait()
+
+        @pl.loop(0, CHUNK // 32)
+        def _(i):
+            r = pl.ds(pl.multiple_of(c * CHUNK + i * 32, 32), 32)
+            o = pl.ds(pl.multiple_of(i * 32, 32), 32)
+            parts, inverse = middle_rows(r)
+            dot = jnp.zeros((32, 1), F32)
+            for h in range(2):
+                cols = slice(h * half, (h + 1) * half)
+                product = final[1, h, r, :].astype(F32) * (parts[h] * inverse)
+                gain_o[:, cols] += jnp.sum(product.reshape(4, 8, half), axis=0)
+                dot += jnp.sum(product * gain[:, cols], axis=-1, keepdims=True)
+            dot = dot * (1.0 / width)
+            for h in range(2):
+                cols = slice(h * half, (h + 1) * half)
+                weighted = final[1, h, r, :].astype(F32) * gain[:, cols]
+                value = cotangent[r, cols].astype(F32) + inverse * (
+                    weighted - parts[h] * inverse * dot
+                )
+                dmiddle[o, cols] = value
+                two[o, cols] = (RESIDUAL * value).astype(BF16)
+
+        dmiddle_saved = save(dmiddle, dmiddle_o.at[span(c)])
+        dmix_t[:, c * CHUNK : (c + 1) * CHUNK] = times_transposed(attn_out[...], two[...]).astype(
+            BF16
+        )
+    for h in range(2):
+        save(final.at[0, h], branch_o.at[h])
+    for copy in saves[-2:] + [feed_saved, dmiddle_saved]:
+        copy.wait()
+    for c in range(chunks):
+        for k in range(3):
+            saves[c * 4 + 1 + k].wait()
+    for job in range(2):
+        for c in range(chunks):
+            for kind in range(1 - job, last + 1):
+                hop(job, c, kind).wait_send()
+
+
+def feed_forward(tensors, joined_t, tokens, cotangent, gain, attn_out, down, gate_w, up_w):
+    rows, width = tokens.shape
+    units = down.shape[0]
+    chunks = rows // CHUNK
+    hops = tensors.bit_length() - 1
+    anywhere = pl.BlockSpec(memory_space=pl.ANY)
+    inside = pl.BlockSpec(memory_space=pltpu.VMEM)
+    return pl.pallas_call(
+        functools.partial(feed_forward_kernel, tensors),
+        in_specs=[inside] * 4 + [anywhere] * 4,
+        out_specs=[anywhere] * 7 + [inside] * 2,
+        out_shape=[
+            jax.ShapeDtypeStruct((2, rows, width // 2), BF16),
+            jax.ShapeDtypeStruct((rows, width), BF16),
+            jax.ShapeDtypeStruct((rows, units), BF16),
+            jax.ShapeDtypeStruct((rows, units), BF16),
+            jax.ShapeDtypeStruct((rows, units), BF16),
+            jax.ShapeDtypeStruct((rows, width), BF16),
+            jax.ShapeDtypeStruct((rows, width), F32),
+            jax.ShapeDtypeStruct((joined_t.shape[0], rows), BF16),
+            jax.ShapeDtypeStruct((8, width), F32),
+        ],
+        scratch_shapes=[
+            pltpu.VMEM(attn_out.shape, BF16),
+            pltpu.VMEM(down.shape, BF16),
+            pltpu.VMEM(gate_w.shape, BF16),
+            pltpu.VMEM(up_w.shape, BF16),
+            pltpu.VMEM((2, rows, width // 2), BF16),
+            pltpu.VMEM((2, 2, rows, width // 2), BF16),
+            pltpu.VMEM((2, rows, width // 2), BF16),
+            pltpu.VMEM((hops - 1, 2, rows, width // 2), BF16),
+            pltpu.VMEM((rows, units), BF16),
+            pltpu.VMEM((CHUNK, width), BF16),
+            pltpu.VMEM((3, rows, units), BF16),
+            pltpu.VMEM((CHUNK, width), BF16),
+            pltpu.VMEM((CHUNK, width), F32),
+            pltpu.SemaphoreType.DMA((4,)),
+            pltpu.SemaphoreType.DMA((6 * chunks + 2,)),
+            pltpu.SemaphoreType.DMA((2, hops + 1, chunks)),
+            pltpu.SemaphoreType.DMA((2, hops + 1, chunks)),
+        ],
+        compiler_params=pltpu.CompilerParams(
+            collective_id=0, has_side_effects=True, vmem_limit_bytes=63 * 1024 * 1024
+        ),
+        cost_estimate=pl.CostEstimate(
+            flops=2 * rows * width * units * 6, bytes_accessed=60 * 1024 * 1024, transcendentals=0
+        ),
+        name="feed_forward",
+    )(joined_t, tokens, cotangent, gain, attn_out, down, gate_w, up_w)
+
+
+def after(value, *others):
+    return lax.optimization_barrier((value, others))[0]
+
+
 def swap(value, axis, size, bit):
     return lax.ppermute(value, axis, [(i, i ^ bit) for i in range(size)])
 
@@ -382,56 +718,101 @@
     return lax.ppermute(value, axis, [(i, (i + by) % size) for i in range(size)])
 
 
-def tensor_sum(value, size):
+def add_low(left, right):
+    return (left.astype(F32) + right.astype(F32)).astype(BF16)
+
+
+def pick(value, index):
+    return lax.dynamic_index_in_dim(value, index, 0, keepdims=False)
+
+
+def tensor_halves(value, size):
     low = value.astype(BF16)
     bit = lax.axis_index("tensor") % 2
-    half = low.shape[0] // 2
-    keep = lax.dynamic_slice_in_dim(low, bit * half, half, 0)
-    give = lax.dynamic_slice_in_dim(low, (1 - bit) * half, half, 0)
-    mine = (keep.astype(F32) + swap(give, "tensor", size, 1).astype(F32)).astype(BF16)
+    parts = low.reshape((2, low.shape[0] // 2) + low.shape[1:])
+    return add_low(pick(parts, bit), swap(pick(parts, 1 - bit), "tensor", size, 1))
+
+
+def tensor_pairs(mine, size):
     step = 2
     while step < size:
-        mine = (mine.astype(F32) + swap(mine, "tensor", size, step).astype(F32)).astype(BF16)
+        mine = add_low(mine, swap(mine, "tensor", size, step))
         step *= 2
+    return mine
+
+
+def tensor_back(mine, size):
+    bit = lax.axis_index("tensor") % 2
     other = swap(mine, "tensor", size, 1)
-    first = jnp.where(bit == 0, mine, other)
-    second = jnp.where(bit == 0, other, mine)
-    return jnp.concatenate([first, second], axis=0).astype(F32)
-
-
-def line_scatter(pieces, size):
+    return jnp.concatenate(
+        [jnp.where(bit == 0, mine, other), jnp.where(bit == 0, other, mine)], axis=0
+    ).astype(F32)
+
+
+def tensor_sum(value, size):
+    return tensor_back(tensor_pairs(tensor_halves(value, size), size), size)
+
+
+def tensor_scatter(value, size):
+    low = value.astype(BF16)
+    t = lax.axis_index("tensor")
+    step = 1
+    while step < size:
+        bit = (t // step) % 2
+        parts = low.reshape((2, low.shape[0] // 2) + low.shape[1:])
+        low = add_low(pick(parts, bit), swap(pick(parts, 1 - bit), "tensor", size, step))
+        step *= 2
+    return low
+
+
+def tensor_unscatter(value, size):
+    t = lax.axis_index("tensor")
+    step = size // 2
+    while step >= 1:
+        bit = (t // step) % 2
+        other = swap(value, "tensor", size, step)
+        value = jnp.concatenate(
+            [jnp.where(bit == 0, value, other), jnp.where(bit == 0, other, value)], axis=0
+        )
+        step //= 2
+    return value
+
+
+def line_send(pieces, size, step, arrived=None):
     z = lax.axis_index("context")
     last = size - 1
-
-    def take(index):
-        return lax.dynamic_index_in_dim(pieces, index, 0, keepdims=False)
-
-    right = left = None
-    for step in range(1, size):
-        up = take(jnp.clip(size + z - step, 0, last))
-        down = take(jnp.clip(last - (size + (last - z) - step), 0, last))
-        if right is not None:
-            up = (up.astype(F32) + right.astype(F32)).astype(BF16)
-            down = (down.astype(F32) + left.astype(F32)).astype(BF16)
-        right = lax.ppermute(up, "context", [(i, i + 1) for i in range(step)])
-        left = lax.ppermute(down, "context", [(last - i, last - i - 1) for i in range(step)])
-    return take(z).astype(F32) + right.astype(F32) + left.astype(F32)
+    up = pick(pieces, jnp.clip(size + z - step, 0, last))
+    down = pick(pieces, jnp.clip(last - (size + (last - z) - step), 0, last))
+    if arrived is not None:
+        up = add_low(up, arrived[0])
+        down = add_low(down, arrived[1])
+    right = lax.ppermute(up, "context", [(i, i + 1) for i in range(step)])
+    left = lax.ppermute(down, "context", [(last - i, last - i - 1) for i in range(step)])
+    return (right, left)
+
+
+def line_end(pieces, arrived):
+    own = pick(pieces, lax.axis_index("context"))
+    return own.astype(F32) + arrived[0].astype(F32) + arrived[1].astype(F32)
+
+
+def line_spread(pair, size, step):
+    right = lax.ppermute(pair[0], "context", [(i, i + 1) for i in range(step - 1, size - 1)])
+    left = lax.ppermute(pair[1], "context", [(i, i - 1) for i in range(1, size - step + 1)])
+    return (right, left)
 
 
 def direct_scatter(pieces, size):
     z = lax.axis_index("context")
-    total = lax.dynamic_index_in_dim(pieces, z, 0, keepdims=False).astype(F32)
+    total = pick(pieces, z).astype(F32)
     for by in range(1, size):
-        piece = lax.dynamic_index_in_dim(pieces, (z + by) % size, 0, keepdims=False)
-        total = total + shift(piece, "context", size, by).astype(F32)
+        total = total + shift(pick(pieces, (z + by) % size), "context", size, by).astype(F32)
     return total
 
 
 def pair_scatter(value):
     d = lax.axis_index("dp")
-    keep = lax.dynamic_index_in_dim(value, d, 0, keepdims=False)
-    give = lax.dynamic_index_in_dim(value, 1 - d, 0, keepdims=False)
-    return (keep.astype(F32) + swap(give, "dp", 2, 1).astype(F32)).astype(BF16)
+    return add_low(pick(value, d), swap(pick(value, 1 - d), "dp", 2, 1))
 
 
 def tensor_gather(value, size):
@@ -470,6 +851,8 @@
     d = lax.axis_index("dp")
     t = lax.axis_index("tensor")
     half_width = width // 2
+    share = half_width // contexts
+    rank = query_down.shape[1]
 
     mine = lax.dynamic_slice_in_dim(group_order, 2 * z, 2)
     offsets = jnp.arange(HALF, dtype=jnp.int32)
@@ -490,16 +873,6 @@
     inputs = tokens[0].astype(F32)
     upstream = cotangent[0].astype(F32)
     grad_feed = (RESIDUAL * upstream).astype(BF16)
-
-    def own_half(value):
-        return lax.dynamic_slice_in_dim(value, d * half_width, half_width, 1)
-
-    def other_half(value):
-        return lax.dynamic_slice_in_dim(value, (1 - d) * half_width, half_width, 1)
-
-    grad_feed_both = jnp.concatenate(
-        [own_half(grad_feed), swap(other_half(grad_feed), "dp", 2, 1)], axis=0
-    )
 
     first_normed, first_inverse = scaled(inputs)
     hidden_one = (first_normed * attn_gain).astype(BF16)
@@ -542,73 +915,117 @@
         axis=1,
     ).astype(BF16)
 
+    feed_t = grad_feed.T.reshape(2, contexts, share, rows)
+    feed_t_sent = after(feed_t, far_all)
+    feed_slots = [pick(jnp.swapaxes(feed_t, 0, 1), z)] + [
+        shift(pick(jnp.swapaxes(feed_t_sent, 0, 1), (z + by) % contexts), "context", contexts, by)
+        for by in range(1, contexts)
+    ]
+
     joined_t, exact_t, lse = attention_forward(
         place, q_t, latent_all, latent_all_t, rope_all, latent_up, latent_up_t
     )
 
-    branch = tensor_sum(transposed_times(joined_t, attn_out), tensors)
-    middle = inputs + RESIDUAL * branch
-    second_normed, second_inverse = scaled(middle)
-    hidden_two = (second_normed * mlp_gain).astype(BF16)
-    hidden_two_both = jnp.concatenate(
-        [own_half(hidden_two), swap(other_half(hidden_two), "dp", 2, 1)], axis=0
-    )
-    grad_hidden = times_transposed(grad_feed, down_proj)
-    gate = matmul(hidden_two, gate_proj)
-    upper = matmul(hidden_two, up_proj)
-    sigma = jax.nn.sigmoid(gate)
-    hidden_mid = (gate * sigma * upper).astype(BF16)
-    grad_gate = (grad_hidden * upper * sigma * (1.0 + gate * (1.0 - sigma))).astype(BF16)
-    grad_upper = (grad_hidden * gate * sigma).astype(BF16)
-
-    def both(value):
-        return jnp.concatenate([value, swap(value, "dp", 2, 1)], axis=0)
-
-    def weight_pieces(left, right):
-        full = transposed_times(left, right).astype(BF16)
-        return full.reshape(contexts, half_width // contexts, right.shape[1])
-
-    grad_hidden_two = tensor_sum(
-        times_transposed(grad_gate, gate_proj) + times_transposed(grad_upper, up_proj), tensors
-    )
-    feed = tensor_sum(matmul(hidden_mid, down_proj), tensors)
-    layer_out = (middle + RESIDUAL * feed).astype(BF16)
-
-    grad_down = line_scatter(weight_pieces(grad_feed_both, both(hidden_mid)), contexts).T
-    grad_gate_proj = line_scatter(weight_pieces(hidden_two_both, both(grad_gate)), contexts)
-    grad_up_proj = line_scatter(weight_pieces(hidden_two_both, both(grad_upper)), contexts)
-
-    grad_norm_two, grad_mlp_gain = norm_back(
-        grad_hidden_two, second_normed, second_inverse, mlp_gain
-    )
-    grad_middle = upstream + grad_norm_two
+    (
+        branch,
+        hidden_two,
+        hidden_mid,
+        grad_gate,
+        grad_upper,
+        feed_part,
+        grad_middle,
+        dmix_t,
+        grad_mlp_gain,
+    ) = feed_forward(
+        tensors,
+        joined_t,
+        tokens[0],
+        cotangent[0],
+        mlp_gain[None],
+        attn_out,
+        down_proj,
+        gate_proj.T,
+        up_proj.T,
+    )
+    grad_mlp_gain = jnp.sum(grad_mlp_gain, axis=0)
+    middle = inputs + RESIDUAL * jnp.concatenate([branch[0], branch[1]], axis=1).astype(F32)
+    hidden_two_t = hidden_two.T
+    two_t_parts = hidden_two_t.reshape(2, half_width, rows)
+    two_t_far = swap(pick(two_t_parts, 1 - d), "dp", 2, 1)
+
+    spread_one = line_spread((hidden_mid, hidden_mid), contexts, 1)
+    gate_far = swap(grad_gate, "dp", 2, 1)
+    upper_far = swap(after(grad_upper, gate_far), "dp", 2, 1)
+
+    spreads = [spread_one]
+    spreads.append(line_spread(spreads[-1], contexts, 2))
+
+    two_t_both = jnp.concatenate([pick(two_t_parts, d), two_t_far], axis=1)
+
+    def weight_pieces(own, far):
+        full = matmul(two_t_both, jnp.concatenate([own, far], axis=0)).astype(BF16)
+        return full.reshape(contexts, share, own.shape[1])
+
+    gate_pieces = weight_pieces(grad_gate, gate_far)
+    gate_moved = line_send(gate_pieces, contexts, 1)
+
     grad_branch = (RESIDUAL * grad_middle).astype(BF16)
-    grad_attn_out_t = lax.dot_general(
-        grad_branch, joined_t, (((0,), (1,)), ((), ())), preferred_element_type=F32
-    ).astype(BF16)
-    grad_attn_out = line_scatter(
-        pair_scatter(
-            grad_attn_out_t.reshape(2, contexts, half_width // contexts, joined_t.shape[0])
-        ),
-        contexts,
-    ).T
-    dmix_t = times_transposed(attn_out, grad_branch).astype(BF16)
-
-    dq_t, grad_latent_up, dlat_t = attention_backward(
-        place,
-        q_t,
-        latent_all,
-        latent_all_t,
-        rope_all,
-        rope_all_t,
-        latent_up,
-        latent_up_t,
-        exact_t,
-        lse,
-        dmix_t,
-        cos_t,
-        sin_t,
-    )
+    grad_branch_t = grad_branch.T
+
+    up_pieces = weight_pieces(grad_upper, upper_far)
+    up_moved = line_send(up_pieces, contexts, 1)
+    feed_half = tensor_halves(feed_part, tensors)
+
+    halves = 2 if heads % (2 * GROUP) == 0 else 1
+    count = heads // halves
+    back = []
+    ready = (up_pieces, gate_pieces, feed_half)
+    steps = 2
+    feed_mid = out_moved = None
+    for half in range(halves):
+        cut = slice(half * count, (half + 1) * count)
+        back.append(
+            attention_backward(
+                after(place, ready),
+                q_t[cut],
+                latent_all,
+                latent_all_t,
+                rope_all,
+                rope_all_t,
+                latent_up[:, half * count * 128 : (half + 1) * count * 128],
+                latent_up_t[half * count * 128 : (half + 1) * count * 128],
+                exact_t[cut],
+                lse[cut],
+                dmix_t[half * count * V_DIM : (half + 1) * count * V_DIM],
+                cos_t,
+                sin_t,
+            )
+        )
+        done = back[-1]
+        if half == 0:
+            feed_mid = tensor_pairs(after(feed_half, dmix_t), tensors)
+            out_full = times_transposed(after(grad_branch_t, done), joined_t).astype(BF16)
+            out_pieces = pair_scatter(out_full.reshape(2, contexts, share, joined_t.shape[0]))
+        gate_moved = line_send(gate_pieces, contexts, steps, after(gate_moved, done))
+        up_moved = line_send(up_pieces, contexts, steps, after(up_moved, done))
+        spreads.append(line_spread(after(spreads[-1], done), contexts, steps + 1)) if (
+            steps + 1 < contexts
+        ) else None
+        steps += 1
+        ready = (done, out_full)
+    dq_t = jnp.concatenate([b[0] for b in back], axis=0)
+    grad_latent_up = jnp.concatenate([b[1] for b in back], axis=1)
+    dlat_t = back[0][2]
+    for b in back[1:]:
+        dlat_t = dlat_t.astype(F32) + b[2].astype(F32)
+
+    dlat_own = tensor_scatter(dlat_t, tensors)
+    total = dlat_own[:, :rows].astype(F32)
+    for by in range(1, contexts):
+        moved = shift(dlat_own[:, by * rows : (by + 1) * rows], "context", contexts, -by)
+        total = total + moved.astype(F32)
+    grad_keys = tensor_unscatter(total.astype(BF16), tensors).astype(F32).T
+
     grad_query_full_t = dq_t.reshape(heads * (NOPE + ROPE), rows)
     grad_query_latent = tensor_sum(
         lax.dot_general(
@@ -620,13 +1037,19 @@
         query_latent, grad_query_full_t, (((0,), (1,)), ((), ())), preferred_element_type=F32
     ).astype(BF16)
 
-    dlat = tensor_sum(dlat_t, tensors).astype(BF16)
-    total = dlat[:, :rows].astype(F32)
-    for by in range(1, contexts):
-        total = total + shift(dlat[:, by * rows : (by + 1) * rows], "context", contexts, -by).astype(
-            F32
-        )
-    grad_keys = total.T
+    while steps < contexts:
+        gate_moved = line_send(gate_pieces, contexts, steps, gate_moved)
+        up_moved = line_send(up_pieces, contexts, steps, up_moved)
+        if steps + 1 < contexts:
+            spreads.append(line_spread(spreads[-1], contexts, steps + 1))
+        steps += 1
+    out_moved = None
+    for step in range(1, contexts):
+        out_moved = line_send(out_pieces, contexts, step, out_moved)
+
+    feed = tensor_back(after(feed_mid, dq_t), tensors)
+    layer_out = (middle + RESIDUAL * feed).astype(BF16)
+
     grad_query_low, grad_query_gain = norm_back(
         grad_query_latent, query_normed, query_inverse, query_gain
     )
@@ -636,7 +1059,6 @@
     grad_low = jnp.concatenate(
         [grad_query_low, grad_cache, unrotate(grad_keys[:, KV_RANK:], cosine, sine)], axis=1
     ).astype(BF16)
-    rank = query_down.shape[1]
     grad_hidden_one = times_transposed(grad_low[:, :rank], query_down) + times_transposed(
         grad_low[:, rank:], latent_down
     )
@@ -645,55 +1067,61 @@
     )
     token_grad = grad_middle + grad_norm_one
 
-    grad_query_up = direct_scatter(
-        pair_scatter(grad_query_up.reshape(2, contexts, -1, grad_query_up.shape[1])), contexts
-    )
-    grad_latent_up = direct_scatter(
-        pair_scatter(grad_latent_up.reshape(2, contexts, -1, grad_latent_up.shape[1])), contexts
-    )
-    grad_down_low = transposed_times(hidden_one, grad_low).astype(BF16)
-    grad_down_low = grad_down_low.reshape(2, contexts, tensors, -1, grad_low.shape[1])
-    grad_down_low = lax.dynamic_index_in_dim(grad_down_low, t, 2, keepdims=False)
-    grad_down_low = direct_scatter(pair_scatter(grad_down_low), contexts).astype(BF16)
-    grad_down_low = (
-        tensor_gather(grad_down_low, tensors).reshape(-1, grad_low.shape[1]).astype(F32)
-    )
-
-    def pieces(value):
-        return value.reshape(2 * contexts, -1)
+    up_rows = grad_query_up.shape[0] // (2 * contexts)
+    lat_rows = grad_latent_up.shape[0] // (2 * contexts)
+    lanes = max(grad_query_up.shape[1], grad_latent_up.shape[1])
+
+    def widen(value):
+        value = jnp.pad(value, ((0, 0), (0, lanes - value.shape[1])))
+        return value.reshape(2, contexts, -1, lanes)
+
+    small = jnp.concatenate([widen(grad_query_up), widen(grad_latent_up)], axis=2)
+    small = direct_scatter(pair_scatter(small), contexts)
+
+    low = matmul(hidden_one.T, grad_low).astype(BF16)
+    low = low.reshape(2, contexts, tensors, -1, grad_low.shape[1])
+    low = lax.dynamic_index_in_dim(low, t, 2, keepdims=False)
+
+    def spare(value):
+        return value.reshape(2, contexts, -1)
 
     gains = jnp.concatenate(
-        [
-            pieces(grad_attn_gain),
-            pieces(grad_query_gain),
-            pieces(grad_latent_gain),
-            pieces(grad_mlp_gain),
-        ],
-        axis=1,
-    )
-    gains = lax.dynamic_index_in_dim(
-        lax.psum(gains, ("dp", "context")), d * contexts + z, 0, keepdims=False
-    )
-    sizes = [v.shape[0] // (2 * contexts) for v in (attn_gain, query_gain, latent_gain, mlp_gain)]
+        [spare(grad_attn_gain), spare(grad_query_gain), spare(grad_latent_gain), spare(grad_mlp_gain)],
+        axis=2,
+    ).astype(BF16)
+    gains = jnp.pad(gains, ((0, 0), (0, 0), (0, grad_low.shape[1] - gains.shape[2])))
+    low = jnp.concatenate([low, gains[:, :, None]], axis=2)
+    low = direct_scatter(pair_scatter(low), contexts)
+    gains = low[-1]
+    low = tensor_gather(low[:-1].astype(BF16), tensors).reshape(-1, grad_low.shape[1]).astype(F32)
     edges = [0]
-    for size in sizes:
-        edges.append(edges[-1] + size)
+    for value in (attn_gain, query_gain, latent_gain, mlp_gain):
+        edges.append(edges[-1] + value.shape[0] // (2 * contexts))
     gain_grads = [gains[a:b] for a, b in zip(edges[:-1], edges[1:])]
+
+    slots = [hidden_mid]
+    for s in range(1, contexts):
+        slots.append(jnp.where(z >= s, spreads[s - 1][0], spreads[contexts - s - 1][1]))
+    hidden_all = jnp.concatenate(slots, axis=0)
+    feed_all = jnp.concatenate(feed_slots, axis=2).reshape(2 * share, contexts * rows)
+    down_full = matmul(feed_all, hidden_all).reshape(2, share, -1)
+    down_far = swap(pick(down_full, 1 - d).astype(BF16), "dp", 2, 1)
+    grad_down = (pick(down_full, d) + down_far.astype(F32)).T
 
     return (
         layer_out[None],
         token_grad[None],
         gain_grads[0],
-        grad_down_low[:, :rank],
+        low[:, :rank],
         gain_grads[1],
-        grad_down_low[:, rank:],
+        low[:, rank:],
         gain_grads[2],
-        grad_query_up,
-        grad_latent_up,
-        grad_attn_out,
+        small[:up_rows, : grad_query_up.shape[1]],
+        small[up_rows:, : grad_latent_up.shape[1]],
+        line_end(out_pieces, out_moved).T,
         gain_grads[3],
-        grad_gate_proj,
-        grad_up_proj,
+        line_end(gate_pieces, gate_moved),
+        line_end(up_pieces, up_moved),
         grad_down,
     )
 

time: 873 us -> 737 us (0.84); the launches traced: 862 us -> 734 us
  waiting for transfers between devices: 319 us -> 152 us
  Pallas kernels: 58.8 us -> 148 us
  matrix products: 117 us -> 55.4 us
  local copies, waits for them, and re-layouts: 87.7 us -> 127 us
  blocking collectives: 28.5 us -> 0 us
  starting transfers between devices: 154 us -> 166 us
  other arithmetic: 93.7 us -> 82.1 us
    ppermute x25 -> x18, waiting for transfers between devices: 147 us -> 42.5 us  [swap(): return lax.ppermute(value, axis, [(i, i ^ bit) for i in range(size)])]
    pallas_call x0 -> x1, Pallas kernels: none -> 96.2 us  [feed_forward(): pl.pallas_call(functools.partial(feed_forward_kernel, tensors), in_specs=...]
    ppermute x24, waiting for transfers between devices: 154 us -> 68.4 us  [the longest x9 24.8 us: line_send(): lax.ppermute(down, 'context', [(last - i, last - i - 1) for i in range(st...]
    dot_general x6 -> x0, matrix products: 38.9 us -> none  [the longest x5 33.5 us: transposed_times(): lax.dot_general(left, right, (((0,), (0,)), ((), ())), preferred_element_...]
    psum x1 -> x0, blocking collectives: 28.5 us -> none  [per_device(): lax.psum(gains, ('dp', 'context'))]
    ppermute x0 -> x8, local copies, waits for them, and re-layouts: none -> 27.2 us  [the longest x3 9.85 us: line_spread(): lax.ppermute(pair[0], 'context', [(i, i + 1) for i in range(step - 1, siz...]
    dot_general x6 -> x3, matrix products: 38.6 us -> 12 us  [times_transposed(): lax.dot_general(left, right, (((1,), (1,)), ((), ())), preferred_element_...]
    ppermute x18, waiting for transfers between devices: 17.9 us -> 41.6 us  [shift(): lax.ppermute(value, axis, [(i, (i + by) % size) for i in range(size)])]
  transfers between devices with their start and end apart: 67 -> 60, of which waited for: 21 -> 15; matrix products, arithmetic and copies ran while one was open for 26% -> 32% of each run, Pallas kernels for 5% -> 5%
where the time goes in v2:
time: 737 us; the launch traced here: 734 us
  starting transfers between devices  166 us (23%)
  waiting for transfers between devices  152 us (21%)
  Pallas kernels  148 us (20%)
  local copies, waits for them, and re-layouts  127 us (17%)
  other arithmetic  82.1 us (11%)
  matrix products  55.4 us (8%)
    pallas_call x1, Pallas kernels, feed_forward(): pl.pallas_call(functools.partial(feed_forward_kernel, tensors), in_specs=...  96.2 us
    ppermute x18, starting transfers between devices, shift(): lax.ppermute(value, axis, [(i, (i + by) % size) for i in range(size)])  82.2 us
    ppermute x18, waiting for transfers between devices, swap(): return lax.ppermute(value, axis, [(i, i ^ bit) for i in range(size)])  42.5 us
    ppermute x18, waiting for transfers between devices, shift(): lax.ppermute(value, axis, [(i, (i + by) % size) for i in range(size)])  41.6 us
    dot_general x6, matrix products, matmul(): return jnp.dot(left, right, preferred_element_type=F32)  38.5 us
    pallas_call x2, Pallas kernels, attention_backward(): pl.pallas_call(functools.partial(backward_kernel, heads), grid=(count //...  36.8 us
    ppermute x9, waiting for transfers between devices, line_send(): lax.ppermute(down, 'context', [(last - i, last - i - 1) for i in range(st...  24.8 us
    convert_element_type x16, other arithmetic, add_low(): return (left.astype(F32) + right.astype(F32)).astype(BF16)  24.6 us
  transfers between devices with their start and end apart: 60, of which 15 were waited for; matrix products, arithmetic and copies ran while one was open for 32% of the time, Pallas kernels for 5%

profile of v2, /device:TPU:9, one launch (start us, length us, event | category | flops | bytes accessed | tf_op | source)
XLA Modules:
  0.0 734.3 jit_solution(3977062401112956435)
XLA Ops:
  20.0 5.6 multiply_reduce_fusion
  26.5 3.7 fusion.27
  30.2 3.4 copy.232
  34.5 2.9 fusion.114
  51.5 15.2 %attention_forward.1 = (bf16[640,512]{1,0:T(8,128)(2,1)}, f32[10,64,512]{2,1,0:T(8,128)}, f32[10,1,512]{2,1,0:T(1,128)}) custom-call(s32[10]{0:T(128)} %pad_add_fusion.place, bf16[10,96,512]{2,1,0:T(8,128)(2,1)} %pad_maximum_fusion.3.q_t, bf16[2048,256]{1,0:T(8,128)(2,1)} %copy.210.latent, bf16[256,2048]{1,0:T(8,128)(2,1)} %slice.202.latent_t, ...), custom_call_target="tpu_custom_call" | custom-call | flops 8053063680 | bytes 12582912 | tf_op jit(solution)/shard_map/attention_forward/pallas_call | solution.py:259
  66.6 96.2 %feed_forward.1 = (bf16[2,512,1280]{2,1,0:T(8,128)(2,1)}, bf16[512,2560]{1,0:T(8,128)(2,1)}, bf16[512,1600]{1,0:T(8,128)(2,1)}, bf16[512,1600]{1,0:T(8,128)(2,1)...) custom-call(bf16[640,512]{1,0:T(8,128)(2,1)} %get-tuple-element.49.j, ...), custom_call_target="tpu_custom_call" | custom-call | flops 25165824000 | bytes 62914560 | tf_op jit(solution)/shard_map/feed_forward/pallas_call | solution.py:665
  162.9 3.8 copy.233
  166.6 4.3 collective-permute-start.53
  171.0 11.6 %collective-permute-start.55 = (bf16[512,1600]{0,1:T(8,128)(2,1)}, bf16[512,1600]{0,1:T(8,128)(2,1)}, u32[]{:S(2)}, u32[]{:S(2)}) collective-permute-start(bf16[512,1600]{0,1:T(8,128)(2,1)} %copy.233), channel_id=1, source_target_pairs={{4,0},{8,4},{12,8},{5,1},{9,5},{13,9},{6,2},{10,6},{14,10},{7,3},{... | collective-permute-start | bytes 4915208 | tf_op jit(solution)/shard_map/ppermute | solution.py:801
  190.0 3.0 copy.245
  194.9 4.7 fusion.26
  207.8 18.2 %collective-permute-done.7 = bf16[512,1600]{0,1:T(8,128)(2,1)} collective-permute-done((bf16[512,1600]{0,1:T(8,128)(2,1)}, bf16[512,1600]{0,1:T(8,128)(2,1)}, u32[]{:S(2)}, u32[]{:S(2)}) %collective-permute-start.7) | collective-permute-done | bytes 1638432 | tf_op jit(solution)/shard_map/ppermute | solution.py:714
  226.0 3.6 copy.215
  230.8 3.5 copy.218
  234.3 19.8 %collective-permute-done.6 = bf16[1280,512]{1,0:T(8,128)(2,1)} collective-permute-done((bf16[1280,512]{1,0:T(8,128)(2,1)}, bf16[1280,512]{1,0:T(8,128)(2,1)}, u32[]{:S(2)}, u32[]{:S(2)}) %collective-permute-start.6) | collective-permute-done | bytes 1310752 | tf_op jit(solution)/shard_map/ppermute | solution.py:714
  254.1 8.8 %convolution_convert_fusion.1 = bf16[1280,1600]{0,1:T(8,128)(2,1)} fusion(bf16[512,1600]{1,0:T(8,128)(2,1)} %copy.218, bf16[512,1600]{1,0:T(8,128)(2,1)} %get-tuple-element.56, bf16[1280,512]{1,0:T(8,128)(2,1)} %collective-permute-done.6, bf16[1280,512]{1,0:T(8,128)(2,1)S(1)} %copy-done.37), kind=kOutput, calls=%fused_computation.1 | convolution fusion | flops 4208148480 | bytes 9994240 | tf_op jit(solution)/shard_map/dot_general | solution.py:28
  262.9 6.8 copy.219
  269.7 3.0 dynamic-slice_bitcast_fusion.7
  275.7 3.6 copy.235
  281.8 3.5 copy.240
  285.3 4.3 collective-permute-start.56
  292.4 4.0 copy.216
  296.4 8.7 %convolution_convert_fusion.2 = bf16[1280,1600]{0,1:T(8,128)(2,1)} fusion(bf16[512,1600]{1,0:T(8,128)(2,1)} %copy.216, bf16[512,1600]{1,0:T(8,128)(2,1)S(1)} %copy-done.30, bf16[1280,512]{1,0:T(8,128)(2,1)} %collective-permute-done.6, bf16[1280,512]{1,0:T(8,128)(2,1)} %get-tuple-element.197), kind=kOutput, calls=%fused_computation.2 | convolution fusion | flops 4208148480 | bytes 9994240 | tf_op jit(solution)/shard_map/dot_general | solution.py:28
  305.1 6.8 copy.217
  311.9 18.4 %attention_backward.2 = (bf16[5,96,512]{2,1,0:T(8,128)(2,1)}, bf16[256,640]{1,0:T(8,128)(2,1)}, bf16[288,2048]{1,0:T(8,128)(2,1)}) custom-call(s32[10]{0:T(128)} %pad_add_fusion.place, bf16[5,96,512]{2,1,0:T(8,128)(2,1)} %get-tuple-element.213.q_t, bf16[2048,256]{1,0:T(8,128)(2,1)} %copy.210.latent, bf16[256,2048]{1,0:T(8,128)(2,1)} %slice.202.latent_t, ...), custom_call_target="tpu_custom_call" | custom-call | flops 10485760000 | bytes 16777216 | tf_op jit(solution)/shard_map/attention_backward/pallas_call | solution.py:317
  332.1 5.1 convolution_convert_fusion.3
  337.2 18.4 %attention_backward.3 = (bf16[5,96,512]{2,1,0:T(8,128)(2,1)}, bf16[256,640]{1,0:T(8,128)(2,1)}, bf16[288,2048]{1,0:T(8,128)(2,1)}) custom-call(s32[10]{0:T(128)} %pad_add_fusion.place, bf16[5,96,512]{2,1,0:T(8,128)(2,1)} %get-tuple-element.212.q_t, bf16[2048,256]{1,0:T(8,128)(2,1)} %copy.210.latent, bf16[256,2048]{1,0:T(8,128)(2,1)} %slice.202.latent_t, ...), custom_call_target="tpu_custom_call" | custom-call | flops 10485760000 | bytes 16777216 | tf_op jit(solution)/shard_map/attention_backward/pallas_call | solution.py:317
  358.7 2.9 collective-permute-start.10
  368.7 3.5 copy.237
  372.3 3.1 dynamic-slice_bitcast_fusion.5
  376.6 3.5 copy.238
  380.2 3.0 broadcast_select_fusion.1
  392.7 3.7 collective-permute-done.14
  396.5 7.4 %collective-permute-start.17 = (bf16[72,512]{1,0:T(8,128)(2,1)S(1)}, bf16[72,512]{1,0:T(8,128)(2,1)S(1)}, u32[]{:S(2)}, u32[]{:S(2)}) collective-permute-start(bf16[72,512]{1,0:T(8,128)(2,1)S(1)} %get-tuple-element.234), channel_id=1, source_target_pairs={{0,4},{4,8},{8,12},{12,0},{1,5},{5,9},{9,13},{13,1},{2,6},{6,10},{... | collective-permute-start | bytes 221192 | tf_op jit(solution)/shard_map/ppermute | solution.py:718
  403.9 24.2 %collective-permute-start.16 = (bf16[72,512]{1,0:T(8,128)(2,1)S(1)}, bf16[72,512]{1,0:T(8,128)(2,1)S(1)}, u32[]{:S(2)}, u32[]{:S(2)}) collective-permute-start(bf16[72,512]{1,0:T(8,128)(2,1)S(1)} %get-tuple-element.235), channel_id=1, source_target_pairs={{0,8},{4,12},{8,0},{12,4},{1,9},{5,13},{9,1},{13,5},{2,10},{6,14},... | collective-permute-start | bytes 221192 | tf_op jit(solution)/shard_map/ppermute | solution.py:718
  433.1 3.8 collective-permute-start.15
  437.8 19.2 %collective-permute-done.15 = bf16[72,512]{1,0:T(8,128)(2,1)S(1)} collective-permute-done((bf16[72,512]{1,0:T(8,128)(2,1)S(1)}, bf16[72,512]{1,0:T(8,128)(2,1)S(1)}, u32[]{:S(2)}, u32[]{:S(2)}) %collective-permute-start.15) | collective-permute-done | bytes 73760 | tf_op jit(solution)/shard_map/ppermute | solution.py:718
  462.8 3.1 fusion.38
  468.2 3.4 collective-permute-start.9
  484.5 4.7 fusion.17
  489.8 2.9 concatenate.111
  492.7 6.4 convolution_convert_fusion
  499.1 8.6 %copy.227 = bf16[2560,1056]{1,0:T(8,128)(2,1)} copy(bf16[2560,1056]{0,1:T(8,128)(2,1)} %convolution_convert_fusion) | data formatting | bytes 10813440 | tf_op jit(solution)/shard_map/convert_element_type | solution.py:1081
  508.0 7.9 %fusion.16 = f32[1,512,2560]{2,1,0:T(8,128)} fusion(f32[512,2560]{1,0:T(8,128)} %get-tuple-element.64, f32[512,2560]{1,0:T(8,128)} %get-tuple-element.246, f32[512]{0:T(512)S(1)} %copy-done.76, f32[2560]{0:T(1024)S(1)} %copy-done.58, f32[512]{0:T(512)S(1)} %copy-done.68, bf16[1,512,2560]{2,1,0:T(8,128)(2,1)S(1)} %copy-done.1), kind=kLoop, calls=%fused_computation.22 | loop fusion | flops 9175040 | bytes 18364416 | tf_op jit(solution)/shard_map/broadcast_in_dim | solution.py:1113
  529.6 4.1 add_convert_fusion
  539.3 19.6 %collective-permute-done.57 = bf16[512,1600]{0,1:T(8,128)(2,1)} collective-permute-done((bf16[512,1600]{0,1:T(8,128)(2,1)}, bf16[512,1600]{0,1:T(8,128)(2,1)}, u32[]{:S(2)}, u32[]{:S(2)}) %collective-permute-start.57) | collective-permute-done | bytes 1638432 | tf_op jit(solution)/shard_map/ppermute | solution.py:801
  558.9 4.1 collective-permute-start.43
  566.0 4.5 collective-permute-start.29
  572.8 6.6 fusion
  583.2 11.3 %collective-permute-done.30 = bf16[128,1280]{1,0:T(8,128)(2,1)S(1)} collective-permute-done((bf16[128,1280]{1,0:T(8,128)(2,1)}, bf16[128,1280]{1,0:T(8,128)(2,1)S(1)}, u32[]{:S(2)}, u32[]{:S(2)}) %collective-permute-start.30) | collective-permute-done | bytes 327712 | tf_op jit(solution)/shard_map/ppermute | solution.py:718
  594.5 4.8 collective-permute-start.42
  599.2 3.2 collective-permute-done.29
  603.9 14.3 %collective-permute-start.23 = (bf16[81,1056]{1,0:T(8,128)(2,1)S(1)}, bf16[81,1056]{1,0:T(8,128)(2,1)S(1)}, u32[]{:S(2)}, u32[]{:S(2)}) collective-permute-start(bf16[81,1056]{1,0:T(8,128)(2,1)S(1)} %get-tuple-element.217), channel_id=1, source_target_pairs={{0,12},{4,0},{8,4},{12,8},{1,13},{5,1},{9,5},{13,9},{2,14},{6,2},{... | collective-permute-start | bytes 513224 | tf_op jit(solution)/shard_map/ppermute | solution.py:718
  621.9 3.3 collective-permute-start.46
  628.3 4.2 collective-permute-done.21
  635.9 23.0 %collective-permute-done.46 = bf16[320,1600]{1,0:T(8,128)(2,1)S(1)} collective-permute-done((bf16[320,1600]{1,0:T(8,128)(2,1)S(1)}, bf16[320,1600]{1,0:T(8,128)(2,1)S(1)}, u32[]{:S(2)}, u32[]{:S(2)}) %collective-permute-start.46) | collective-permute-done | bytes 1024032 | tf_op jit(solution)/shard_map/ppermute | solution.py:789
  663.4 11.6 %collective-permute-start.24 = (bf16[80,1056]{1,0:T(8,128)(2,1)S(1)}, bf16[80,1056]{1,0:T(8,128)(2,1)S(1)}, u32[]{:S(2)}, u32[]{:S(2)}) collective-permute-start(bf16[80,1056]{1,0:T(8,128)(2,1)S(1)} %get-tuple-element.177), channel_id=1, source_target_pairs={{0,1},{1,2},{2,3},{3,0},{4,5},{5,6},{6,7},{7,4},{8,9},{9,10},{10,1... | collective-permute-start | bytes 506888 | tf_op jit(solution)/shard_map/ppermute | solution.py:718
  676.2 3.2 fusion.46
  686.5 2.9 collective-permute-start.48
  695.3 4.0 collective-permute-start.34
  699.3 3.4 fusion.47
  702.7 17.3 %collective-permute-done.36 = bf16[320,640]{1,0:T(8,128)(2,1)S(1)} collective-permute-done((bf16[320,640]{1,0:T(8,128)(2,1)S(1)}, bf16[320,640]{1,0:T(8,128)(2,1)S(1)}, u32[]{:S(2)}, u32[]{:S(2)}) %collective-permute-start.36) | collective-permute-done | bytes 409632 | tf_op jit(solution)/shard_map/ppermute | solution.py:790
  722.1 3.6 fusion.41
  725.7 7.4 %collective-permute-done.37 = bf16[320,640]{1,0:T(8,128)(2,1)S(1)} collective-permute-done((bf16[320,640]{1,0:T(8,128)(2,1)S(1)}, bf16[320,640]{1,0:T(8,128)(2,1)S(1)}, u32[]{:S(2)}, u32[]{:S(2)}) %collective-permute-start.37) | collective-permute-done | bytes 409632 | tf_op jit(solution)/shard_map/ppermute | solution.py:790
  (407 shorter events, 173.4 us)
Async XLA Ops:
  9.1 29.7 %collective-permute-start.2 = (bf16[256,288]{0,1:T(8,128)(2,1)}, bf16[256,288]{0,1:T(8,128)(2,1)}, u32[]{:S(2)}, u32[]{:S(2)}) collective-permute-start(bf16[256,288]{0,1:T(8,128)(2,1)} %constant_dynamic-slice_fusion), channel_id=1, source_target_pairs={{0,12},{4,0},{8,4},{12,8},{1,13},{5,1},{9,5},{13,9},{2,14},{6,2},{... | collective-permute-start | bytes 442376 | tf_op jit(solution)/shard_map/ppermute | solution.py:718
  9.1 29.7 %collective-permute-start.1 = (bf16[256,288]{0,1:T(8,128)(2,1)}, bf16[256,288]{0,1:T(8,128)(2,1)}, u32[]{:S(2)}, u32[]{:S(2)}) collective-permute-start(bf16[256,288]{0,1:T(8,128)(2,1)} %constant_dynamic-slice_fusion), channel_id=1, source_target_pairs={{0,8},{4,12},{8,0},{12,4},{1,9},{5,13},{9,1},{13,5},{2,10},{6,14},... | collective-permute-start | bytes 442376 | tf_op jit(solution)/shard_map/ppermute | solution.py:718
  11.6 27.2 %collective-permute-start = (bf16[256,288]{0,1:T(8,128)(2,1)}, bf16[256,288]{0,1:T(8,128)(2,1)}, u32[]{:S(2)}, u32[]{:S(2)}) collective-permute-start(bf16[256,288]{0,1:T(8,128)(2,1)} %constant_dynamic-slice_fusion), channel_id=1, source_target_pairs={{0,4},{4,8},{8,12},{12,0},{1,5},{5,9},{9,13},{13,1},{2,6},{6,10},{... | collective-permute-start | bytes 442376 | tf_op jit(solution)/shard_map/ppermute | solution.py:718
  25.6 336.0 %copy-start.64 = (f32[512]{0:T(512)}, f32[512]{0:T(512)S(1)}, u32[]{:S(2)}) copy-start(f32[512]{0:T(512)S(1)} %add_rsqrt_fusion.1) | copy-start | bytes 6148
  40.7 5.5 collective-permute-start.3
  166.6 107.4 %collective-permute-start.53 = (bf16[512,1600]{0,1:T(8,128)(2,1)}, bf16[512,1600]{0,1:T(8,128)(2,1)}, u32[]{:S(2)}, u32[]{:S(2)}) collective-permute-start(bf16[512,1600]{0,1:T(8,128)(2,1)} %copy.233), channel_id=1, source_target_pairs={{0,4},{4,8},{8,12},{1,5},{5,9},{9,13},{2,6},{6,10},{10,14},{3,7},{... | collective-permute-start | bytes 4915208 | tf_op jit(solution)/shard_map/ppermute | solution.py:800
  171.0 108.4 %collective-permute-start.55 = (bf16[512,1600]{0,1:T(8,128)(2,1)}, bf16[512,1600]{0,1:T(8,128)(2,1)}, u32[]{:S(2)}, u32[]{:S(2)}) collective-permute-start(bf16[512,1600]{0,1:T(8,128)(2,1)} %copy.233), channel_id=1, source_target_pairs={{4,0},{8,4},{12,8},{5,1},{9,5},{13,9},{6,2},{10,6},{14,10},{7,3},{... | collective-permute-start | bytes 4915208 | tf_op jit(solution)/shard_map/ppermute | solution.py:801
  186.4 14.2 %collective-permute-start.4 = (bf16[256,2560]{1,0:T(8,128)(2,1)}, bf16[256,2560]{1,0:T(8,128)(2,1)}, u32[]{:S(2)}, u32[]{:S(2)}) collective-permute-start(bf16[256,2560]{1,0:T(8,128)(2,1)} %dynamic-slice_bitcast_fusion.4), channel_id=1, source_target_pairs={{0,1},{1,0},{2,3},{3,2},{4,5},{5,4},{6,7},{7,6},{8,9},{9,8},{10,11... | collective-permute-start | bytes 3932168 | tf_op jit(solution)/shard_map/ppermute | solution.py:714
  188.8 37.2 %collective-permute-start.7 = (bf16[512,1600]{0,1:T(8,128)(2,1)}, bf16[512,1600]{0,1:T(8,128)(2,1)}, u32[]{:S(2)}, u32[]{:S(2)}) collective-permute-start(bf16[512,1600]{0,1:T(8,128)(2,1)} %copy.214), channel_id=1, source_target_pairs={{0,16},{16,0},{1,17},{17,1},{2,18},{18,2},{3,19},{19,3},{4,20},{20... | collective-permute-start | bytes 4915208 | tf_op jit(solution)/shard_map/ppermute | solution.py:714
  194.7 59.4 %collective-permute-start.6 = (bf16[1280,512]{1,0:T(8,128)(2,1)}, bf16[1280,512]{1,0:T(8,128)(2,1)}, u32[]{:S(2)}, u32[]{:S(2)}) collective-permute-start(bf16[1280,512]{1,0:T(8,128)(2,1)} %get-tuple-element.198), channel_id=1, source_target_pairs={{0,16},{16,0},{1,17},{17,1},{2,18},{18,2},{3,19},{19,3},{4,20},{20... | collective-permute-start | bytes 3932168 | tf_op jit(solution)/shard_map/ppermute | solution.py:714
  202.3 83.0 %collective-permute-start.5 = (bf16[256,2560]{1,0:T(8,128)(2,1)S(1)}, bf16[256,2560]{1,0:T(8,128)(2,1)}, u32[]{:S(2)}, u32[]{:S(2)}) collective-permute-start(bf16[256,2560]{1,0:T(8,128)(2,1)S(1)} %fusion.36), channel_id=1, source_target_pairs={{0,2},{1,3},{2,0},{3,1},{4,6},{5,7},{6,4},{7,5},{8,10},{9,11},{10,... | collective-permute-start | bytes 3932168 | tf_op jit(solution)/shard_map/ppermute | solution.py:714
  229.6 62.8 %collective-permute-start.8 = (bf16[512,1600]{0,1:T(8,128)(2,1)}, bf16[512,1600]{0,1:T(8,128)(2,1)}, u32[]{:S(2)}, u32[]{:S(2)}) collective-permute-start(bf16[512,1600]{0,1:T(8,128)(2,1)} %copy.215), channel_id=1, source_target_pairs={{0,16},{16,0},{1,17},{17,1},{2,18},{18,2},{3,19},{19,3},{4,20},{20... | collective-permute-start | bytes 4915208 | tf_op jit(solution)/shard_map/ppermute | solution.py:714
  272.7 110.5 %collective-permute-start.38 = (bf16[320,1600]{1,0:T(8,128)(2,1)}, bf16[320,1600]{1,0:T(8,128)(2,1)}, u32[]{:S(2)}, u32[]{:S(2)}) collective-permute-start(bf16[320,1600]{1,0:T(8,128)(2,1)} %get-tuple-element.191), channel_id=1, source_target_pairs={{0,4},{1,5},{2,6},{3,7},{16,20},{17,21},{18,22},{19,23}} | collective-permute-start | bytes 3072008 | tf_op jit(solution)/shard_map/ppermute | solution.py:789
  274.0 110.1 %collective-permute-start.39 = (bf16[320,1600]{1,0:T(8,128)(2,1)}, bf16[320,1600]{1,0:T(8,128)(2,1)}, u32[]{:S(2)}, u32[]{:S(2)}) collective-permute-start(bf16[320,1600]{1,0:T(8,128)(2,1)} %get-tuple-element.190), channel_id=1, source_target_pairs={{12,8},{13,9},{14,10},{15,11},{28,24},{29,25},{30,26},{31,27}} | collective-permute-start | bytes 3072008 | tf_op jit(solution)/shard_map/ppermute | solution.py:790
  279.3 89.4 %collective-permute-start.54 = (bf16[512,1600]{0,1:T(8,128)(2,1)}, bf16[512,1600]{0,1:T(8,128)(2,1)}, u32[]{:S(2)}, u32[]{:S(2)}) collective-permute-start(bf16[512,1600]{0,1:T(8,128)(2,1)} %collective-permute-done.53), channel_id=1, source_target_pairs={{4,8},{8,12},{5,9},{9,13},{6,10},{10,14},{7,11},{11,15},{20,24},{2... | collective-permute-start | bytes 4915208 | tf_op jit(solution)/shard_map/ppermute | solution.py:800
  285.3 90.0 %collective-permute-start.56 = (bf16[512,1600]{0,1:T(8,128)(2,1)}, bf16[512,1600]{0,1:T(8,128)(2,1)}, u32[]{:S(2)}, u32[]{:S(2)}) collective-permute-start(bf16[512,1600]{0,1:T(8,128)(2,1)} %collective-permute-done.55), channel_id=1, source_target_pairs={{4,0},{8,4},{5,1},{9,5},{6,2},{10,6},{7,3},{11,7},{20,16},{24,20},... | collective-permute-start | bytes 4915208 | tf_op jit(solution)/shard_map/ppermute | solution.py:801
  358.7 32.1 %collective-permute-start.10 = (bf16[256,768]{1,0:T(8,128)(2,1)}, bf16[256,768]{1,0:T(8,128)(2,1)}, u32[]{:S(2)}, u32[]{:S(2)}) collective-permute-start(bf16[256,768]{1,0:T(8,128)(2,1)} %dynamic-slice_bitcast_fusion.16), channel_id=1, source_target_pairs={{0,1},{1,0},{2,3},{3,2},{4,5},{5,4},{6,7},{7,6},{8,9},{9,8},{10,11... | collective-permute-start | bytes 1179656 | tf_op jit(solution)/shard_map/ppermute | solution.py:714
  368.7 18.3 %collective-permute-start.13 = (bf16[144,2048]{1,0:T(8,128)(2,1)}, bf16[144,2048]{1,0:T(8,128)(2,1)}, u32[]{:S(2)}, u32[]{:S(2)}) collective-permute-start(bf16[144,2048]{1,0:T(8,128)(2,1)} %dynamic-slice_bitcast_fusion.13), channel_id=1, source_target_pairs={{0,1},{1,0},{2,3},{3,2},{4,5},{5,4},{6,7},{7,6},{8,9},{9,8},{10,11... | collective-permute-start | bytes 1769480 | tf_op jit(solution)/shard_map/ppermute | solution.py:714
  375.3 83.6 %collective-permute-start.44 = (bf16[320,1600]{1,0:T(8,128)(2,1)}, bf16[320,1600]{1,0:T(8,128)(2,1)}, u32[]{:S(2)}, u32[]{:S(2)}) collective-permute-start(bf16[320,1600]{1,0:T(8,128)(2,1)} %get-tuple-element.185), channel_id=1, source_target_pairs={{0,4},{1,5},{2,6},{3,7},{16,20},{17,21},{18,22},{19,23}} | collective-permute-start | bytes 3072008 | tf_op jit(solution)/shard_map/ppermute | solution.py:789
  383.2 78.3 %collective-permute-start.45 = (bf16[320,1600]{1,0:T(8,128)(2,1)S(1)}, bf16[320,1600]{1,0:T(8,128)(2,1)S(1)}, u32[]{:S(2)}, u32[]{:S(2)}) collective-permute-start(bf16[320,1600]{1,0:T(8,128)(2,1)S(1)} %copy-done.40), channel_id=1, source_target_pairs={{12,8},{13,9},{14,10},{15,11},{28,24},{29,25},{30,26},{31,27}} | collective-permute-start | bytes 3072008 | tf_op jit(solution)/shard_map/ppermute | solution.py:790
  384.1 78.6 %slice-start = ((s8[4259840]{0:T(1024)(128)(4,1)}), s8[4194304]{0:T(1024)(128)(4,1)S(1)}, s32[]{:S(2)}) async-start(s8[4259840]{0:T(1024)(128)(4,1)} %bitcast.232), calls=%async_computation | async-start | bytes 8388608
  388.3 8.1 %collective-permute-start.14 = (bf16[72,2048]{1,0:T(8,128)(2,1)S(1)}, bf16[72,2048]{1,0:T(8,128)(2,1)S(1)}, u32[]{:S(2)}, u32[]{:S(2)}) collective-permute-start(bf16[72,2048]{1,0:T(8,128)(2,1)S(1)} %dynamic-slice_bitcast_fusion.20), channel_id=1, source_target_pairs={{0,2},{1,3},{2,0},{3,1},{4,6},{5,7},{6,4},{7,5},{8,10},{9,11},{10,... | collective-permute-start | bytes 884744 | tf_op jit(solution)/shard_map/ppermute | solution.py:714
  389.6 82.2 %slice-start.4 = ((s8[4259840]{0:T(1024)(128)(4,1)}), s8[4194304]{0:T(1024)(128)(4,1)S(1)}, s32[]{:S(2)}) async-start(s8[4259840]{0:T(1024)(128)(4,1)} %bitcast.241), calls=%async_computation.4 | async-start | bytes 8388608
  392.4 37.0 %collective-permute-start.11 = (bf16[256,768]{1,0:T(8,128)(2,1)S(1)}, bf16[256,768]{1,0:T(8,128)(2,1)S(1)}, u32[]{:S(2)}, u32[]{:S(2)}) collective-permute-start(bf16[256,768]{1,0:T(8,128)(2,1)S(1)} %fusion.70), channel_id=1, source_target_pairs={{0,2},{1,3},{2,0},{3,1},{4,6},{5,7},{6,4},{7,5},{8,10},{9,11},{10,... | collective-permute-start | bytes 1179656 | tf_op jit(solution)/shard_map/ppermute | solution.py:714
  396.5 34.8 %collective-permute-start.17 = (bf16[72,512]{1,0:T(8,128)(2,1)S(1)}, bf16[72,512]{1,0:T(8,128)(2,1)S(1)}, u32[]{:S(2)}, u32[]{:S(2)}) collective-permute-start(bf16[72,512]{1,0:T(8,128)(2,1)S(1)} %get-tuple-element.234), channel_id=1, source_target_pairs={{0,4},{4,8},{8,12},{12,0},{1,5},{5,9},{9,13},{13,1},{2,6},{6,10},{... | collective-permute-start | bytes 221192 | tf_op jit(solution)/shard_map/ppermute | solution.py:718
  403.9 29.2 %collective-permute-start.16 = (bf16[72,512]{1,0:T(8,128)(2,1)S(1)}, bf16[72,512]{1,0:T(8,128)(2,1)S(1)}, u32[]{:S(2)}, u32[]{:S(2)}) collective-permute-start(bf16[72,512]{1,0:T(8,128)(2,1)S(1)} %get-tuple-element.235), channel_id=1, source_target_pairs={{0,8},{4,12},{8,0},{12,4},{1,9},{5,13},{9,1},{13,5},{2,10},{6,14},... | collective-permute-start | bytes 221192 | tf_op jit(solution)/shard_map/ppermute | solution.py:718
  429.4 36.5 %collective-permute-start.40 = (bf16[320,1600]{1,0:T(8,128)(2,1)S(1)}, bf16[320,1600]{1,0:T(8,128)(2,1)S(1)}, u32[]{:S(2)}, u32[]{:S(2)}) collective-permute-start(bf16[320,1600]{1,0:T(8,128)(2,1)S(1)} %get-tuple-element.189), channel_id=1, source_target_pairs={{0,4},{4,8},{1,5},{5,9},{2,6},{6,10},{3,7},{7,11},{16,20},{20,24},... | collective-permute-start | bytes 3072008 | tf_op jit(solution)/shard_map/ppermute | solution.py:789
  431.4 36.9 %collective-permute-start.41 = (bf16[320,1600]{1,0:T(8,128)(2,1)S(1)}, bf16[320,1600]{1,0:T(8,128)(2,1)S(1)}, u32[]{:S(2)}, u32[]{:S(2)}) collective-permute-start(bf16[320,1600]{1,0:T(8,128)(2,1)S(1)} %get-tuple-element.188), channel_id=1, source_target_pairs={{12,8},{8,4},{13,9},{9,5},{14,10},{10,6},{15,11},{11,7},{28,24},{2... | collective-permute-start | bytes 3072008 | tf_op jit(solution)/shard_map/ppermute | solution.py:790
  433.1 23.8 %collective-permute-start.15 = (bf16[72,512]{1,0:T(8,128)(2,1)S(1)}, bf16[72,512]{1,0:T(8,128)(2,1)S(1)}, u32[]{:S(2)}, u32[]{:S(2)}) collective-permute-start(bf16[72,512]{1,0:T(8,128)(2,1)S(1)} %get-tuple-element.233), channel_id=1, source_target_pairs={{0,12},{4,0},{8,4},{12,8},{1,13},{5,1},{9,5},{13,9},{2,14},{6,2},{... | collective-permute-start | bytes 221192 | tf_op jit(solution)/shard_map/ppermute | solution.py:718
  457.0 109.0 %collective-permute-start.52 = (bf16[2,320,512]{2,1,0:T(8,128)(2,1)}, bf16[2,320,512]{2,1,0:T(8,128)(2,1)}, u32[]{:S(2)}, u32[]{:S(2)}) collective-permute-start(bf16[2,320,512]{2,1,0:T(8,128)(2,1)} %get-tuple-element.193), channel_id=1, source_target_pairs={{0,12},{4,0},{8,4},{12,8},{1,13},{5,1},{9,5},{13,9},{2,14},{6,2},{... | collective-permute-start | bytes 1966088 | tf_op jit(solution)/shard_map/ppermute | solution.py:718
  458.9 107.1 %collective-permute-start.51 = (bf16[2,320,512]{2,1,0:T(8,128)(2,1)}, bf16[2,320,512]{2,1,0:T(8,128)(2,1)}, u32[]{:S(2)}, u32[]{:S(2)}) collective-permute-start(bf16[2,320,512]{2,1,0:T(8,128)(2,1)} %get-tuple-element.194), channel_id=1, source_target_pairs={{0,8},{4,12},{8,0},{12,4},{1,9},{5,13},{9,1},{13,5},{2,10},{6,14},... | collective-permute-start | bytes 1966088 | tf_op jit(solution)/shard_map/ppermute | solution.py:718
  461.5 10.1 %collective-permute-start.18 = (bf16[72,512]{1,0:T(8,128)(2,1)S(1)}, bf16[72,512]{1,0:T(8,128)(2,1)S(1)}, u32[]{:S(2)}, u32[]{:S(2)}) collective-permute-start(bf16[72,512]{1,0:T(8,128)(2,1)S(1)} %add_convert_fusion.5), channel_id=1, source_target_pairs={{0,2},{1,3},{2,0},{3,1},{4,6},{5,7},{6,4},{7,5},{8,10},{9,11},{10,... | collective-permute-start | bytes 221192 | tf_op jit(solution)/shard_map/ppermute | solution.py:714
  465.9 104.6 %collective-permute-start.50 = (bf16[2,320,512]{2,1,0:T(8,128)(2,1)}, bf16[2,320,512]{2,1,0:T(8,128)(2,1)}, u32[]{:S(2)}, u32[]{:S(2)}) collective-permute-start(bf16[2,320,512]{2,1,0:T(8,128)(2,1)} %get-tuple-element.192), channel_id=1, source_target_pairs={{0,4},{4,8},{8,12},{12,0},{1,5},{5,9},{9,13},{13,1},{2,6},{6,10},{... | collective-permute-start | bytes 1966088 | tf_op jit(solution)/shard_map/ppermute | solution.py:718
  468.2 51.4 %collective-permute-start.9 = (bf16[256,2560]{1,0:T(8,128)(2,1)}, bf16[256,2560]{1,0:T(8,128)(2,1)}, u32[]{:S(2)}, u32[]{:S(2)}) collective-permute-start(bf16[256,2560]{1,0:T(8,128)(2,1)} %add_convert_fusion.1), channel_id=1, source_target_pairs={{0,1},{1,0},{2,3},{3,2},{4,5},{5,4},{6,7},{7,6},{8,9},{9,8},{10,11... | collective-permute-start | bytes 3932168 | tf_op jit(solution)/shard_map/ppermute | solution.py:714
  471.7 2.7 collective-permute-start.19
  474.4 3.3 collective-permute-start.12
  477.7 44.8 %collective-permute-start.27 = (bf16[4,128,1280]{2,1,0:T(8,128)(2,1)}, bf16[4,128,1280]{2,1,0:T(8,128)(2,1)}, u32[]{:S(2)}, u32[]{:S(2)}) collective-permute-start(bf16[4,128,1280]{2,1,0:T(8,128)(2,1)} %fusion.56), channel_id=1, source_target_pairs={{0,16},{16,0},{1,17},{17,1},{2,18},{18,2},{3,19},{19,3},{4,20},{20... | collective-permute-start | bytes 3932168 | tf_op jit(solution)/shard_map/ppermute | solution.py:714
  519.7 14.1 %collective-permute-start.58 = (bf16[512,1600]{0,1:T(8,128)(2,1)}, bf16[512,1600]{0,1:T(8,128)(2,1)S(1)}, u32[]{:S(2)}, u32[]{:S(2)}) collective-permute-start(bf16[512,1600]{0,1:T(8,128)(2,1)} %collective-permute-done.54), channel_id=1, source_target_pairs={{8,12},{9,13},{10,14},{11,15},{24,28},{25,29},{26,30},{27,31}} | collective-permute-start | bytes 4915208 | tf_op jit(solution)/shard_map/ppermute | solution.py:800
  522.5 36.4 %collective-permute-start.57 = (bf16[512,1600]{0,1:T(8,128)(2,1)}, bf16[512,1600]{0,1:T(8,128)(2,1)}, u32[]{:S(2)}, u32[]{:S(2)}) collective-permute-start(bf16[512,1600]{0,1:T(8,128)(2,1)} %collective-permute-done.56), channel_id=1, source_target_pairs={{4,0},{5,1},{6,2},{7,3},{20,16},{21,17},{22,18},{23,19}} | collective-permute-start | bytes 4915208 | tf_op jit(solution)/shard_map/ppermute | solution.py:801
  534.9 44.6 %collective-permute-start.31 = (bf16[4,320,640]{2,1,0:T(8,128)(2,1)}, bf16[4,320,640]{2,1,0:T(8,128)(2,1)}, u32[]{:S(2)}, u32[]{:S(2)}) collective-permute-start(bf16[4,320,640]{2,1,0:T(8,128)(2,1)} %dynamic-slice_bitcast_fusion), channel_id=1, source_target_pairs={{0,16},{16,0},{1,17},{17,1},{2,18},{18,2},{3,19},{19,3},{4,20},{20... | collective-permute-start | bytes 4915208 | tf_op jit(solution)/shard_map/ppermute | solution.py:714
  558.9 104.5 %collective-permute-start.43 = (bf16[320,1600]{1,0:T(8,128)(2,1)}, bf16[320,1600]{1,0:T(8,128)(2,1)}, u32[]{:S(2)}, u32[]{:S(2)}) collective-permute-start(bf16[320,1600]{1,0:T(8,128)(2,1)} %get-tuple-element.187), channel_id=1, source_target_pairs={{12,8},{8,4},{4,0},{13,9},{9,5},{5,1},{14,10},{10,6},{6,2},{15,11}... | collective-permute-start | bytes 3072008 | tf_op jit(solution)/shard_map/ppermute | solution.py:790
  566.0 28.5 %collective-permute-start.30 = (bf16[128,1280]{1,0:T(8,128)(2,1)}, bf16[128,1280]{1,0:T(8,128)(2,1)S(1)}, u32[]{:S(2)}, u32[]{:S(2)}) collective-permute-start(bf16[128,1280]{1,0:T(8,128)(2,1)} %get-tuple-element.208), channel_id=1, source_target_pairs={{0,12},{4,0},{8,4},{12,8},{1,13},{5,1},{9,5},{13,9},{2,14},{6,2},{... | collective-permute-start | bytes 983048 | tf_op jit(solution)/shard_map/ppermute | solution.py:718
  566.0 36.4 %collective-permute-start.29 = (bf16[128,1280]{1,0:T(8,128)(2,1)}, bf16[128,1280]{1,0:T(8,128)(2,1)S(1)}, u32[]{:S(2)}, u32[]{:S(2)}) collective-permute-start(bf16[128,1280]{1,0:T(8,128)(2,1)} %get-tuple-element.209), channel_id=1, source_target_pairs={{0,8},{4,12},{8,0},{12,4},{1,9},{5,13},{9,1},{13,5},{2,10},{6,14},... | collective-permute-start | bytes 983048 | tf_op jit(solution)/shard_map/ppermute | solution.py:718
  570.5 31.9 %collective-permute-start.28 = (bf16[128,1280]{1,0:T(8,128)(2,1)}, bf16[128,1280]{1,0:T(8,128)(2,1)S(1)}, u32[]{:S(2)}, u32[]{:S(2)}) collective-permute-start(bf16[128,1280]{1,0:T(8,128)(2,1)} %get-tuple-element.207), channel_id=1, source_target_pairs={{0,4},{4,8},{8,12},{12,0},{1,5},{5,9},{9,13},{13,1},{2,6},{6,10},{... | collective-permute-start | bytes 983048 | tf_op jit(solution)/shard_map/ppermute | solution.py:718
  579.5 24.2 %collective-permute-start.20 = (bf16[4,81,1056]{2,0,1:T(4,128)(2,1)S(1)}, bf16[4,81,1056]{2,0,1:T(4,128)(2,1)S(1)}, u32[]{:S(2)}, u32[]{:S(2)}) collective-permute-start(bf16[4,81,1056]{2,0,1:T(4,128)(2,1)S(1)} %bitcast.272), channel_id=1, source_target_pairs={{0,16},{16,0},{1,17},{17,1},{2,18},{18,2},{3,19},{19,3},{4,20},{20... | collective-permute-start | bytes 2052872 | tf_op jit(solution)/shard_map/ppermute | solution.py:714
  580.7 80.7 %slice-start.2 = ((s8[4259840]{0:T(1024)(128)(4,1)}), s8[4194304]{0:T(1024)(128)(4,1)S(1)}, s32[]{:S(2)}) async-start(s8[4259840]{0:T(1024)(128)(4,1)} %bitcast.235), calls=%async_computation.2 | async-start | bytes 8388608
  594.5 80.6 %collective-permute-start.42 = (bf16[320,1600]{1,0:T(8,128)(2,1)S(1)}, bf16[320,1600]{1,0:T(8,128)(2,1)S(1)}, u32[]{:S(2)}, u32[]{:S(2)}) collective-permute-start(bf16[320,1600]{1,0:T(8,128)(2,1)S(1)} %copy-done.43), channel_id=1, source_target_pairs={{0,4},{4,8},{8,12},{1,5},{5,9},{9,13},{2,6},{6,10},{10,14},{3,7},{... | collective-permute-start | bytes 3072008 | tf_op jit(solution)/shard_map/ppermute | solution.py:789
  603.9 18.0 %collective-permute-start.23 = (bf16[81,1056]{1,0:T(8,128)(2,1)S(1)}, bf16[81,1056]{1,0:T(8,128)(2,1)S(1)}, u32[]{:S(2)}, u32[]{:S(2)}) collective-permute-start(bf16[81,1056]{1,0:T(8,128)(2,1)S(1)} %get-tuple-element.217), channel_id=1, source_target_pairs={{0,12},{4,0},{8,4},{12,8},{1,13},{5,1},{9,5},{13,9},{2,14},{6,2},{... | collective-permute-start | bytes 513224 | tf_op jit(solution)/shard_map/ppermute | solution.py:718
  618.2 8.8 %collective-permute-start.22 = (bf16[81,1056]{1,0:T(8,128)(2,1)S(1)}, bf16[81,1056]{1,0:T(8,128)(2,1)S(1)}, u32[]{:S(2)}, u32[]{:S(2)}) collective-permute-start(bf16[81,1056]{1,0:T(8,128)(2,1)S(1)} %get-tuple-element.218), channel_id=1, source_target_pairs={{0,8},{4,12},{8,0},{12,4},{1,9},{5,13},{9,1},{13,5},{2,10},{6,14},... | collective-permute-start | bytes 513224 | tf_op jit(solution)/shard_map/ppermute | solution.py:718
  618.2 14.3 %collective-permute-start.21 = (bf16[81,1056]{1,0:T(8,128)(2,1)S(1)}, bf16[81,1056]{1,0:T(8,128)(2,1)S(1)}, u32[]{:S(2)}, u32[]{:S(2)}) collective-permute-start(bf16[81,1056]{1,0:T(8,128)(2,1)S(1)} %get-tuple-element.216), channel_id=1, source_target_pairs={{0,4},{4,8},{8,12},{12,0},{1,5},{5,9},{9,13},{13,1},{2,6},{6,10},{... | collective-permute-start | bytes 513224 | tf_op jit(solution)/shard_map/ppermute | solution.py:718
  621.9 37.0 %collective-permute-start.46 = (bf16[320,1600]{1,0:T(8,128)(2,1)S(1)}, bf16[320,1600]{1,0:T(8,128)(2,1)S(1)}, u32[]{:S(2)}, u32[]{:S(2)}) collective-permute-start(bf16[320,1600]{1,0:T(8,128)(2,1)S(1)} %copy-done.42), channel_id=1, source_target_pairs={{0,4},{4,8},{1,5},{5,9},{2,6},{6,10},{3,7},{7,11},{16,20},{20,24},... | collective-permute-start | bytes 3072008 | tf_op jit(solution)/shard_map/ppermute | solution.py:789
  627.0 33.3 %collective-permute-start.47 = (bf16[320,1600]{1,0:T(8,128)(2,1)S(1)}, bf16[320,1600]{1,0:T(8,128)(2,1)S(1)}, u32[]{:S(2)}, u32[]{:S(2)}) collective-permute-start(bf16[320,1600]{1,0:T(8,128)(2,1)S(1)} %copy-done.41), channel_id=1, source_target_pairs={{12,8},{8,4},{13,9},{9,5},{14,10},{10,6},{15,11},{11,7},{28,24},{2... | collective-permute-start | bytes 3072008 | tf_op jit(solution)/shard_map/ppermute | solution.py:790
  632.5 46.9 %collective-permute-start.32 = (bf16[320,640]{1,0:T(8,128)(2,1)S(1)}, bf16[320,640]{1,0:T(8,128)(2,1)S(1)}, u32[]{:S(2)}, u32[]{:S(2)}) collective-permute-start(bf16[320,640]{1,0:T(8,128)(2,1)S(1)} %get-tuple-element.205), channel_id=1, source_target_pairs={{0,4},{1,5},{2,6},{3,7},{16,20},{17,21},{18,22},{19,23}} | collective-permute-start | bytes 1228808 | tf_op jit(solution)/shard_map/ppermute | solution.py:789
  658.9 32.8 %collective-permute-start.35 = (bf16[320,640]{1,0:T(8,128)(2,1)}, bf16[320,640]{1,0:T(8,128)(2,1)}, u32[]{:S(2)}, u32[]{:S(2)}) collective-permute-start(bf16[320,640]{1,0:T(8,128)(2,1)} %get-tuple-element.206), channel_id=1, source_target_pairs={{12,8},{13,9},{14,10},{15,11},{28,24},{29,25},{30,26},{31,27}} | collective-permute-start | bytes 1228808 | tf_op jit(solution)/shard_map/ppermute | solution.py:790
  660.3 39.0 %collective-permute-start.59 = (bf16[320,1600]{1,0:T(8,128)(2,1)S(1)}, bf16[320,1600]{1,0:T(8,128)(2,1)}, u32[]{:S(2)}, u32[]{:S(2)}) collective-permute-start(bf16[320,1600]{1,0:T(8,128)(2,1)S(1)} %fusion.60), channel_id=1, source_target_pairs={{0,16},{16,0},{1,17},{17,1},{2,18},{18,2},{3,19},{19,3},{4,20},{20... | collective-permute-start | bytes 3072008 | tf_op jit(solution)/shard_map/ppermute | solution.py:714
  663.4 17.0 %collective-permute-start.24 = (bf16[80,1056]{1,0:T(8,128)(2,1)S(1)}, bf16[80,1056]{1,0:T(8,128)(2,1)S(1)}, u32[]{:S(2)}, u32[]{:S(2)}) collective-permute-start(bf16[80,1056]{1,0:T(8,128)(2,1)S(1)} %get-tuple-element.177), channel_id=1, source_target_pairs={{0,1},{1,2},{2,3},{3,0},{4,5},{5,6},{6,7},{7,4},{8,9},{9,10},{10,1... | collective-permute-start | bytes 506888 | tf_op jit(solution)/shard_map/ppermute | solution.py:718
  675.0 9.1 %collective-permute-start.25 = (bf16[80,1056]{1,0:T(8,128)(2,1)S(1)}, bf16[80,1056]{1,0:T(8,128)(2,1)S(1)}, u32[]{:S(2)}, u32[]{:S(2)}) collective-permute-start(bf16[80,1056]{1,0:T(8,128)(2,1)S(1)} %get-tuple-element.177), channel_id=1, source_target_pairs={{0,2},{1,3},{2,0},{3,1},{4,6},{5,7},{6,4},{7,5},{8,10},{9,11},{10,... | collective-permute-start | bytes 506888 | tf_op jit(solution)/shard_map/ppermute | solution.py:718
  679.5 7.0 collective-permute-start.26
  680.3 12.3 %collective-permute-start.33 = (bf16[320,640]{1,0:T(8,128)(2,1)}, bf16[320,640]{1,0:T(8,128)(2,1)}, u32[]{:S(2)}, u32[]{:S(2)}) collective-permute-start(bf16[320,640]{1,0:T(8,128)(2,1)} %fusion.63), channel_id=1, source_target_pairs={{0,4},{4,8},{1,5},{5,9},{2,6},{6,10},{3,7},{7,11},{16,20},{20,24},... | collective-permute-start | bytes 1228808 | tf_op jit(solution)/shard_map/ppermute | solution.py:789
  684.1 38.0 %collective-permute-start.49 = (bf16[320,1600]{1,0:T(8,128)(2,1)}, bf16[320,1600]{1,0:T(8,128)(2,1)}, u32[]{:S(2)}, u32[]{:S(2)}) collective-permute-start(bf16[320,1600]{1,0:T(8,128)(2,1)} %get-tuple-element.181), channel_id=1, source_target_pairs={{12,8},{8,4},{4,0},{13,9},{9,5},{5,1},{14,10},{10,6},{6,2},{15,11}... | collective-permute-start | bytes 3072008 | tf_op jit(solution)/shard_map/ppermute | solution.py:790
  686.5 35.6 %collective-permute-start.48 = (bf16[320,1600]{1,0:T(8,128)(2,1)}, bf16[320,1600]{1,0:T(8,128)(2,1)}, u32[]{:S(2)}, u32[]{:S(2)}) collective-permute-start(bf16[320,1600]{1,0:T(8,128)(2,1)} %get-tuple-element.180), channel_id=1, source_target_pairs={{0,4},{4,8},{8,12},{1,5},{5,9},{9,13},{2,6},{6,10},{10,14},{3,7},{... | collective-permute-start | bytes 3072008 | tf_op jit(solution)/shard_map/ppermute | solution.py:789
  694.0 26.1 %collective-permute-start.36 = (bf16[320,640]{1,0:T(8,128)(2,1)S(1)}, bf16[320,640]{1,0:T(8,128)(2,1)S(1)}, u32[]{:S(2)}, u32[]{:S(2)}) collective-permute-start(bf16[320,640]{1,0:T(8,128)(2,1)S(1)} %get-tuple-element.204), channel_id=1, source_target_pairs={{12,8},{8,4},{13,9},{9,5},{14,10},{10,6},{15,11},{11,7},{28,24},{2... | collective-permute-start | bytes 1228808 | tf_op jit(solution)/shard_map/ppermute | solution.py:790
  695.3 30.4 %collective-permute-start.34 = (bf16[320,640]{1,0:T(8,128)(2,1)S(1)}, bf16[320,640]{1,0:T(8,128)(2,1)S(1)}, u32[]{:S(2)}, u32[]{:S(2)}) collective-permute-start(bf16[320,640]{1,0:T(8,128)(2,1)S(1)} %get-tuple-element.203), channel_id=1, source_target_pairs={{0,4},{4,8},{8,12},{1,5},{5,9},{9,13},{2,6},{6,10},{10,14},{3,7},{... | collective-permute-start | bytes 1228808 | tf_op jit(solution)/shard_map/ppermute | solution.py:789
  720.2 13.0 %collective-permute-start.37 = (bf16[320,640]{1,0:T(8,128)(2,1)S(1)}, bf16[320,640]{1,0:T(8,128)(2,1)S(1)}, u32[]{:S(2)}, u32[]{:S(2)}) collective-permute-start(bf16[320,640]{1,0:T(8,128)(2,1)S(1)} %fusion.62), channel_id=1, source_target_pairs={{12,8},{8,4},{4,0},{13,9},{9,5},{5,1},{14,10},{10,6},{6,2},{15,11}... | collective-permute-start | bytes 1228808 | tf_op jit(solution)/shard_map/ppermute | solution.py:790
  (87 other events, 759.9 us)
